TPU v7x, 32 devices: a whole 2x2x4 slice. The times are simulated.
32 devices in a mesh: seq: 16 (over z, x, core), head: 2 (over y).
Axes of the slice: x: 2, y: 2, z: 4, core: 2. Of those that a mesh axis runs over, the one named last changes fastest.
Arguments:
- queries: bfloat16 [6144, 5120], P(('seq', 'head')), may hold values from -6 to 6
- keys: bfloat16 [6144, 1024], P(('seq', 'head')), may hold values from -6 to 6
- values: bfloat16 [6144, 1024], P(('seq', 'head')), may hold values from -6 to 6
- outputs: bfloat16 [6144, 5120], P(('seq', 'head')), may hold values from -2 to 2
- output_gradient: bfloat16 [6144, 5120], P(('seq', 'head')), may hold values from -6 to 6
- lse: bfloat16 [6144, 40], P(('seq', 'head'))
- ranks: int32 [6144], P(('seq', 'head')), may hold values from 0 to 2048, as said below
Outputs:
- query_grads: bfloat16 [6144, 5120], P(('seq', 'head'))
- key_gradient_output: bfloat16 [6144, 1024], P(('seq', 'head'))
- value_gradient: bfloat16 [6144, 1024], P(('seq', 'head'))
Inputs may be any that keep to these rules, and one draw needn't show every extreme that they name: Home shard s holds slots s * 384 to (s + 1) * 384 - 1. Its live slots are its first c_s slots, with 1 <= c_s <= 384, holding the consecutive ranks P_s, P_s + 1, ..., where P_s is the number of survivors of the shards before s; its other slots hold 2048. One shard holds exactly 384 survivors; all shards together 2048.
All inputs are finite; a program needn't handle non-finite values.
Results may differ from a plain program's by a relative error of at most 0.0056.
Values may be sent and summed in bfloat16 or wider, within the bound.
No kernel may reach another device: no remote copies, remote signals or barrier semaphores. Data moves between devices by JAX's collectives and lax.ppermute only.
A program may use at most 64 MiB of HBM per device.

v0:
```python
import functools

import jax
import jax.numpy as jnp
from jax import lax
from jax.experimental import pallas as pl
from jax.experimental.pallas import tpu as pltpu
from jax.sharding import Mesh
from jax.sharding import PartitionSpec as P

QUERY_HEADS = 40
KEY_VALUE_HEADS = 8
HEAD_SIZE = 128
BALANCED_TOKENS = 128


block_keys = 512


def per_device(queries, keys, values, outputs, output_gradient, lse, ranks, seq="seq"):
    sequence_count = lax.axis_size(seq)
    head_total = lax.axis_size("head")
    home_rows = queries.shape[0]
    capacity = home_rows * head_total
    slots = capacity // sequence_count
    surviving_tokens = BALANCED_TOKENS * sequence_count
    group_size = QUERY_HEADS // KEY_VALUE_HEADS
    local_key_value = KEY_VALUE_HEADS // head_total
    scale = HEAD_SIZE ** (-0.5)

    def split_heads(array):
        return array.reshape(home_rows, head_total, array.shape[1] // head_total)

    moved = (
        lax.all_to_all(split_heads(queries), "head", split_axis=1, concat_axis=0, tiled=True),
        lax.all_to_all(split_heads(keys), "head", split_axis=1, concat_axis=0, tiled=True),
        lax.all_to_all(split_heads(values), "head", split_axis=1, concat_axis=0, tiled=True),
        lax.all_to_all(
            split_heads(output_gradient), "head", split_axis=1, concat_axis=0, tiled=True
        ),
        lax.all_to_all(split_heads(lse), "head", split_axis=1, concat_axis=0, tiled=True),
        lax.all_to_all(split_heads(outputs), "head", split_axis=1, concat_axis=0, tiled=True),
    )
    shard_rank_list = lax.all_gather(ranks, "head", axis=0, tiled=True)
    first_rank = shard_rank_list[0]
    living_count = jnp.sum((shard_rank_list < surviving_tokens).astype(jnp.int32))
    table = lax.all_gather(
        jnp.stack([first_rank, living_count])[None, :], seq, axis=0, tiled=True
    )

    def to_pairs(array):
        flat = array.reshape(slots, sequence_count, array.shape[-1])
        return jnp.roll(flat, first_rank, axis=1)

    arrived = (
        lax.all_to_all(to_pairs(moved[0]), seq, split_axis=1, concat_axis=1, tiled=True),
        lax.all_to_all(to_pairs(moved[1]), seq, split_axis=1, concat_axis=1, tiled=True),
        lax.all_to_all(to_pairs(moved[2]), seq, split_axis=1, concat_axis=1, tiled=True),
        lax.all_to_all(to_pairs(moved[3]), seq, split_axis=1, concat_axis=1, tiled=True),
        lax.all_to_all(to_pairs(moved[4]), seq, split_axis=1, concat_axis=1, tiled=True),
        lax.all_to_all(to_pairs(moved[5]), seq, split_axis=1, concat_axis=1, tiled=True),
    )
    my_index = lax.axis_index(seq)
    starts = table[:, 0]
    count_table = table[:, 1]
    offset = (my_index - starts) % sequence_count
    within = jnp.arange(slots, dtype=jnp.int32)[:, None] * sequence_count + offset[None, :]
    alive = within < count_table[None, :]
    target_rank = jnp.where(
        alive, (starts[None, :] + within) // sequence_count, BALANCED_TOKENS
    ).reshape(-1)

    def place(array):
        width = array.shape[-1]
        return (
            jnp.zeros((BALANCED_TOKENS, width), array.dtype)
            .at[target_rank]
            .set(array.reshape(slots * sequence_count, width), mode="drop")
        )

    query_row_block = place(arrived[0]).reshape(
        BALANCED_TOKENS, local_key_value, group_size, HEAD_SIZE
    )
    key_row_block = place(arrived[1]).reshape(BALANCED_TOKENS, local_key_value, HEAD_SIZE)
    value_row_block = place(arrived[2]).reshape(BALANCED_TOKENS, local_key_value, HEAD_SIZE)
    grad_rows = place(arrived[3]).reshape(BALANCED_TOKENS, local_key_value, group_size, HEAD_SIZE)
    lse_rows = (
        place(arrived[4]).astype(jnp.float32).reshape(BALANCED_TOKENS, local_key_value, group_size)
    )
    out_rows = (
        place(arrived[5])
        .astype(jnp.float32)
        .reshape(BALANCED_TOKENS, local_key_value, group_size, HEAD_SIZE)
    )
    delta_rows = (
        jnp.sum(grad_rows.astype(jnp.float32) * out_rows, axis=-1)
        .astype(jnp.bfloat16)
        .astype(jnp.float32)
    )
    gathered = (
        lax.all_gather(key_row_block, seq, axis=0, tiled=True),
        lax.all_gather(value_row_block, seq, axis=0, tiled=True),
    )
    all_keys = gathered[0].reshape(sequence_count, BALANCED_TOKENS, local_key_value, HEAD_SIZE)
    all_values = gathered[1].reshape(sequence_count, BALANCED_TOKENS, local_key_value, HEAD_SIZE)
    rows_per = block_keys // sequence_count
    inner = 1
    outer = BALANCED_TOKENS // rows_per // inner
    query_rank = jnp.arange(BALANCED_TOKENS, dtype=jnp.int32) * sequence_count + my_index
    lse_t = lse_rows.transpose(1, 2, 0)
    delta_t = delta_rows.transpose(1, 2, 0)
    position = jnp.arange(sequence_count * rows_per, dtype=jnp.int32)

    def key_step(query_acc, row_start):
        key_blk = lax.dynamic_slice_in_dim(all_keys, row_start, rows_per, 1).reshape(
            sequence_count * rows_per, local_key_value, HEAD_SIZE
        )
        value_blk = lax.dynamic_slice_in_dim(all_values, row_start, rows_per, 1).reshape(
            sequence_count * rows_per, local_key_value, HEAD_SIZE
        )
        key_owner_rank = (row_start + position % rows_per) * sequence_count + position // rows_per
        mask = key_owner_rank[None, None, None, :] <= query_rank[None, None, :, None]
        scores = (
            jnp.einsum(
                "rgmc,kgc->gmrk", query_row_block, key_blk, preferred_element_type=jnp.float32
            )
            * scale
        )
        probs = jnp.where(mask, jnp.exp(scores - lse_t[..., None]), 0.0)
        dprob = jnp.einsum(
            "rgmc,kgc->gmrk", grad_rows, value_blk, preferred_element_type=jnp.float32
        )
        dscore = probs * (dprob - delta_t[..., None])
        probs_low = probs.astype(jnp.bfloat16)
        dscore_low = dscore.astype(jnp.bfloat16)
        query_acc = query_acc + scale * jnp.einsum(
            "gmrk,kgc->rgmc", dscore_low, key_blk, preferred_element_type=jnp.float32
        )
        key_part = scale * jnp.einsum(
            "gmrk,rgmc->kgc", dscore_low, query_row_block, preferred_element_type=jnp.float32
        )
        value_part = jnp.einsum(
            "gmrk,rgmc->kgc", probs_low, grad_rows, preferred_element_type=jnp.float32
        )
        return (
            query_acc,
            key_part.reshape(sequence_count, rows_per, local_key_value * HEAD_SIZE),
            value_part.reshape(sequence_count, rows_per, local_key_value * HEAD_SIZE),
        )

    def outer_step(query_acc, outer_index):

        def inner_step(query_inner, inner_index):
            row_start = (outer_index * inner + inner_index) * rows_per
            query_new, key_part, value_part = key_step(query_inner, row_start)
            return (query_new, (key_part, value_part))

        query_acc, (key_parts, value_parts) = lax.scan(
            inner_step, query_acc, jnp.arange(inner, dtype=jnp.int32)
        )
        key_parts = key_parts.transpose(1, 0, 2, 3).reshape(
            sequence_count, inner * rows_per, local_key_value * HEAD_SIZE
        )
        value_parts = value_parts.transpose(1, 0, 2, 3).reshape(
            sequence_count, inner * rows_per, local_key_value * HEAD_SIZE
        )
        received = (
            lax.all_to_all(key_parts, seq, split_axis=0, concat_axis=0, tiled=True),
            lax.all_to_all(value_parts, seq, split_axis=0, concat_axis=0, tiled=True),
        )
        return (query_acc, (jnp.sum(received[0], axis=0), jnp.sum(received[1], axis=0)))

    start_acc = jnp.zeros((BALANCED_TOKENS, local_key_value, group_size, HEAD_SIZE), jnp.float32)
    query_acc, (key_sums, value_sums) = lax.scan(
        outer_step, start_acc, jnp.arange(outer, dtype=jnp.int32)
    )
    query_done = query_acc.reshape(
        BALANCED_TOKENS, local_key_value * group_size * HEAD_SIZE
    ).astype(jnp.bfloat16)
    key_done = key_sums.reshape(BALANCED_TOKENS, local_key_value * HEAD_SIZE).astype(jnp.bfloat16)
    value_done = value_sums.reshape(BALANCED_TOKENS, local_key_value * HEAD_SIZE).astype(
        jnp.bfloat16
    )
    safe_rows = jnp.minimum(target_rank, BALANCED_TOKENS - 1)
    alive_flat = alive.reshape(-1)

    def collect(array):
        picked = jnp.where(alive_flat[:, None], array[safe_rows], jnp.zeros((), array.dtype))
        return picked.reshape(slots, sequence_count, array.shape[-1])

    returned = (
        lax.all_to_all(collect(query_done), seq, split_axis=1, concat_axis=1, tiled=True),
        lax.all_to_all(collect(key_done), seq, split_axis=1, concat_axis=1, tiled=True),
        lax.all_to_all(collect(value_done), seq, split_axis=1, concat_axis=1, tiled=True),
    )

    def to_home(array):
        unrolled = jnp.roll(array, -first_rank, axis=1)
        return unrolled.reshape(capacity, 1, array.shape[-1])

    homed = (
        lax.all_to_all(to_home(returned[0]), "head", split_axis=0, concat_axis=1, tiled=True),
        lax.all_to_all(to_home(returned[1]), "head", split_axis=0, concat_axis=1, tiled=True),
        lax.all_to_all(to_home(returned[2]), "head", split_axis=0, concat_axis=1, tiled=True),
    )
    query_grads = homed[0].reshape(home_rows, head_total * homed[0].shape[-1])
    key_gradient_output = homed[1].reshape(home_rows, head_total * homed[1].shape[-1])
    value_gradient = homed[2].reshape(home_rows, head_total * homed[2].shape[-1])
    return (query_grads, key_gradient_output, value_gradient)

LOG2E = 1.4426950408889634
KEY_TILE = 256
ROW_TILE = 128
INFO_ROWS = 16
AUX_LANES = 256
SMEM = pl.BlockSpec(memory_space=pltpu.SMEM)
VMEM = pl.BlockSpec(memory_space=pltpu.VMEM)
ANY = pl.BlockSpec(memory_space=pl.ANY)
GROUP = QUERY_HEADS // KEY_VALUE_HEADS
WIDTH = GROUP * HEAD_SIZE
CHIPS = (5, 4, 1)
CORE = 2
SHARD_TILES = 3
PASS_ROWS = (256, 512, 768)


def pack_pairs_kernel(limit, ranks_ref, k_ref, v_ref, out_ref):
    home_rows = k_ref.shape[0]
    live = jnp.where(ranks_ref[...] < limit, 1.0, 0.0)
    info = jnp.broadcast_to(
        jnp.sum(live, axis=1, keepdims=True), (INFO_ROWS, 2 * HEAD_SIZE)
    ).astype(out_ref.dtype)
    for g in range(KEY_VALUE_HEADS):
        columns = slice(g * HEAD_SIZE, (g + 1) * HEAD_SIZE)
        out_ref[g, :home_rows, :HEAD_SIZE] = k_ref[:, columns]
        out_ref[g, :home_rows, HEAD_SIZE:] = v_ref[:, columns]
        out_ref[g, home_rows:, :] = info


def pack_pairs(limit, ranks, keys, values):
    home_rows = keys.shape[0]
    return pl.pallas_call(
        functools.partial(pack_pairs_kernel, limit),
        out_shape=jax.ShapeDtypeStruct(
            (KEY_VALUE_HEADS, home_rows + INFO_ROWS, 2 * HEAD_SIZE), keys.dtype
        ),
        in_specs=[VMEM] * 3,
        out_specs=VMEM,
        name="pack_pairs",
    )(ranks.reshape(1, home_rows), keys, values)


def pack_rows_kernel(partners, me_ref, q_hbm, do_hbm, out, sems):
    copies = []
    for n, partner in enumerate(partners):
        start = pl.multiple_of((me_ref[0] ^ partner) * WIDTH, HEAD_SIZE)
        for m, source in enumerate((q_hbm, do_hbm)):
            copies.append(
                pltpu.make_async_copy(
                    source.at[:, pl.ds(start, WIDTH)],
                    out.at[n, :, pl.ds(m * WIDTH, WIDTH)],
                    sems.at[2 * n + m],
                )
            )
    for copy in copies:
        copy.start()
    for copy in copies:
        copy.wait()


def pack_rows(partners, me, queries, output_gradient):
    home_rows = queries.shape[0]
    return pl.pallas_call(
        functools.partial(pack_rows_kernel, partners),
        out_shape=jax.ShapeDtypeStruct((len(partners), home_rows, 2 * WIDTH), queries.dtype),
        in_specs=[SMEM, ANY, ANY],
        out_specs=VMEM,
        scratch_shapes=[pltpu.SemaphoreType.DMA((2 * len(partners),))],
        name="pack_rows",
    )(me, queries, output_gradient)


def pack_small_kernel(lse_ref, do_ref, o_ref, out, columns, lanes):
    home_rows = do_ref.shape[0]
    columns[...] = jnp.zeros_like(columns)
    for g in range(KEY_VALUE_HEADS):
        columns[:, 16 * g : 16 * g + GROUP] = lse_ref[:, g * GROUP : (g + 1) * GROUP].astype(
            jnp.float32
        )
    for h in range(QUERY_HEADS):
        head = slice(h * HEAD_SIZE, (h + 1) * HEAD_SIZE)
        product = do_ref[:, head].astype(jnp.float32) * o_ref[:, head].astype(jnp.float32)
        column = 16 * (h // GROUP) + 8 + h % GROUP
        columns[:, column : column + 1] = jnp.sum(product, axis=1, keepdims=True)
    lanes[...] = jnp.zeros_like(lanes)
    lanes[:, :home_rows] = columns[...].T
    for g in range(KEY_VALUE_HEADS):
        out[g] = lanes[16 * g : 16 * g + INFO_ROWS, :].astype(out.dtype)


def pack_small(lse, output_gradient, outputs):
    f32 = jnp.float32
    return pl.pallas_call(
        pack_small_kernel,
        out_shape=jax.ShapeDtypeStruct((KEY_VALUE_HEADS, INFO_ROWS, AUX_LANES), jnp.bfloat16),
        in_specs=[VMEM] * 3,
        out_specs=VMEM,
        scratch_shapes=[
            pltpu.VMEM((lse.shape[0], HEAD_SIZE), f32),
            pltpu.VMEM((HEAD_SIZE, AUX_LANES), f32),
        ],
        compiler_params=pltpu.CompilerParams(vmem_limit_bytes=32 * 1024 * 1024),
        name="pack_small",
    )(lse, output_gradient, outputs)


def compact_kernel(arrived, out, counts_ref):
    home_rows = arrived.shape[1] - INFO_ROWS
    capacity = out.shape[0] - INFO_ROWS
    row = lax.broadcasted_iota(jnp.int32, (capacity, home_rows), 0)
    within = lax.broadcasted_iota(jnp.int32, (capacity, home_rows), 1)
    total = jnp.int32(0)
    picked = []
    for block in range(KEY_VALUE_HEADS):
        count = jnp.max(arrived[block, home_rows:, :].astype(jnp.float32)).astype(jnp.int32)
        counts_ref[block] = count
        hit = (row == within + total) & (within < count)
        picked.append(jnp.where(hit, 1.0, 0.0).astype(jnp.bfloat16))
        total = total + count
    acc = jnp.zeros((capacity, out.shape[1]), jnp.float32)
    for block in range(KEY_VALUE_HEADS):
        acc += jnp.dot(
            picked[block], arrived[block, :home_rows, :], preferred_element_type=jnp.float32
        )
    out[:capacity, :] = acc.astype(out.dtype)
    line = lax.broadcasted_iota(jnp.int32, (INFO_ROWS, out.shape[1]), 0)
    out[capacity:, :] = (
        jnp.where(line == 0, total // 64, jnp.where(line == 1, total % 64, 0))
        .astype(jnp.float32)
        .astype(out.dtype)
    )


def compact(arrived):
    blocks, rows, columns = arrived.shape
    capacity = blocks * (rows - INFO_ROWS) // 2
    return pl.pallas_call(
        compact_kernel,
        out_shape=(
            jax.ShapeDtypeStruct((capacity + INFO_ROWS, columns), arrived.dtype),
            jax.ShapeDtypeStruct((blocks,), jnp.int32),
        ),
        in_specs=[VMEM],
        out_specs=(VMEM, SMEM),
        compiler_params=pltpu.CompilerParams(vmem_limit_bytes=32 * 1024 * 1024),
        name="compact",
    )(arrived)


def load_rows(me, counts_ref, arrays, q_s, do_s, sems):
    home_rows = q_s.shape[0] // KEY_VALUE_HEADS
    q_hbm, do_hbm, beside, pairs, crossed = arrays
    column = pl.multiple_of(me * WIDTH, HEAD_SIZE)
    left, right = pl.ds(0, WIDTH), pl.ds(WIDTH, WIDTH)
    sources = [
        (0, q_hbm.at[:, pl.ds(column, WIDTH)], do_hbm.at[:, pl.ds(column, WIDTH)]),
        (CORE, beside.at[0, :, left], beside.at[0, :, right]),
    ]
    for chip, pair, cross in zip(CHIPS, pairs, crossed):
        sources.append((chip, pair.at[0, :, left], pair.at[0, :, right]))
        sources.append((chip ^ CORE, cross.at[0, :, left], cross.at[0, :, right]))
    plans = []
    for n, (partner, q, do) in enumerate(sources):
        source = me ^ partner
        rows = pl.ds(pl.multiple_of(source * home_rows, 64), home_rows)
        shard = counts_ref[source & ~1] + counts_ref[source | 1]
        needed = ((source & 1) == 0) | (shard > ROW_TILE)
        plans.append(
            (
                needed,
                [
                    pltpu.make_async_copy(q, q_s.at[rows, :], sems.at[2 * n]),
                    pltpu.make_async_copy(do, do_s.at[rows, :], sems.at[2 * n + 1]),
                ],
            )
        )

    def each(act):
        for needed, copies in plans:

            @pl.when(needed)
            def _():
                for copy in copies:
                    act(copy)

    return each


def list_tiles(counts_ref, tiles, starts):
    length = jnp.int32(0)
    total = jnp.int32(0)
    for shard in range(KEY_VALUE_HEADS // 2):
        count = counts_ref[2 * shard] + counts_ref[2 * shard + 1]
        starts[shard] = total
        total = total + count
        for t in range(SHARD_TILES):
            live = count > t * ROW_TILE

            @pl.when(live)
            def _():
                tiles[length] = SHARD_TILES * shard + t

            length = length + live.astype(jnp.int32)
    return length, total


def spread_lanes(aux_s, lse_s, delta_s):
    lane = lax.broadcasted_iota(jnp.int32, (INFO_ROWS, ROW_TILE), 1)
    for shard in range(KEY_VALUE_HEADS // 2):
        low = aux_s[2 * shard].astype(jnp.float32)
        high = aux_s[2 * shard + 1].astype(jnp.float32)
        half = ROW_TILE // 2
        middle = jnp.where(
            lane < half, low[:, ROW_TILE:], pltpu.roll(high[:, :ROW_TILE], half, axis=1)
        )
        last = pltpu.roll(high, AUX_LANES - half, axis=1)[:, :ROW_TILE]
        for t, rows in enumerate((low[:, :ROW_TILE], middle, last)):
            row = SHARD_TILES * shard + t
            for h in range(GROUP):
                columns = slice(h * ROW_TILE, (h + 1) * ROW_TILE)
                lse_s[row : row + 1, columns] = rows[h : h + 1] * LOG2E
                delta_s[row : row + 1, columns] = rows[8 + h : 9 + h]


def row_tile(tile, q_s, do_s, lse_s, delta_s):
    def stack(ref):
        rows = ref[pl.ds(pl.multiple_of(tile * ROW_TILE, ROW_TILE), ROW_TILE), :]
        return jnp.concatenate(
            [rows[:, h * HEAD_SIZE : (h + 1) * HEAD_SIZE] for h in range(GROUP)], axis=0
        )

    return stack(q_s), stack(do_s), lse_s[pl.ds(tile, 1), :], delta_s[pl.ds(tile, 1), :]


def tile_step(key, value, key_t, rows, position, bound, acc_k, acc_v, add_dq):
    q, do, lse, delta = rows
    scale = HEAD_SIZE ** (-0.5)
    dims = (((1,), (1,)), ((), ()))
    scores = lax.dot_general(key, q, dims, preferred_element_type=jnp.float32)
    prob = jnp.where(position <= bound, jnp.exp2(scores * (scale * LOG2E) - lse), 0.0)
    dprob = lax.dot_general(value, do, dims, preferred_element_type=jnp.float32)
    dscore = (prob * (dprob - delta)).astype(jnp.bfloat16)
    acc_v[...] += jnp.dot(prob.astype(jnp.bfloat16), do, preferred_element_type=jnp.float32)
    acc_k[...] += jnp.dot(dscore, q, preferred_element_type=jnp.float32)
    add_dq(jnp.dot(key_t, dscore, preferred_element_type=jnp.float32))


def far_kernel(me_ref, counts_ref, *rest):
    aux_s, arrays, kvs, rest = rest[0], rest[1:10], rest[10:13], rest[13:]
    arrays = (*arrays[:3], arrays[3:6], arrays[6:9])
    downs, dqt_out, full_ref, rest = rest[:3], rest[3], rest[4], rest[5:]
    (
        q_s, do_s, lse_s, delta_s, dqt, kv_s, acc_k, acc_v, tiles, starts, limits, sems, kv_sem,
        down_sem, dq_sem, down_s,
    ) = rest
    capacity = downs[0].shape[0] - INFO_ROWS
    scale = HEAD_SIZE ** (-0.5)
    each = load_rows(me_ref[0], counts_ref, arrays, q_s, do_s, sems)
    each(lambda copy: copy.start())
    kv_copies = [
        pltpu.make_async_copy(kvs[n], kv_s.at[n], kv_sem.at[n])
        for n in range(3)
    ]
    for copy in kv_copies:
        copy.start()
    length, total = list_tiles(counts_ref, tiles, starts)

    def zero_tile(n, carry):
        dqt[tiles[n]] = jnp.zeros(dqt.shape[1:], jnp.float32)
        return carry

    lax.fori_loop(0, length, zero_tile, 0)
    spread_lanes(aux_s, lse_s, delta_s)
    for copy in kv_copies:
        copy.wait()
    most = total
    for n in range(3):
        info = kv_s[n, capacity:, :].astype(jnp.float32)
        limit = (jnp.max(info[0:1]) * 64.0 + jnp.max(info[1:2])).astype(jnp.int32)
        limits[n] = jnp.minimum(limit, capacity)
        most = jnp.maximum(most, limit)
    full = most > capacity
    full_ref[0] = full.astype(jnp.int32)
    for n in range(3):
        down_s[n, capacity:, :] = jnp.full(
            (INFO_ROWS, 2 * HEAD_SIZE), jnp.where(full, 1.0, 0.0)
        ).astype(jnp.bfloat16)
    each(lambda copy: copy.wait())
    lane = lax.broadcasted_iota(jnp.int32, (1, WIDTH), 1) % ROW_TILE

    def block_step(step, carry):
        index = 2 - step
        limit = limits[index]

        def run(rows):
            key = kv_s[index, :rows, :HEAD_SIZE]
            value = kv_s[index, :rows, HEAD_SIZE:]
            key_t = key.T
            acc_k[:rows] = jnp.zeros((rows, HEAD_SIZE), jnp.float32)
            acc_v[:rows] = jnp.zeros((rows, HEAD_SIZE), jnp.float32)
            position = lax.broadcasted_iota(jnp.int32, (rows, 1), 0)

            def row_step(n, inner):
                tile = tiles[n]
                shard = tile // SHARD_TILES
                count = counts_ref[2 * shard] + counts_ref[2 * shard + 1]
                alive = lane < count - (tile % SHARD_TILES) * ROW_TILE
                bound = jnp.where(alive, limit - 1, -1)

                def add_dq(part):
                    dqt[tile] += part

                tile_step(
                    key, value, key_t, row_tile(tile, q_s, do_s, lse_s, delta_s), position, bound,
                    acc_k.at[pl.ds(0, rows), :], acc_v.at[pl.ds(0, rows), :], add_dq,
                )
                return inner

            lax.fori_loop(0, length, row_step, 0)
            down_s[index, :rows, :HEAD_SIZE] = (acc_k[:rows] * scale).astype(jnp.bfloat16)
            down_s[index, :rows, HEAD_SIZE:] = acc_v[:rows].astype(jnp.bfloat16)
            if rows < capacity:
                down_s[index, rows:capacity, :] = jnp.zeros(
                    (capacity - rows, 2 * HEAD_SIZE), jnp.bfloat16
                )

        below = 0
        for rows in PASS_ROWS:

            @pl.when((limit > below) & (limit <= rows))
            def _():
                run(rows)

            below = rows

        @pl.when(limit == 0)
        def _():
            down_s[index, :capacity, :] = jnp.zeros((capacity, 2 * HEAD_SIZE), jnp.bfloat16)

        return carry

    lax.fori_loop(0, 3, block_step, 0)
    down_copies = [
        pltpu.make_async_copy(down_s.at[n], downs[n], down_sem.at[n]) for n in range(3)
    ]
    for copy in down_copies:
        copy.start()

    def dq_copy(n):
        tile = tiles[n]
        return pltpu.make_async_copy(dqt.at[tile], dqt_out.at[tile], dq_sem.at[n])

    def start_dq(n, carry):
        dq_copy(n).start()
        return carry

    def wait_dq(n, carry):
        dq_copy(n).wait()
        return carry

    lax.fori_loop(0, length, start_dq, 0)
    for copy in down_copies:
        copy.wait()
    lax.fori_loop(0, length, wait_dq, 0)


def own_kernel(me_ref, counts_ref, *rest):
    aux_s, arrays, kv, dqt_in, rest = rest[0], rest[1:10], rest[10], rest[11], rest[13:]
    arrays = (*arrays[:3], arrays[3:6], arrays[6:9])
    kept, passed, own, rest = rest[:4], rest[4:8], rest[8], rest[9:]
    q_s, do_s, lse_s, delta_s, dqt, acc_k, acc_v, tiles, starts, sems, dq_sem = rest
    capacity = kv.shape[0] - INFO_ROWS
    home_rows = kept[0].shape[0]
    scale = HEAD_SIZE ** (-0.5)
    me = me_ref[0]
    each = load_rows(me, counts_ref, arrays, q_s, do_s, sems)
    each(lambda copy: copy.start())
    length, total = list_tiles(counts_ref, tiles, starts)
    limit = jnp.minimum(total, capacity)

    def dq_copy(n):
        tile = tiles[n]
        return pltpu.make_async_copy(dqt_in.at[tile], dqt.at[tile], dq_sem.at[n])

    def start_dq(n, carry):
        dq_copy(n).start()
        return carry

    def wait_dq(n, carry):
        dq_copy(n).wait()
        return carry

    lax.fori_loop(0, length, start_dq, 0)
    own[...] = jnp.zeros_like(own)
    spread_lanes(aux_s, lse_s, delta_s)
    each(lambda copy: copy.wait())
    lax.fori_loop(0, length, wait_dq, 0)
    lane = lax.broadcasted_iota(jnp.int32, (1, WIDTH), 1) % ROW_TILE

    def key_step(kt, carry):
        start = pl.multiple_of(kt * KEY_TILE, KEY_TILE)
        key = kv[pl.ds(start, KEY_TILE), :HEAD_SIZE]
        value = kv[pl.ds(start, KEY_TILE), HEAD_SIZE:]
        key_t = key.T
        acc_k[...] = jnp.zeros_like(acc_k)
        acc_v[...] = jnp.zeros_like(acc_v)
        position = start + lax.broadcasted_iota(jnp.int32, (KEY_TILE, 1), 0)

        def row_step(n, inner):
            tile = tiles[n]
            shard = tile // SHARD_TILES
            offset = (tile % SHARD_TILES) * ROW_TILE
            count = counts_ref[2 * shard] + counts_ref[2 * shard + 1]
            first = starts[shard] + offset

            @pl.when(first + ROW_TILE > start)
            def _():
                bound = jnp.where(lane < count - offset, first + lane, -1)

                def add_dq(part):
                    dqt[tile] += part

                tile_step(
                    key, value, key_t, row_tile(tile, q_s, do_s, lse_s, delta_s), position, bound,
                    acc_k, acc_v, add_dq,
                )

            return inner

        lax.fori_loop(0, length, row_step, 0)
        own[pl.ds(start, KEY_TILE), :HEAD_SIZE] = acc_k[...] * scale
        own[pl.ds(start, KEY_TILE), HEAD_SIZE:] = acc_v[...]
        return carry

    lax.fori_loop(0, (limit + KEY_TILE - 1) // KEY_TILE, key_step, 0)

    half = ROW_TILE // 2
    outs = [(chip, kept[n]) for n, chip in enumerate((0, *CHIPS))]
    outs += [(chip ^ CORE, passed[n]) for n, chip in enumerate((0, *CHIPS))]
    for partner, out in outs:
        block = me ^ partner
        shard = block // 2
        count = counts_ref[block & ~1] + counts_ref[block | 1]

        def put(rows, t, first):
            live = count > t * ROW_TILE
            size = rows.stop - rows.start

            @pl.when(live)
            def _():
                for h in range(GROUP):
                    columns = slice(h * HEAD_SIZE, (h + 1) * HEAD_SIZE)
                    part = (dqt[SHARD_TILES * shard + t, :, columns] * scale).T
                    out[rows, columns] = part[first : first + size].astype(jnp.bfloat16)

            @pl.when(jnp.logical_not(live))
            def _():
                out[rows, :] = jnp.zeros((size, WIDTH), jnp.bfloat16)

        @pl.when((block & 1) == 0)
        def _():
            put(slice(0, ROW_TILE), 0, 0)
            put(slice(ROW_TILE, home_rows), 1, 0)

        @pl.when((block & 1) == 1)
        def _():
            put(slice(0, half), 1, half)
            put(slice(half, home_rows), 2, 0)


def row_scratch(plane_rows):
    bf16, f32 = jnp.bfloat16, jnp.float32
    tile_count = plane_rows // ROW_TILE
    return [
        pltpu.VMEM((plane_rows, WIDTH), bf16),
        pltpu.VMEM((plane_rows, WIDTH), bf16),
        pltpu.VMEM((tile_count, WIDTH), f32),
        pltpu.VMEM((tile_count, WIDTH), f32),
        pltpu.VMEM((tile_count, HEAD_SIZE, WIDTH), f32),
    ]


def far_attention(me, counts, small, arrays, kvs):
    bf16, f32 = jnp.bfloat16, jnp.float32
    blocks = KEY_VALUE_HEADS
    rows = kvs[0].shape[0]
    columns = 2 * HEAD_SIZE
    plane_rows = 2 * (rows - INFO_ROWS)
    tile_count = plane_rows // ROW_TILE
    return pl.pallas_call(
        far_kernel,
        out_shape=(jax.ShapeDtypeStruct((rows, columns), bf16),) * 3
        + (
            jax.ShapeDtypeStruct((tile_count, HEAD_SIZE, WIDTH), f32),
            jax.ShapeDtypeStruct((1,), jnp.int32),
        ),
        in_specs=[SMEM] * 2 + [VMEM] + [ANY] * 12,
        out_specs=[ANY] * 4 + [SMEM],
        scratch_shapes=row_scratch(plane_rows)
        + [
            pltpu.VMEM((3, rows, columns), bf16),
            pltpu.VMEM((rows - INFO_ROWS, HEAD_SIZE), f32),
            pltpu.VMEM((rows - INFO_ROWS, HEAD_SIZE), f32),
            pltpu.SMEM((tile_count + 1,), jnp.int32),
            pltpu.SMEM((blocks,), jnp.int32),
            pltpu.SMEM((3,), jnp.int32),
            pltpu.SemaphoreType.DMA((2 * blocks,)),
            pltpu.SemaphoreType.DMA((3,)),
            pltpu.SemaphoreType.DMA((3,)),
            pltpu.SemaphoreType.DMA((tile_count,)),
            pltpu.VMEM((3, rows, columns), bf16),
        ],
        compiler_params=pltpu.CompilerParams(vmem_limit_bytes=48 * 1024 * 1024),
        cost_estimate=pl.CostEstimate(
            flops=10_000_000_000, bytes_accessed=12_000_000, transcendentals=8_000_000
        ),
        name="far_attention",
    )(me, counts, small, *arrays, *kvs)


def own_attention(me, counts, small, arrays, kv, dqt, note):
    bf16, f32 = jnp.bfloat16, jnp.float32
    blocks = KEY_VALUE_HEADS
    capacity = kv.shape[0] - INFO_ROWS
    plane_rows = 2 * capacity
    tile_count = plane_rows // ROW_TILE
    return pl.pallas_call(
        own_kernel,
        out_shape=(jax.ShapeDtypeStruct((plane_rows // blocks, WIDTH), bf16),) * 8
        + (jax.ShapeDtypeStruct((capacity, 2 * HEAD_SIZE), f32),),
        in_specs=[SMEM] * 2 + [VMEM] + [ANY] * 9 + [VMEM, ANY, ANY],
        out_specs=[VMEM] * 9,
        scratch_shapes=row_scratch(plane_rows)
        + [
            pltpu.VMEM((KEY_TILE, HEAD_SIZE), f32),
            pltpu.VMEM((KEY_TILE, HEAD_SIZE), f32),
            pltpu.SMEM((tile_count + 1,), jnp.int32),
            pltpu.SMEM((blocks,), jnp.int32),
            pltpu.SemaphoreType.DMA((2 * blocks,)),
            pltpu.SemaphoreType.DMA((tile_count,)),
        ],
        compiler_params=pltpu.CompilerParams(vmem_limit_bytes=48 * 1024 * 1024),
        cost_estimate=pl.CostEstimate(
            flops=1_000_000, bytes_accessed=100_000, transcendentals=1_000
        ),
        name="own_attention",
    )(me, counts, small, *arrays, kv, dqt, note)


def unpack_rows_kernel(me_ref, kept, passed, *rest):
    pairs, out = rest[:3], rest[3]
    home_rows = kept.shape[0]
    me = me_ref[0]

    def put(partner, rows):
        start = pl.multiple_of((me ^ partner) * WIDTH, HEAD_SIZE)
        out[:, pl.ds(start, WIDTH)] = rows

    put(0, kept[...])
    put(CORE, passed[...])
    for chip, pair in zip(CHIPS, pairs):
        put(chip, pair[:home_rows])
        put(chip ^ CORE, pair[home_rows:])


def unpack_rows(me, kept, passed, pairs):
    home_rows = kept.shape[0]
    return pl.pallas_call(
        unpack_rows_kernel,
        out_shape=jax.ShapeDtypeStruct((home_rows, KEY_VALUE_HEADS * WIDTH), jnp.bfloat16),
        in_specs=[SMEM] + [VMEM] * 5,
        out_specs=VMEM,
        name="unpack_rows",
    )(me, kept, passed, *pairs)


def plane_device(queries, keys, values, outputs, output_gradient, lse, ranks):
    planes = lax.axis_size("outer")
    plane = ("inner", "head")
    blocks = KEY_VALUE_HEADS
    home_rows = queries.shape[0]
    plane_rows = blocks * home_rows
    capacity = plane_rows // 2
    surviving_tokens = BALANCED_TOKENS * planes * lax.axis_size("inner")
    bf16, f32 = jnp.bfloat16, jnp.float32
    me = lax.axis_index(plane).reshape(1).astype(jnp.int32)

    def swap(array, k):
        return lax.ppermute(array, plane, [(i, i ^ k) for i in range(blocks)])

    sent = pack_pairs(surviving_tokens, ranks, keys, values)
    arrived = lax.all_to_all(sent, plane, split_axis=0, concat_axis=0, tiled=True)
    packed = [
        pack_rows((chip, chip ^ CORE), me, queries, output_gradient) for chip in CHIPS
    ]
    pairs = [swap(rows, chip) for rows, chip in zip(packed, CHIPS)]
    beside = swap(pack_rows((CORE,), me, queries, output_gradient), CORE)
    small = lax.all_to_all(
        pack_small(lse, output_gradient, outputs), plane, split_axis=0, concat_axis=0, tiled=True
    )
    crossed = [swap(pair[1:], CORE) for pair in pairs]
    arrays = [queries, output_gradient, beside, *pairs, *crossed]

    mine, counts = compact(arrived)
    up = [
        lax.ppermute(mine, "outer", [(i, i + k) for i in range(planes - k)])
        for k in range(1, planes)
    ]

    *down, dqt, full = far_attention(me, counts, small, arrays, up)
    note = swap(down[0][capacity:, :HEAD_SIZE], CORE)
    *dqs, own = own_attention(me, counts, small, arrays, mine, dqt, note)
    kept, passed = dqs[:4], dqs[4:]
    full = full[0] > 0
    for k in (3, 2, 1):
        back = lax.ppermute(down[k - 1], "outer", [(i + k, i) for i in range(planes - k)])
        own = own + back[:capacity].astype(f32)
        full = full | (back[capacity, 0] > 0)
    passed = [swap(rows, CORE) for rows in passed]
    joined = [jnp.concatenate([kept[n], passed[n]], axis=0) for n in range(1, 4)]
    own, joined[2] = lax.optimization_barrier((own, joined[2]))
    pairs = [swap(rows, chip) for rows, chip in zip(joined, CHIPS)]
    dq_home = unpack_rows(me, kept[0], passed[0], pairs)

    starts = jnp.cumsum(counts) - counts
    within = jnp.arange(home_rows, dtype=jnp.int32)
    local = jnp.where(within[None, :] < counts[:, None], starts[:, None] + within[None, :], -1)
    pick = (
        jnp.arange(capacity, dtype=jnp.int32)[:, None] == local.reshape(1, plane_rows)
    ).astype(bf16)
    spread = lax.dot_general(
        pick, own.astype(bf16), (((0,), (0,)), ((), ())), preferred_element_type=f32
    ).astype(bf16)
    kv_home = lax.all_to_all(
        spread.reshape(blocks, home_rows, 2 * HEAD_SIZE),
        plane, split_axis=0, concat_axis=0, tiled=True,
    )
    dk = kv_home[:, :, :HEAD_SIZE].transpose(1, 0, 2).reshape(home_rows, blocks * HEAD_SIZE)
    dv = kv_home[:, :, HEAD_SIZE:].transpose(1, 0, 2).reshape(home_rows, blocks * HEAD_SIZE)
    return (dq_home, dk, dv), full


def solution(mesh):
    spec = P(("seq", "head"), None)
    heads = mesh.shape["head"]
    inner = max(KEY_VALUE_HEADS // heads, 1)
    planes = mesh.shape["seq"] // inner
    if planes != 4 or inner * heads != KEY_VALUE_HEADS:
        return jax.shard_map(
            per_device,
            mesh=mesh,
            in_specs=(spec,) * 6 + (P(("seq", "head")),),
            out_specs=(spec,) * 3,
            check_vma=False,
        )
    axes = ("outer", "inner", "head")

    def device(*blocks):
        fast, full = plane_device(*blocks)
        return lax.cond(full, lambda: per_device(*blocks, seq=("outer", "inner")), lambda: fast)

    return jax.shard_map(
        device,
        mesh=Mesh(mesh.devices.reshape(planes, inner, heads), axes),
        in_specs=(P(axes, None),) * 6 + (P(axes),),
        out_specs=(P(axes, None),) * 3,
        check_vma=False,
    )
```

profile of v0, /device:TPU:8, one launch (start us, length us, event | category | flops | bytes accessed | tf_op | source)
XLA Modules:
  0.0 209.5 jit_solution(11920636947004900237)
XLA Ops:
  7.2 2.2 %pack_pairs.1 = bf16[8,208,256]{2,1,0:T(8,128)(2,1)} custom-call(s32[1,192]{1,0:T(1,128)} %bitcast.289, bf16[192,1024]{1,0:T(8,128)(2,1)} %k_ref.1, bf16[192,1024]{1,0:T(8,128)(2,1)} %v_ref.1), custom_call_target="tpu_custom_call" | custom-call | tf_op jit(solution)/shard_map/pack_pairs/pallas_call | solution.py:242
  9.3 3.7 %all-to-all-start.20 = ((bf16[8,208,256]{2,1,0:T(8,128)(2,1)}), bf16[8,208,256]{2,1,0:T(8,128)(2,1)S(1)}, u32[]{:S(2)}, u32[]{:S(2)}) async-start(bf16[8,208,256]{2,1,0:T(8,128)(2,1)} %pack_pairs.1), calls=%async_computation.20 | async-start | bytes 1703936 | tf_op jit(solution)/shard_map/all_to_all | solution.py:802
  13.1 2.3 %pack_rows.5 = bf16[2,192,1280]{2,1,0:T(8,128)(2,1)} custom-call(s32[1]{0:T(128)} %bitcast.48.me_ref, bf16[192,5120]{1,0:T(8,128)(2,1)} %rest_1_.3, bf16[192,5120]{1,0:T(8,128)(2,1)} %rest_2_.3), custom_call_target="tpu_custom_call" | custom-call | tf_op jit(solution)/shard_map/pack_rows/pallas_call | solution.py:273
  15.4 3.0 %collective-permute-start.1 = (bf16[2,192,1280]{2,1,0:T(8,128)(2,1)}, bf16[2,192,1280]{2,1,0:T(8,128)(2,1)S(1)}, u32[]{:S(2)}, u32[]{:S(2)}) collective-permute-start(bf16[2,192,1280]{2,1,0:T(8,128)(2,1)} %pack_rows.5), channel_id=1, source_target_pairs={{0,5},{1,4},{2,7},{3,6},{4,1},{5,0},{6,3},{7,2},{8,13},{9,12},{10,... | collective-permute-start | bytes 2949128 | tf_op jit(solution)/shard_map/ppermute | solution.py:799
  18.3 2.3 %pack_rows.6 = bf16[2,192,1280]{2,1,0:T(8,128)(2,1)} custom-call(s32[1]{0:T(128)} %bitcast.48.me_ref, bf16[192,5120]{1,0:T(8,128)(2,1)} %rest_1_.3, bf16[192,5120]{1,0:T(8,128)(2,1)} %rest_2_.3), custom_call_target="tpu_custom_call" | custom-call | tf_op jit(solution)/shard_map/pack_rows/pallas_call | solution.py:273
  20.7 0.6 collective-permute-start.2
  21.3 2.3 %pack_rows.7 = bf16[2,192,1280]{2,1,0:T(8,128)(2,1)} custom-call(s32[1]{0:T(128)} %bitcast.48.me_ref, bf16[192,5120]{1,0:T(8,128)(2,1)} %rest_1_.3, bf16[192,5120]{1,0:T(8,128)(2,1)} %rest_2_.3), custom_call_target="tpu_custom_call" | custom-call | tf_op jit(solution)/shard_map/pack_rows/pallas_call | solution.py:273
  23.7 1.9 pack_rows.4
  25.7 0.3 all-to-all-done.20.arrived
  26.0 1.8 compact.1
  27.8 3.5 %collective-permute-start.7 = (bf16[784,256]{1,0:T(8,128)(2,1)}, bf16[784,256]{1,0:T(8,128)(2,1)S(1)}, u32[]{:S(2)}, u32[]{:S(2)}) collective-permute-start(bf16[784,256]{1,0:T(8,128)(2,1)} %get-tuple-element.385.rest_10_), channel_id=1, source_target_pairs={{0,8},{8,16},{16,24},{1,9},{9,17},{17,25},{2,10},{10,18},{18,26},{... | collective-permute-start | bytes 1204232 | tf_op jit(solution)/shard_map/ppermute | solution.py:816
  31.3 16.7 %collective-permute-done.1.rest_4_ = bf16[2,192,1280]{2,1,0:T(8,128)(2,1)S(1)} collective-permute-done((bf16[2,192,1280]{2,1,0:T(8,128)(2,1)}, bf16[2,192,1280]{2,1,0:T(8,128)(2,1)S(1)}, u32[]{:S(2)}, u32[]{:S(2)}) %collective-permute-start.1) | collective-permute-done | bytes 983072 | tf_op jit(solution)/shard_map/ppermute | solution.py:799
  48.0 0.8 slice.65
  48.8 18.9 %collective-permute-done.2.rest_5_ = bf16[2,192,1280]{2,1,0:T(8,128)(2,1)S(1)} collective-permute-done((bf16[2,192,1280]{2,1,0:T(8,128)(2,1)}, bf16[2,192,1280]{2,1,0:T(8,128)(2,1)S(1)}, u32[]{:S(2)}, u32[]{:S(2)}) %collective-permute-start.2) | collective-permute-done | bytes 983072 | tf_op jit(solution)/shard_map/ppermute | solution.py:799
  67.7 0.9 slice.66
  68.6 0.2 copy-done.27
  68.8 1.8 slice.67
  70.6 0.3 collective-permute-start.6
  70.9 5.3 %collective-permute-start.8 = (bf16[784,256]{1,0:T(8,128)(2,1)}, bf16[784,256]{1,0:T(8,128)(2,1)}, u32[]{:S(2)}, u32[]{:S(2)}) collective-permute-start(bf16[784,256]{1,0:T(8,128)(2,1)} %get-tuple-element.385.rest_10_), channel_id=1, source_target_pairs={{0,16},{8,24},{1,17},{9,25},{2,18},{10,26},{3,19},{11,27},{4,20},{... | collective-permute-start | bytes 1204232 | tf_op jit(solution)/shard_map/ppermute | solution.py:816
  76.2 0.7 copy-done.13
  76.9 1.4 collective-permute-start.9
  78.5 3.6 %pack_small.1 = bf16[8,16,256]{2,1,0:T(8,128)(2,1)S(1)} custom-call(bf16[192,40]{1,0:T(8,128)(2,1)S(1)} %copy.214.lse_ref, bf16[192,5120]{1,0:T(8,128)(2,1)} %rest_2_.3, bf16[192,5120]{1,0:T(8,128)(2,1)} %o_ref.1), custom_call_target="tpu_custom_call" | custom-call | tf_op jit(solution)/shard_map/pack_small/pallas_call | solution.py:303
  82.1 7.3 %all_to_all.185.rest_0_ = bf16[8,16,256]{2,1,0:T(8,128)(2,1)S(1)} all-to-all(bf16[8,16,256]{2,1,0:T(8,128)(2,1)S(1)} %pack_small.1), channel_id=1, replica_groups=mesh['outer'=4,'inner'=4,'head'=2] {'inner','head'}, dimensions={0} | all-to-all | bytes 131072 | tf_op jit(solution)/shard_map/all_to_all | solution.py:808
  89.4 12.4 %collective-permute-done.8.rest_11_ = bf16[784,256]{1,0:T(8,128)(2,1)} collective-permute-done((bf16[784,256]{1,0:T(8,128)(2,1)}, bf16[784,256]{1,0:T(8,128)(2,1)}, u32[]{:S(2)}, u32[]{:S(2)}) %collective-permute-start.8) | collective-permute-done | bytes 401440 | tf_op jit(solution)/shard_map/ppermute | solution.py:816
  101.8 12.1 %far_attention.1 = (bf16[784,256]{1,0:T(8,128)(2,1)S(1)}, bf16[784,256]{1,0:T(8,128)(2,1)S(1)}, bf16[784,256]{1,0:T(8,128)(2,1)S(1)}, f32[12,128,640]{2,1,0:T(8,128)}, s32[1]{0:T(128)}) custom-call(s32[1]{0:T(128)} %bitcast.48.me_ref, s32[8]{0:T(128)S(1)} %get-tuple-element.384.counts_ref, bf16[8,16,256]{2,1,0:T(8,128)(2,1)S(1)} %all_to_all.185.rest_0_, ...), custom_call_target="tpu_custom_call" | custom-call | flops 10000000000 | bytes 12000000 | tf_op jit(solution)/shard_map/far_attention/pallas_call | solution.py:700
  113.9 0.8 copy-done.11
  114.7 0.8 copy-done.12
  115.4 0.7 copy-done.10
  116.2 0.8 reduce-window.9
  117.0 1.9 collective-permute-start.12
  118.9 1.4 collective-permute-start.10
  120.3 1.3 collective-permute-start.11
  121.6 0.6 copy-done.6
  122.2 1.0 copy-done.1
  123.3 0.7 copy-done.7
  123.9 0.7 copy-done.9
  124.6 13.3 %own_attention.1 = (bf16[192,640]{1,0:T(8,128)(2,1)S(1)}, bf16[192,640]{1,0:T(8,128)(2,1)S(1)}, bf16[192,640]{1,0:T(8,128)(2,1)S(1)}, bf16[192,640]{1,0:T(8,128)...) custom-call(s32[1]{0:T(128)} %bitcast.48.me_ref, ...), custom_call_target="tpu_custom_call" | custom-call | flops 1000000 | bytes 100000 | tf_op jit(solution)/shard_map/own_attention/pallas_call | solution.py:737
  137.9 0.7 copy-done.2
  138.6 0.7 copy-done.3
  139.2 0.7 copy-done.5
  139.9 0.7 copy-done.15
  140.6 0.7 copy-done.17
  141.3 0.7 copy-done.18
  142.0 0.5 collective-permute-start.14
  142.7 1.1 collective-permute-done.14
  143.8 0.4 collective-permute-start.18
  144.2 1.0 pad_maximum_fusion
  145.2 12.1 %collective-permute-done.11 = bf16[784,256]{1,0:T(8,128)(2,1)} collective-permute-done((bf16[784,256]{1,0:T(8,128)(2,1)}, bf16[784,256]{1,0:T(8,128)(2,1)}, u32[]{:S(2)}, u32[]{:S(2)}) %collective-permute-start.11) | collective-permute-done | bytes 401440 | tf_op jit(solution)/shard_map/ppermute | solution.py:826
  157.3 1.4 convert_add_fusion
  158.7 2.3 %fusion.63 = bf16[1536,256]{1,0:T(8,128)(2,1)} fusion(s32[1536]{0:T(1024)S(1)} %select_n.177, bf16[768,256]{1,0:T(8,128)(2,1)S(1)} %convert_add_fusion), kind=kOutput, calls=%fused_computation.125 | convolution fusion | flops 605552640 | bytes 1185792 | tf_op jit(solution)/shard_map/dot_general | solution.py:841
  161.0 3.7 %all-to-all-start.22 = ((bf16[8,192,256]{2,1,0:T(8,128)(2,1)}), bf16[8,192,256]{2,1,0:T(8,128)(2,1)S(1)}, u32[]{:S(2)}, u32[]{:S(2)}) async-start(bf16[8,192,256]{2,1,0:T(8,128)(2,1)} %bitcast.56), calls=%async_computation.22 | async-start | bytes 1572864 | tf_op jit(solution)/shard_map/all_to_all | solution.py:844
  164.8 2.9 %collective-permute-start.17 = (bf16[384,640]{1,0:T(8,128)(2,1)S(1)}, bf16[384,640]{1,0:T(8,128)(2,1)S(1)}, u32[]{:S(2)}, u32[]{:S(2)}) collective-permute-start(bf16[384,640]{1,0:T(8,128)(2,1)S(1)} %pad_maximum_fusion.1), channel_id=1, source_target_pairs={{0,5},{1,4},{2,7},{3,6},{4,1},{5,0},{6,3},{7,2},{8,13},{9,12},{10,... | collective-permute-start | bytes 1474568 | tf_op jit(solution)/shard_map/ppermute | solution.py:799
  167.7 0.8 pad_maximum_fusion.2
  168.5 0.5 collective-permute-start.19
  169.8 1.2 slice.68
  171.7 1.2 slice.69
  173.4 1.2 slice.70
  175.2 13.1 %collective-permute-done.17.rest_0_ = bf16[384,640]{1,0:T(8,128)(2,1)S(1)} collective-permute-done((bf16[384,640]{1,0:T(8,128)(2,1)S(1)}, bf16[384,640]{1,0:T(8,128)(2,1)S(1)}, u32[]{:S(2)}, u32[]{:S(2)}) %collective-permute-start.17) | collective-permute-done | bytes 491552 | tf_op jit(solution)/shard_map/ppermute | solution.py:799
  188.3 9.2 %collective-permute-done.19.rest_1_ = bf16[384,640]{1,0:T(8,128)(2,1)S(1)} collective-permute-done((bf16[384,640]{1,0:T(8,128)(2,1)}, bf16[384,640]{1,0:T(8,128)(2,1)S(1)}, u32[]{:S(2)}, u32[]{:S(2)}) %collective-permute-start.19) | collective-permute-done | bytes 491552 | tf_op jit(solution)/shard_map/ppermute | solution.py:799
  197.5 0.8 copy-done.32
  198.3 3.1 %unpack_rows.1 = bf16[192,5120]{1,0:T(8,128)(2,1)} custom-call(s32[1]{0:T(128)} %bitcast.48.me_ref, bf16[192,640]{1,0:T(8,128)(2,1)} %copy-done.2, bf16[192,640]{1,0:T(8,128)(2,1)} %copy-done.33, bf16[384,640]{1,0:T(8,128)(2,1)} %copy-done.31, bf16[384,640]{1,0:T(8,128)(2,1)} %copy-done.32, bf16[384,640]{1,0:T(8,128)(2,1)} %collective-permute-done.20.rest_2_), custom_call_target="tpu_custom_call" | custom-call | tf_op jit(solution)/shard_map/unpack_rows/pallas_call | solution.py:778
  201.4 0.2 slice_bitcast_fusion
  201.6 1.0 conditional.1
  201.6 1.0 copy_bitcast_fusion
  (73 shorter events, 0.8 us)
Async XLA Ops:
  9.3 16.6 %all-to-all-start.20 = ((bf16[8,208,256]{2,1,0:T(8,128)(2,1)}), bf16[8,208,256]{2,1,0:T(8,128)(2,1)S(1)}, u32[]{:S(2)}, u32[]{:S(2)}) async-start(bf16[8,208,256]{2,1,0:T(8,128)(2,1)} %pack_pairs.1), calls=%async_computation.20 | async-start | bytes 1703936 | tf_op jit(solution)/shard_map/all_to_all | solution.py:802
  15.4 32.6 %collective-permute-start.1 = (bf16[2,192,1280]{2,1,0:T(8,128)(2,1)}, bf16[2,192,1280]{2,1,0:T(8,128)(2,1)S(1)}, u32[]{:S(2)}, u32[]{:S(2)}) collective-permute-start(bf16[2,192,1280]{2,1,0:T(8,128)(2,1)} %pack_rows.5), channel_id=1, source_target_pairs={{0,5},{1,4},{2,7},{3,6},{4,1},{5,0},{6,3},{7,2},{8,13},{9,12},{10,... | collective-permute-start | bytes 2949128 | tf_op jit(solution)/shard_map/ppermute | solution.py:799
  20.7 47.0 %collective-permute-start.2 = (bf16[2,192,1280]{2,1,0:T(8,128)(2,1)}, bf16[2,192,1280]{2,1,0:T(8,128)(2,1)S(1)}, u32[]{:S(2)}, u32[]{:S(2)}) collective-permute-start(bf16[2,192,1280]{2,1,0:T(8,128)(2,1)} %pack_rows.6), channel_id=1, source_target_pairs={{0,4},{1,5},{2,6},{3,7},{4,0},{5,1},{6,2},{7,3},{8,12},{9,13},{10,... | collective-permute-start | bytes 2949128 | tf_op jit(solution)/shard_map/ppermute | solution.py:799
  23.7 44.9 %collective-permute-start.3 = (bf16[2,192,1280]{2,1,0:T(8,128)(2,1)}, bf16[2,192,1280]{2,1,0:T(8,128)(2,1)}, u32[]{:S(2)}, u32[]{:S(2)}) collective-permute-start(bf16[2,192,1280]{2,1,0:T(8,128)(2,1)} %pack_rows.7), channel_id=1, source_target_pairs={{0,1},{1,0},{2,3},{3,2},{4,5},{5,4},{6,7},{7,6},{8,9},{9,8},{10,11... | collective-permute-start | bytes 2949128 | tf_op jit(solution)/shard_map/ppermute | solution.py:799
  25.6 52.7 %copy-start.34 = (bf16[192,40]{0,1:T(8,128)(2,1)S(1)}, bf16[192,40]{0,1:T(8,128)(2,1)}, u32[]{:S(2)}) copy-start(bf16[192,40]{0,1:T(8,128)(2,1)} %param.20) | copy-start | bytes 46084
  25.6 45.3 %collective-permute-start = (bf16[1,192,1280]{2,1,0:T(8,128)(2,1)}, bf16[1,192,1280]{2,1,0:T(8,128)(2,1)S(1)}, u32[]{:S(2)}, u32[]{:S(2)}) collective-permute-start(bf16[1,192,1280]{2,1,0:T(8,128)(2,1)} %pack_rows.4), channel_id=1, source_target_pairs={{0,2},{1,3},{2,0},{3,1},{4,6},{5,7},{6,4},{7,5},{8,10},{9,11},{10,... | collective-permute-start | bytes 1474568 | tf_op jit(solution)/shard_map/ppermute | solution.py:799
  27.8 88.4 %copy-start.8 = (s32[8]{0:T(128)}, s32[8]{0:T(128)S(1)}, u32[]{:S(2)}) copy-start(s32[8]{0:T(128)S(1)} %get-tuple-element.384.counts_ref) | copy-start | bytes 100
  27.8 48.3 %collective-permute-start.7 = (bf16[784,256]{1,0:T(8,128)(2,1)}, bf16[784,256]{1,0:T(8,128)(2,1)S(1)}, u32[]{:S(2)}, u32[]{:S(2)}) collective-permute-start(bf16[784,256]{1,0:T(8,128)(2,1)} %get-tuple-element.385.rest_10_), channel_id=1, source_target_pairs={{0,8},{8,16},{16,24},{1,9},{9,17},{17,25},{2,10},{10,18},{18,26},{... | collective-permute-start | bytes 1204232 | tf_op jit(solution)/shard_map/ppermute | solution.py:816
  48.8 52.9 %collective-permute-start.4 = (bf16[1,192,1280]{2,1,0:T(8,128)(2,1)}, bf16[1,192,1280]{2,1,0:T(8,128)(2,1)S(1)}, u32[]{:S(2)}, u32[]{:S(2)}) collective-permute-start(bf16[1,192,1280]{2,1,0:T(8,128)(2,1)} %slice.65), channel_id=1, source_target_pairs={{0,2},{1,3},{2,0},{3,1},{4,6},{5,7},{6,4},{7,5},{8,10},{9,11},{10,... | collective-permute-start | bytes 1474568 | tf_op jit(solution)/shard_map/ppermute | solution.py:799
  67.7 1.1 copy-start.27
  68.6 33.2 %collective-permute-start.5 = (bf16[1,192,1280]{2,1,0:T(8,128)(2,1)}, bf16[1,192,1280]{2,1,0:T(8,128)(2,1)S(1)}, u32[]{:S(2)}, u32[]{:S(2)}) collective-permute-start(bf16[1,192,1280]{2,1,0:T(8,128)(2,1)} %slice.66), channel_id=1, source_target_pairs={{0,2},{1,3},{2,0},{3,1},{4,6},{5,7},{6,4},{7,5},{8,10},{9,11},{10,... | collective-permute-start | bytes 1474568 | tf_op jit(solution)/shard_map/ppermute | solution.py:799
  70.6 31.1 %collective-permute-start.6 = (bf16[1,192,1280]{2,1,0:T(8,128)(2,1)}, bf16[1,192,1280]{2,1,0:T(8,128)(2,1)S(1)}, u32[]{:S(2)}, u32[]{:S(2)}) collective-permute-start(bf16[1,192,1280]{2,1,0:T(8,128)(2,1)} %slice.67), channel_id=1, source_target_pairs={{0,2},{1,3},{2,0},{3,1},{4,6},{5,7},{6,4},{7,5},{8,10},{9,11},{10,... | collective-permute-start | bytes 1474568 | tf_op jit(solution)/shard_map/ppermute | solution.py:799
  70.9 30.8 %collective-permute-start.8 = (bf16[784,256]{1,0:T(8,128)(2,1)}, bf16[784,256]{1,0:T(8,128)(2,1)}, u32[]{:S(2)}, u32[]{:S(2)}) collective-permute-start(bf16[784,256]{1,0:T(8,128)(2,1)} %get-tuple-element.385.rest_10_), channel_id=1, source_target_pairs={{0,16},{8,24},{1,17},{9,25},{2,18},{10,26},{3,19},{11,27},{4,20},{... | collective-permute-start | bytes 1204232 | tf_op jit(solution)/shard_map/ppermute | solution.py:816
  76.2 0.7 copy-start.13
  76.9 24.8 %collective-permute-start.9 = (bf16[784,256]{1,0:T(8,128)(2,1)}, bf16[784,256]{1,0:T(8,128)(2,1)}, u32[]{:S(2)}, u32[]{:S(2)}) collective-permute-start(bf16[784,256]{1,0:T(8,128)(2,1)} %get-tuple-element.385.rest_10_), channel_id=1, source_target_pairs={{0,24},{1,25},{2,26},{3,27},{4,28},{5,29},{6,30},{7,31}} | collective-permute-start | bytes 1204232 | tf_op jit(solution)/shard_map/ppermute | solution.py:816
  78.5 23.3 %copy-start.14 = (bf16[784,256]{1,0:T(8,128)(2,1)S(1)}, bf16[784,256]{1,0:T(8,128)(2,1)}, u32[]{:S(2)}) copy-start(bf16[784,256]{1,0:T(8,128)(2,1)} %copy-done.13) | copy-start | bytes 1204228
  78.5 23.3 %copy-start.20 = (bf16[192,5120]{1,0:T(8,128)(2,1)S(1)}, bf16[192,5120]{1,0:T(8,128)(2,1)}, u32[]{:S(2)}) copy-start(bf16[192,5120]{1,0:T(8,128)(2,1)} %rest_2_.3) | copy-start | bytes 5898244
  101.8 12.2 %copy-start = (bf16[1,192,1280]{2,1,0:T(8,128)(2,1)}, bf16[1,192,1280]{2,1,0:T(8,128)(2,1)S(1)}, u32[]{:S(2)}) copy-start(bf16[1,192,1280]{2,1,0:T(8,128)(2,1)S(1)} %collective-permute-done.6.rest_9_) | copy-start | bytes 1474564
  113.9 0.8 copy-start.11
  114.7 0.8 copy-start.12
  115.4 0.7 copy-start.10
  116.2 5.4 %collective-permute-start.13 = (bf16[16,128]{1,0:T(8,128)(2,1)S(1)}, bf16[16,128]{1,0:T(8,128)(2,1)S(1)}, u32[]{:S(2)}, u32[]{:S(2)}) collective-permute-start(bf16[16,128]{1,0:T(8,128)(2,1)S(1)} %slice.51), channel_id=1, source_target_pairs={{0,2},{1,3},{2,0},{3,1},{4,6},{5,7},{6,4},{7,5},{8,10},{9,11},{10,... | collective-permute-start | bytes 12296 | tf_op jit(solution)/shard_map/ppermute | solution.py:799
  117.0 40.3 %collective-permute-start.12 = (bf16[784,256]{1,0:T(8,128)(2,1)}, bf16[784,256]{1,0:T(8,128)(2,1)}, u32[]{:S(2)}, u32[]{:S(2)}) collective-permute-start(bf16[784,256]{1,0:T(8,128)(2,1)} %copy-done.10), channel_id=1, source_target_pairs={{8,0},{16,8},{24,16},{9,1},{17,9},{25,17},{10,2},{18,10},{26,18},{... | collective-permute-start | bytes 1204232 | tf_op jit(solution)/shard_map/ppermute | solution.py:826
  118.9 26.3 %collective-permute-start.10 = (bf16[784,256]{1,0:T(8,128)(2,1)}, bf16[784,256]{1,0:T(8,128)(2,1)}, u32[]{:S(2)}, u32[]{:S(2)}) collective-permute-start(bf16[784,256]{1,0:T(8,128)(2,1)} %copy-done.12), channel_id=1, source_target_pairs={{24,0},{25,1},{26,2},{27,3},{28,4},{29,5},{30,6},{31,7}} | collective-permute-start | bytes 1204232 | tf_op jit(solution)/shard_map/ppermute | solution.py:826
  120.3 37.0 %collective-permute-start.11 = (bf16[784,256]{1,0:T(8,128)(2,1)}, bf16[784,256]{1,0:T(8,128)(2,1)}, u32[]{:S(2)}, u32[]{:S(2)}) collective-permute-start(bf16[784,256]{1,0:T(8,128)(2,1)} %copy-done.11), channel_id=1, source_target_pairs={{16,0},{24,8},{17,1},{25,9},{18,2},{26,10},{19,3},{27,11},{20,4},{... | collective-permute-start | bytes 1204232 | tf_op jit(solution)/shard_map/ppermute | solution.py:826
  121.6 0.6 copy-start.6
  122.2 1.0 copy-start.1
  123.3 0.7 copy-start.7
  123.9 0.7 copy-start.9
  124.6 17.9 %copy-start.38 = (s32[8,1]{0,1:T(1,128)S(1)}, s32[8,1]{0,1:T(1,128)}, u32[]{:S(2)}) copy-start(s32[8,1]{0,1:T(1,128)} %reduce-window.9) | copy-start | bytes 100
  137.9 0.7 copy-start.2
  138.6 0.7 copy-start.3
  139.2 0.7 copy-start.5
  139.9 0.7 copy-start.15
  140.6 0.7 copy-start.17
  141.3 0.7 copy-start.18
  142.0 1.8 collective-permute-start.14
  142.7 22.1 %collective-permute-start.16 = (bf16[192,640]{1,0:T(8,128)(2,1)}, bf16[192,640]{1,0:T(8,128)(2,1)S(1)}, u32[]{:S(2)}, u32[]{:S(2)}) collective-permute-start(bf16[192,640]{1,0:T(8,128)(2,1)} %copy-done.18), channel_id=1, source_target_pairs={{0,2},{1,3},{2,0},{3,1},{4,6},{5,7},{6,4},{7,5},{8,10},{9,11},{10,... | collective-permute-start | bytes 737288 | tf_op jit(solution)/shard_map/ppermute | solution.py:799
  143.8 23.9 %collective-permute-start.18 = (bf16[192,640]{1,0:T(8,128)(2,1)}, bf16[192,640]{1,0:T(8,128)(2,1)S(1)}, u32[]{:S(2)}, u32[]{:S(2)}) collective-permute-start(bf16[192,640]{1,0:T(8,128)(2,1)} %copy-done.17), channel_id=1, source_target_pairs={{0,2},{1,3},{2,0},{3,1},{4,6},{5,7},{6,4},{7,5},{8,10},{9,11},{10,... | collective-permute-start | bytes 737288 | tf_op jit(solution)/shard_map/ppermute | solution.py:799
  158.7 6.0 %copy-start.4 = (bf16[192,640]{1,0:T(8,128)(2,1)S(1)}, bf16[192,640]{1,0:T(8,128)(2,1)}, u32[]{:S(2)}) copy-start(bf16[192,640]{1,0:T(8,128)(2,1)} %copy-done.3) | copy-start | bytes 737284
  161.0 8.1 %copy-start.16 = (bf16[192,640]{1,0:T(8,128)(2,1)S(1)}, bf16[192,640]{1,0:T(8,128)(2,1)}, u32[]{:S(2)}) copy-start(bf16[192,640]{1,0:T(8,128)(2,1)} %copy-done.15) | copy-start | bytes 737284
  161.0 40.4 %all-to-all-start.22 = ((bf16[8,192,256]{2,1,0:T(8,128)(2,1)}), bf16[8,192,256]{2,1,0:T(8,128)(2,1)S(1)}, u32[]{:S(2)}, u32[]{:S(2)}) async-start(bf16[8,192,256]{2,1,0:T(8,128)(2,1)} %bitcast.56), calls=%async_computation.22 | async-start | bytes 1572864 | tf_op jit(solution)/shard_map/all_to_all | solution.py:844
  164.8 23.5 %collective-permute-start.17 = (bf16[384,640]{1,0:T(8,128)(2,1)S(1)}, bf16[384,640]{1,0:T(8,128)(2,1)S(1)}, u32[]{:S(2)}, u32[]{:S(2)}) collective-permute-start(bf16[384,640]{1,0:T(8,128)(2,1)S(1)} %pad_maximum_fusion.1), channel_id=1, source_target_pairs={{0,5},{1,4},{2,7},{3,6},{4,1},{5,0},{6,3},{7,2},{8,13},{9,12},{10,... | collective-permute-start | bytes 1474568 | tf_op jit(solution)/shard_map/ppermute | solution.py:799
  168.5 29.0 %collective-permute-start.19 = (bf16[384,640]{1,0:T(8,128)(2,1)}, bf16[384,640]{1,0:T(8,128)(2,1)S(1)}, u32[]{:S(2)}, u32[]{:S(2)}) collective-permute-start(bf16[384,640]{1,0:T(8,128)(2,1)} %pad_maximum_fusion.2), channel_id=1, source_target_pairs={{0,4},{1,5},{2,6},{3,7},{4,0},{5,1},{6,2},{7,3},{8,12},{9,13},{10,... | collective-permute-start | bytes 1474568 | tf_op jit(solution)/shard_map/ppermute | solution.py:799
  169.1 28.4 %collective-permute-start.20 = (bf16[384,640]{1,0:T(8,128)(2,1)S(1)}, bf16[384,640]{1,0:T(8,128)(2,1)}, u32[]{:S(2)}, u32[]{:S(2)}) collective-permute-start(bf16[384,640]{1,0:T(8,128)(2,1)S(1)} %pad_maximum_fusion), channel_id=1, source_target_pairs={{0,1},{1,0},{2,3},{3,2},{4,5},{5,4},{6,7},{7,6},{8,9},{9,8},{10,11... | collective-permute-start | bytes 1474568 | tf_op jit(solution)/shard_map/ppermute | solution.py:799
  169.2 6.0 %collective-permute-start.15 = (bf16[192,640]{1,0:T(8,128)(2,1)S(1)}, bf16[192,640]{1,0:T(8,128)(2,1)S(1)}, u32[]{:S(2)}, u32[]{:S(2)}) collective-permute-start(bf16[192,640]{1,0:T(8,128)(2,1)S(1)} %copy-done.16), channel_id=1, source_target_pairs={{0,2},{1,3},{2,0},{3,1},{4,6},{5,7},{6,4},{7,5},{8,10},{9,11},{10,... | collective-permute-start | bytes 737288 | tf_op jit(solution)/shard_map/ppermute | solution.py:799
  175.2 23.1 %copy-start.33 = (bf16[192,640]{1,0:T(8,128)(2,1)}, bf16[192,640]{1,0:T(8,128)(2,1)S(1)}, u32[]{:S(2)}) copy-start(bf16[192,640]{1,0:T(8,128)(2,1)S(1)} %collective-permute-done.15.passed) | copy-start | bytes 737284
  188.3 9.2 %copy-start.31 = (bf16[384,640]{1,0:T(8,128)(2,1)}, bf16[384,640]{1,0:T(8,128)(2,1)S(1)}, u32[]{:S(2)}) copy-start(bf16[384,640]{1,0:T(8,128)(2,1)S(1)} %collective-permute-done.17.rest_0_) | copy-start | bytes 1474564
  197.5 0.8 copy-start.32
  198.3 3.3 %copy-start.21 = (bf16[192,5120]{1,0:T(8,128)(2,1)S(1)}, bf16[192,5120]{1,0:T(8,128)(2,1)}, u32[]{:S(2)}) copy-start(bf16[192,5120]{1,0:T(8,128)(2,1)} %rest_2_.3) | copy-start | bytes 5898244
  198.3 3.3 %copy-start.28 = (bf16[192,1024]{1,0:T(8,128)(2,1)S(1)}, bf16[192,1024]{1,0:T(8,128)(2,1)}, u32[]{:S(2)}) copy-start(bf16[192,1024]{1,0:T(8,128)(2,1)} %k_ref.1) | copy-start | bytes 1179652
  198.3 3.3 %copy-start.35 = (bf16[192,40]{0,1:T(8,128)(2,1)S(1)}, bf16[192,40]{0,1:T(8,128)(2,1)}, u32[]{:S(2)}) copy-start(bf16[192,40]{0,1:T(8,128)(2,1)} %param.20) | copy-start | bytes 46084
  198.3 3.3 %copy-start.36 = (s32[192]{0:T(256)S(1)}, s32[192]{0:T(256)}, u32[]{:S(2)}) copy-start(s32[192]{0:T(256)} %param.21) | copy-start | bytes 2308
where the time goes:
time: 210 us; the launch traced here: 209 us
  waiting for transfers between devices  83.7 us (40%)
  Pallas kernels  44.9 us (21%)
  starting transfers between devices  30.7 us (15%)
  local copies, waits for them, and re-layouts  19.6 us (9%)
  between operations  16.8 us (8%)
  blocking collectives  7.3 us (3%)
  other arithmetic  4.09 us (2%)
  matrix products  2.31 us (1%)
    ppermute x15, waiting for transfers between devices, swap(): return lax.ppermute(array, plane, [(i, i ^ k) for i in range(blocks)])  59 us
    pallas_call x1, Pallas kernels, own_attention(): pl.pallas_call(own_kernel, out_shape=(jax.ShapeDtypeStruct((plane_rows //...  13.3 us
    ppermute x3, waiting for transfers between devices, plane_device(): lax.ppermute(mine, 'outer', [(i, i + k) for i in range(planes - k)])  12.4 us
    pallas_call x1, Pallas kernels, far_attention(): pl.pallas_call(far_kernel, out_shape=(jax.ShapeDtypeStruct((rows, columns...  12.1 us
    ppermute x3, waiting for transfers between devices, plane_device(): lax.ppermute(down[k - 1], 'outer', [(i + k, i) for i in range(planes - k)])  12.1 us
    unnamed x61, local copies, waits for them, and re-layouts  11.3 us
    ppermute x3, starting transfers between devices, plane_device(): lax.ppermute(mine, 'outer', [(i, i + k) for i in range(planes - k)])  10.2 us
    pallas_call x4, Pallas kernels, pack_rows(): pl.pallas_call(functools.partial(pack_rows_kernel, partners), out_shape=j...  8.83 us
  transfers between devices with their start and end apart: 23, of which 8 were waited for; matrix products, arithmetic and copies ran while one was open for 7% of the time, Pallas kernels for 15%

commit v1 on v0

--- a/solution.py
+++ b/solution.py
@@ -215,7 +215,7 @@
 AUX_LANES = 256
 SMEM = pl.BlockSpec(memory_space=pltpu.SMEM)
 VMEM = pl.BlockSpec(memory_space=pltpu.VMEM)
-ANY = pl.BlockSpec(memory_space=pl.ANY)
+HBM = pl.BlockSpec(memory_space=pltpu.HBM)
 GROUP = QUERY_HEADS // KEY_VALUE_HEADS
 WIDTH = GROUP * HEAD_SIZE
 CHIPS = (5, 4, 1)
@@ -273,7 +273,7 @@
     return pl.pallas_call(
         functools.partial(pack_rows_kernel, partners),
         out_shape=jax.ShapeDtypeStruct((len(partners), home_rows, 2 * WIDTH), queries.dtype),
-        in_specs=[SMEM, ANY, ANY],
+        in_specs=[SMEM, HBM, HBM],
         out_specs=VMEM,
         scratch_shapes=[pltpu.SemaphoreType.DMA((2 * len(partners),))],
         name="pack_rows",
@@ -577,10 +577,10 @@
 def own_kernel(me_ref, counts_ref, *rest):
     aux_s, arrays, kv, dqt_in, rest = rest[0], rest[1:10], rest[10], rest[11], rest[13:]
     arrays = (*arrays[:3], arrays[3:6], arrays[6:9])
-    kept, passed, own, rest = rest[:4], rest[4:8], rest[8], rest[9:]
-    q_s, do_s, lse_s, delta_s, dqt, acc_k, acc_v, tiles, starts, sems, dq_sem = rest
+    dq_out, own, rest = rest[0], rest[1], rest[2:]
+    q_s, do_s, lse_s, delta_s, dqt, acc_k, acc_v, tiles, starts, sems, dq_sem, dq_s, out_sem = rest
     capacity = kv.shape[0] - INFO_ROWS
-    home_rows = kept[0].shape[0]
+    home_rows = dq_out.shape[1]
     scale = HEAD_SIZE ** (-0.5)
     me = me_ref[0]
     each = load_rows(me, counts_ref, arrays, q_s, do_s, sems)
@@ -645,37 +645,34 @@
     lax.fori_loop(0, (limit + KEY_TILE - 1) // KEY_TILE, key_step, 0)
 
     half = ROW_TILE // 2
-    outs = [(chip, kept[n]) for n, chip in enumerate((0, *CHIPS))]
-    outs += [(chip ^ CORE, passed[n]) for n, chip in enumerate((0, *CHIPS))]
-    for partner, out in outs:
-        block = me ^ partner
+    copies = []
+    for block in range(KEY_VALUE_HEADS):
         shard = block // 2
-        count = counts_ref[block & ~1] + counts_ref[block | 1]
-
-        def put(rows, t, first):
+        count = counts_ref[2 * shard] + counts_ref[2 * shard + 1]
+        if block % 2 == 0:
+            pieces = ((0, ROW_TILE, 0, 0), (ROW_TILE, half, 1, 0))
+        else:
+            pieces = ((0, half, 1, half), (half, ROW_TILE, 2, 0))
+        for offset, size, t, first in pieces:
             live = count > t * ROW_TILE
-            size = rows.stop - rows.start
+            rows = slice(offset, offset + size)
 
             @pl.when(live)
             def _():
                 for h in range(GROUP):
                     columns = slice(h * HEAD_SIZE, (h + 1) * HEAD_SIZE)
                     part = (dqt[SHARD_TILES * shard + t, :, columns] * scale).T
-                    out[rows, columns] = part[first : first + size].astype(jnp.bfloat16)
+                    dq_s[block, rows, columns] = part[first : first + size].astype(jnp.bfloat16)
 
             @pl.when(jnp.logical_not(live))
             def _():
-                out[rows, :] = jnp.zeros((size, WIDTH), jnp.bfloat16)
-
-        @pl.when((block & 1) == 0)
-        def _():
-            put(slice(0, ROW_TILE), 0, 0)
-            put(slice(ROW_TILE, home_rows), 1, 0)
-
-        @pl.when((block & 1) == 1)
-        def _():
-            put(slice(0, half), 1, half)
-            put(slice(half, home_rows), 2, 0)
+                dq_s[block, rows, :] = jnp.zeros((size, WIDTH), jnp.bfloat16)
+
+        copy = pltpu.make_async_copy(dq_s.at[block], dq_out.at[block], out_sem.at[block])
+        copy.start()
+        copies.append(copy)
+    for copy in copies:
+        copy.wait()
 
 
 def row_scratch(plane_rows):
@@ -704,8 +701,8 @@
             jax.ShapeDtypeStruct((tile_count, HEAD_SIZE, WIDTH), f32),
             jax.ShapeDtypeStruct((1,), jnp.int32),
         ),
-        in_specs=[SMEM] * 2 + [VMEM] + [ANY] * 12,
-        out_specs=[ANY] * 4 + [SMEM],
+        in_specs=[SMEM] * 2 + [VMEM] + [HBM] * 12,
+        out_specs=[HBM] * 4 + [SMEM],
         scratch_shapes=row_scratch(plane_rows)
         + [
             pltpu.VMEM((3, rows, columns), bf16),
@@ -736,10 +733,12 @@
     tile_count = plane_rows // ROW_TILE
     return pl.pallas_call(
         own_kernel,
-        out_shape=(jax.ShapeDtypeStruct((plane_rows // blocks, WIDTH), bf16),) * 8
-        + (jax.ShapeDtypeStruct((capacity, 2 * HEAD_SIZE), f32),),
-        in_specs=[SMEM] * 2 + [VMEM] + [ANY] * 9 + [VMEM, ANY, ANY],
-        out_specs=[VMEM] * 9,
+        out_shape=(
+            jax.ShapeDtypeStruct((blocks, plane_rows // blocks, WIDTH), bf16),
+            jax.ShapeDtypeStruct((capacity, 2 * HEAD_SIZE), f32),
+        ),
+        in_specs=[SMEM] * 2 + [VMEM] + [HBM] * 9 + [VMEM, HBM, HBM],
+        out_specs=[HBM, VMEM],
         scratch_shapes=row_scratch(plane_rows)
         + [
             pltpu.VMEM((KEY_TILE, HEAD_SIZE), f32),
@@ -748,6 +747,8 @@
             pltpu.SMEM((blocks,), jnp.int32),
             pltpu.SemaphoreType.DMA((2 * blocks,)),
             pltpu.SemaphoreType.DMA((tile_count,)),
+            pltpu.VMEM((blocks, plane_rows // blocks, WIDTH), bf16),
+            pltpu.SemaphoreType.DMA((blocks,)),
         ],
         compiler_params=pltpu.CompilerParams(vmem_limit_bytes=48 * 1024 * 1024),
         cost_estimate=pl.CostEstimate(
@@ -757,31 +758,53 @@
     )(me, counts, small, *arrays, kv, dqt, note)
 
 
-def unpack_rows_kernel(me_ref, kept, passed, *rest):
-    pairs, out = rest[:3], rest[3]
-    home_rows = kept.shape[0]
-    me = me_ref[0]
-
-    def put(partner, rows):
-        start = pl.multiple_of((me ^ partner) * WIDTH, HEAD_SIZE)
-        out[:, pl.ds(start, WIDTH)] = rows
-
-    put(0, kept[...])
-    put(CORE, passed[...])
-    for chip, pair in zip(CHIPS, pairs):
-        put(chip, pair[:home_rows])
-        put(chip ^ CORE, pair[home_rows:])
-
-
-def unpack_rows(me, kept, passed, pairs):
-    home_rows = kept.shape[0]
+def unpack_rows_kernel(parts, out):
+    for g in range(KEY_VALUE_HEADS):
+        out[:, g * WIDTH : (g + 1) * WIDTH] = parts[g]
+
+
+def unpack_rows(parts):
     return pl.pallas_call(
         unpack_rows_kernel,
-        out_shape=jax.ShapeDtypeStruct((home_rows, KEY_VALUE_HEADS * WIDTH), jnp.bfloat16),
-        in_specs=[SMEM] + [VMEM] * 5,
+        out_shape=jax.ShapeDtypeStruct((parts.shape[1], KEY_VALUE_HEADS * WIDTH), parts.dtype),
+        in_specs=[VMEM],
         out_specs=VMEM,
         name="unpack_rows",
-    )(me, kept, passed, *pairs)
+    )(parts)
+
+
+def combine_kernel(counts_ref, own, *rest):
+    backs, out = rest[:3], rest[3]
+    home_rows = out.shape[1]
+    capacity = own.shape[0]
+    total = own[...]
+    for back in backs:
+        total += back[:capacity, :].astype(jnp.float32)
+    total = total.astype(jnp.bfloat16)
+    within = lax.broadcasted_iota(jnp.int32, (home_rows, capacity), 0)
+    place = lax.broadcasted_iota(jnp.int32, (home_rows, capacity), 1)
+    start = jnp.int32(0)
+    for block in range(KEY_VALUE_HEADS):
+        count = counts_ref[block]
+        hit = (place == within + start) & (within < count)
+        out[block] = jnp.dot(
+            jnp.where(hit, 1.0, 0.0).astype(jnp.bfloat16),
+            total,
+            preferred_element_type=jnp.float32,
+        ).astype(jnp.bfloat16)
+        start = start + count
+
+
+def combine(counts, own, backs, home_rows):
+    blocks = KEY_VALUE_HEADS
+    return pl.pallas_call(
+        combine_kernel,
+        out_shape=jax.ShapeDtypeStruct((blocks, home_rows, own.shape[1]), jnp.bfloat16),
+        in_specs=[SMEM] + [VMEM] * 4,
+        out_specs=VMEM,
+        compiler_params=pltpu.CompilerParams(vmem_limit_bytes=32 * 1024 * 1024),
+        name="combine",
+    )(counts, own, *backs)
 
 
 def plane_device(queries, keys, values, outputs, output_gradient, lse, ranks):
@@ -808,43 +831,31 @@
     small = lax.all_to_all(
         pack_small(lse, output_gradient, outputs), plane, split_axis=0, concat_axis=0, tiled=True
     )
+    mine, counts = compact(arrived)
+    up = [lax.ppermute(mine, "outer", [(i, i + 1) for i in range(planes - 1)])]
+    up[0], small = lax.optimization_barrier((up[0], small))
+    up.append(lax.ppermute(up[0], "outer", [(i, i + 1) for i in range(1, planes - 1)]))
+    up.append(lax.ppermute(up[1], "outer", [(i, i + 1) for i in range(2, planes - 1)]))
+    up[2], *pairs = lax.optimization_barrier((up[2], *pairs))
     crossed = [swap(pair[1:], CORE) for pair in pairs]
     arrays = [queries, output_gradient, beside, *pairs, *crossed]
 
-    mine, counts = compact(arrived)
-    up = [
-        lax.ppermute(mine, "outer", [(i, i + k) for i in range(planes - k)])
-        for k in range(1, planes)
-    ]
-
     *down, dqt, full = far_attention(me, counts, small, arrays, up)
     note = swap(down[0][capacity:, :HEAD_SIZE], CORE)
-    *dqs, own = own_attention(me, counts, small, arrays, mine, dqt, note)
-    kept, passed = dqs[:4], dqs[4:]
+    backs = [
+        lax.ppermute(down[k - 1], "outer", [(i + k, i) for i in range(planes - k)])
+        for k in (3, 2, 1)
+    ]
+    dq, own = own_attention(me, counts, small, arrays, mine, dqt, note)
+    dq_home = unpack_rows(
+        lax.all_to_all(dq, plane, split_axis=0, concat_axis=0, tiled=True)
+    )
+    kv_home = lax.all_to_all(
+        combine(counts, own, backs, home_rows), plane, split_axis=0, concat_axis=0, tiled=True
+    )
     full = full[0] > 0
-    for k in (3, 2, 1):
-        back = lax.ppermute(down[k - 1], "outer", [(i + k, i) for i in range(planes - k)])
-        own = own + back[:capacity].astype(f32)
+    for back in backs:
         full = full | (back[capacity, 0] > 0)
-    passed = [swap(rows, CORE) for rows in passed]
-    joined = [jnp.concatenate([kept[n], passed[n]], axis=0) for n in range(1, 4)]
-    own, joined[2] = lax.optimization_barrier((own, joined[2]))
-    pairs = [swap(rows, chip) for rows, chip in zip(joined, CHIPS)]
-    dq_home = unpack_rows(me, kept[0], passed[0], pairs)
-
-    starts = jnp.cumsum(counts) - counts
-    within = jnp.arange(home_rows, dtype=jnp.int32)
-    local = jnp.where(within[None, :] < counts[:, None], starts[:, None] + within[None, :], -1)
-    pick = (
-        jnp.arange(capacity, dtype=jnp.int32)[:, None] == local.reshape(1, plane_rows)
-    ).astype(bf16)
-    spread = lax.dot_general(
-        pick, own.astype(bf16), (((0,), (0,)), ((), ())), preferred_element_type=f32
-    ).astype(bf16)
-    kv_home = lax.all_to_all(
-        spread.reshape(blocks, home_rows, 2 * HEAD_SIZE),
-        plane, split_axis=0, concat_axis=0, tiled=True,
-    )
     dk = kv_home[:, :, :HEAD_SIZE].transpose(1, 0, 2).reshape(home_rows, blocks * HEAD_SIZE)
     dv = kv_home[:, :, HEAD_SIZE:].transpose(1, 0, 2).reshape(home_rows, blocks * HEAD_SIZE)
     return (dq_home, dk, dv), full

time: 210 us -> 219 us (1.043)
  the two profiles are of different devices: /device:TPU:8 before, /device:TPU:17 now
where the time goes in v1:
time: 219 us; the launch traced here: 215 us
  blocking collectives  67.5 us (31%)
  waiting for transfers between devices  56.9 us (26%)
  Pallas kernels  43.6 us (20%)
  starting transfers between devices  23.7 us (11%)
  between operations  16.9 us (8%)
  local copies, waits for them, and re-layouts  6.29 us (3%)
    all_to_all x1, blocking collectives, plane_device(): lax.all_to_all(pack_small(lse, output_gradient, outputs), plane, split_ax...  35.7 us
    ppermute x3, waiting for transfers between devices, plane_device(): lax.ppermute(down[k - 1], 'outer', [(i + k, i) for i in range(planes - k)])  20.7 us
    all_to_all x1, waiting for transfers between devices, plane_device(): lax.all_to_all(dq, plane, split_axis=0, concat_axis=0, tiled=True)  18.7 us
    all_to_all x1, blocking collectives, plane_device(): lax.all_to_all(sent, plane, split_axis=0, concat_axis=0, tiled=True)  17 us
    pallas_call x1, Pallas kernels, far_attention(): pl.pallas_call(far_kernel, out_shape=(jax.ShapeDtypeStruct((rows, columns...  15.9 us
    all_to_all x1, blocking collectives, plane_device(): lax.all_to_all(combine(counts, own, backs, home_rows), plane, split_axis=...  14.8 us
    ppermute x1, waiting for transfers between devices, plane_device(): lax.ppermute(up[0], 'outer', [(i, i + 1) for i in range(1, planes - 1)])  10.6 us
    pallas_call x4, Pallas kernels, pack_rows(): pl.pallas_call(functools.partial(pack_rows_kernel, partners), out_shape=j...  8.29 us
  transfers between devices with their start and end apart: 15, of which 9 were waited for; matrix products, arithmetic and copies ran while one was open for 1% of the time, Pallas kernels for 9%

profile of v1, /device:TPU:17, one launch (start us, length us, event | category | flops | bytes accessed | tf_op | source)
XLA Modules:
  0.0 214.8 jit_solution(17475251205347458353)
XLA Ops:
  7.2 0.0 copy-start.5
  7.2 2.3 %pack_pairs.1 = bf16[8,208,256]{2,1,0:T(8,128)(2,1)} custom-call(s32[1,192]{1,0:T(1,128)} %bitcast.283, bf16[192,1024]{1,0:T(8,128)(2,1)} %k_ref.1, bf16[192,1024]{1,0:T(8,128)(2,1)} %v_ref.1), custom_call_target="tpu_custom_call" | custom-call | tf_op jit(solution)/shard_map/pack_pairs/pallas_call | solution.py:242
  9.5 17.0 %all_to_all.190.arrived = bf16[8,208,256]{2,1,0:T(8,128)(2,1)S(1)} all-to-all(bf16[8,208,256]{2,1,0:T(8,128)(2,1)} %pack_pairs.1), channel_id=1, replica_groups=mesh['outer'=4,'inner'=4,'head'=2] {'inner','head'}, dimensions={0} | all-to-all | bytes 1703936 | tf_op jit(solution)/shard_map/all_to_all | solution.py:825
  26.5 1.1 compact.1
  27.6 3.2 %collective-permute-start = (bf16[784,256]{1,0:T(8,128)(2,1)S(1)}, bf16[784,256]{1,0:T(8,128)(2,1)}, u32[]{:S(2)}, u32[]{:S(2)}) collective-permute-start(bf16[784,256]{1,0:T(8,128)(2,1)S(1)} %get-tuple-element.382.rest_10_), channel_id=1, source_target_pairs={{0,8},{8,16},{16,24},{1,9},{9,17},{17,25},{2,10},{10,18},{18,26},{... | collective-permute-start | bytes 1204232 | tf_op jit(solution)/shard_map/ppermute | solution.py:835
  30.8 0.0 copy-done.5
  30.8 2.1 pack_rows.5
  32.9 0.4 collective-permute-start.4
  33.3 2.1 pack_rows.6
  35.4 0.0 copy-start.19
  35.4 1.3 collective-permute-start.5
  36.7 2.3 %pack_rows.7 = bf16[2,192,1280]{2,1,0:T(8,128)(2,1)} custom-call(s32[1]{0:T(128)} %bitcast.48.me_ref, bf16[192,5120]{1,0:T(8,128)(2,1)} %rest_1_.3, bf16[192,5120]{1,0:T(8,128)(2,1)} %rest_2_.3), custom_call_target="tpu_custom_call" | custom-call | tf_op jit(solution)/shard_map/pack_rows/pallas_call | solution.py:273
  39.0 1.2 collective-permute-start.6
  40.1 0.0 copy-done.19
  40.1 0.1 copy.217.lse_ref
  40.3 3.5 %pack_small.1 = bf16[8,16,256]{2,1,0:T(8,128)(2,1)S(1)} custom-call(bf16[192,40]{1,0:T(8,128)(2,1)S(1)} %copy.217.lse_ref, bf16[192,5120]{1,0:T(8,128)(2,1)} %rest_2_.3, bf16[192,5120]{1,0:T(8,128)(2,1)} %o_ref.1), custom_call_target="tpu_custom_call" | custom-call | tf_op jit(solution)/shard_map/pack_small/pallas_call | solution.py:303
  43.7 35.7 %all_to_all.191.rest_0_ = bf16[8,16,256]{2,1,0:T(8,128)(2,1)S(1)} all-to-all(bf16[8,16,256]{2,1,0:T(8,128)(2,1)S(1)} %pack_small.1), channel_id=1, replica_groups=mesh['outer'=4,'inner'=4,'head'=2] {'inner','head'}, dimensions={0} | all-to-all | bytes 131072 | tf_op jit(solution)/shard_map/all_to_all | solution.py:831
  79.4 0.0 collective-permute-done.rest_10_
  79.4 1.9 collective-permute-start.2
  81.3 10.6 %collective-permute-done.2.rest_11_ = bf16[784,256]{1,0:T(8,128)(2,1)} collective-permute-done((bf16[784,256]{1,0:T(8,128)(2,1)}, bf16[784,256]{1,0:T(8,128)(2,1)}, u32[]{:S(2)}, u32[]{:S(2)}) %collective-permute-start.2) | collective-permute-done | bytes 401440 | tf_op jit(solution)/shard_map/ppermute | solution.py:837
  92.0 3.0 %collective-permute-start.3 = (bf16[784,256]{1,0:T(8,128)(2,1)}, bf16[784,256]{1,0:T(8,128)(2,1)}, u32[]{:S(2)}, u32[]{:S(2)}) collective-permute-start(bf16[784,256]{1,0:T(8,128)(2,1)} %collective-permute-done.2.rest_11_), channel_id=1, source_target_pairs={{16,24},{17,25},{18,26},{19,27},{20,28},{21,29},{22,30},{23,31}} | collective-permute-start | bytes 1204232 | tf_op jit(solution)/shard_map/ppermute | solution.py:838
  94.9 1.9 pack_rows.4
  96.8 0.0 copy-start.6
  96.8 1.4 collective-permute-start.1
  98.2 0.0 collective-permute-done.4.rest_4_
  98.2 0.0 collective-permute-done.5.rest_5_
  98.2 0.0 collective-permute-done.6.rest_6_
  98.2 0.0 copy-start.2
  98.2 3.8 %collective-permute-done.3.rest_12_ = bf16[784,256]{1,0:T(8,128)(2,1)} collective-permute-done((bf16[784,256]{1,0:T(8,128)(2,1)}, bf16[784,256]{1,0:T(8,128)(2,1)}, u32[]{:S(2)}, u32[]{:S(2)}) %collective-permute-start.3) | collective-permute-done | bytes 401440 | tf_op jit(solution)/shard_map/ppermute | solution.py:838
  102.1 2.0 collective-permute-start.7
  104.1 0.1 collective-permute-start.8
  104.2 0.6 collective-permute-start.9
  104.8 0.0 collective-permute-done.1.rest_3_
  104.8 0.8 collective-permute-done.7.rest_7_
  105.6 0.7 collective-permute-done.8.rest_8_
  106.3 0.7 collective-permute-done.9.rest_9_
  107.0 0.0 copy-done
  107.0 0.0 copy-done.6
  107.0 15.9 %far_attention.1 = (bf16[784,256]{1,0:T(8,128)(2,1)S(1)}, bf16[784,256]{1,0:T(8,128)(2,1)S(1)}, bf16[784,256]{1,0:T(8,128)(2,1)S(1)}, f32[12,128,640]{2,1,0:T(8,128)}, s32[1]{0:T(128)}) custom-call(s32[1]{0:T(128)} %bitcast.48.me_ref, s32[8]{0:T(128)S(1)} %get-tuple-element.381.counts_ref, bf16[8,16,256]{2,1,0:T(8,128)(2,1)S(1)} %all_to_all.191.rest_0_, ...), custom_call_target="tpu_custom_call" | custom-call | flops 10000000000 | bytes 12000000 | tf_op jit(solution)/shard_map/far_attention/pallas_call | solution.py:697
  123.0 0.7 collective-permute-start.10
  123.6 1.3 collective-permute-start.11
  125.0 1.9 collective-permute-start.12
  126.9 0.4 collective-permute-start.13
  127.4 0.8 collective-permute-done.13.rest_12_
  128.2 1.2 copy-done.1
  129.4 1.2 copy-done.3
  130.6 8.1 %own_attention.1 = (bf16[8,192,640]{2,1,0:T(8,128)(2,1)}, f32[768,256]{1,0:T(8,128)S(1)}) custom-call(s32[1]{0:T(128)} %bitcast.48.me_ref, s32[8]{0:T(128)S(1)} %get-tuple-element.381.counts_ref, bf16[8,16,256]{2,1,0:T(8,128)(2,1)S(1)} %all_to_all.191.rest_0_, bf16[192,5120]{1,0:T(8,128)(2,1)S(1)} %copy-done.10, bf16[192,5120]{1,0:T(8,128)(2,1)S(1)} %copy-done.6, ...), custom_call_target="tpu_custom_call" | custom-call | flops 1000000 | bytes 100000 | tf_op jit(solution)/shard_map/own_attention/pallas_call | solution.py:734
  138.7 0.0 collective-permute-done.10.rest_0_
  138.7 12.1 %collective-permute-done.11.rest_1_ = bf16[784,256]{1,0:T(8,128)(2,1)S(1)} collective-permute-done((bf16[784,256]{1,0:T(8,128)(2,1)S(1)}, bf16[784,256]{1,0:T(8,128)(2,1)S(1)}, u32[]{:S(2)}, u32[]{:S(2)}) %collective-permute-start.11) | collective-permute-done | bytes 401440 | tf_op jit(solution)/shard_map/ppermute | solution.py:846
  150.7 8.6 %collective-permute-done.12.rest_2_ = bf16[784,256]{1,0:T(8,128)(2,1)S(1)} collective-permute-done((bf16[784,256]{1,0:T(8,128)(2,1)S(1)}, bf16[784,256]{1,0:T(8,128)(2,1)S(1)}, u32[]{:S(2)}, u32[]{:S(2)}) %collective-permute-start.12) | collective-permute-done | bytes 401440 | tf_op jit(solution)/shard_map/ppermute | solution.py:846
  159.3 1.4 combine.1
  160.8 14.8 %all_to_all.192 = bf16[8,192,256]{2,1,0:T(8,128)(2,1)S(1)} all-to-all(bf16[8,192,256]{2,1,0:T(8,128)(2,1)S(1)} %combine.1), channel_id=1, replica_groups=mesh['outer'=4,'inner'=4,'head'=2] {'inner','head'}, dimensions={0} | all-to-all | bytes 1572864 | tf_op jit(solution)/shard_map/all_to_all | solution.py:853
  175.6 4.4 %all-to-all-start.23 = ((bf16[8,192,640]{2,1,0:T(8,128)(2,1)}), bf16[8,192,640]{2,1,0:T(8,128)(2,1)}, u32[]{:S(2)}, u32[]{:S(2)}) async-start(bf16[8,192,640]{2,1,0:T(8,128)(2,1)} %get-tuple-element.395), calls=%async_computation.23 | async-start | bytes 3932160 | tf_op jit(solution)/shard_map/all_to_all | solution.py:851
  180.6 0.5 slice.53
  181.8 0.5 slice.54
  182.9 0.5 slice.55
  184.1 1.1 slice_bitcast_fusion
  185.2 0.0 copy-start.17
  185.2 0.0 copy-start.20
  185.2 18.7 %all-to-all-done.23.parts = bf16[8,192,640]{2,1,0:T(8,128)(2,1)} async-done(((bf16[8,192,640]{2,1,0:T(8,128)(2,1)}), bf16[8,192,640]{2,1,0:T(8,128)(2,1)}, u32[]{:S(2)}, u32[]{:S(2)}) %all-to-all-start.23) | async-done | bytes 1966112 | tf_op jit(solution)/shard_map/all_to_all | solution.py:851
  203.9 3.0 %unpack_rows.1 = bf16[192,5120]{1,0:T(8,128)(2,1)} custom-call(bf16[8,192,640]{2,1,0:T(8,128)(2,1)} %all-to-all-done.23.parts), custom_call_target="tpu_custom_call" | custom-call | tf_op jit(solution)/shard_map/unpack_rows/pallas_call | solution.py:767
  206.9 0.0 copy-done.14
  207.0 1.0 conditional.1
  207.0 1.0 copy_bitcast_fusion
  (19 shorter events, 0.1 us)
Async XLA Ops:
  7.2 23.7 %copy-start.5 = (bf16[192,5120]{1,0:T(8,128)(2,1)S(1)}, bf16[192,5120]{1,0:T(8,128)(2,1)}, u32[]{:S(2)}) copy-start(bf16[192,5120]{1,0:T(8,128)(2,1)} %rest_2_.3) | copy-start | bytes 5898244
  27.6 51.8 %collective-permute-start = (bf16[784,256]{1,0:T(8,128)(2,1)S(1)}, bf16[784,256]{1,0:T(8,128)(2,1)}, u32[]{:S(2)}, u32[]{:S(2)}) collective-permute-start(bf16[784,256]{1,0:T(8,128)(2,1)S(1)} %get-tuple-element.382.rest_10_), channel_id=1, source_target_pairs={{0,8},{8,16},{16,24},{1,9},{9,17},{17,25},{2,10},{10,18},{18,26},{... | collective-permute-start | bytes 1204232 | tf_op jit(solution)/shard_map/ppermute | solution.py:835
  32.9 65.3 %collective-permute-start.4 = (bf16[2,192,1280]{2,1,0:T(8,128)(2,1)}, bf16[2,192,1280]{2,1,0:T(8,128)(2,1)S(1)}, u32[]{:S(2)}, u32[]{:S(2)}) collective-permute-start(bf16[2,192,1280]{2,1,0:T(8,128)(2,1)} %pack_rows.5), channel_id=1, source_target_pairs={{0,5},{1,4},{2,7},{3,6},{4,1},{5,0},{6,3},{7,2},{8,13},{9,12},{10,... | collective-permute-start | bytes 2949128 | tf_op jit(solution)/shard_map/ppermute | solution.py:822
  35.4 4.8 %copy-start.19 = (bf16[192,40]{0,1:T(8,128)(2,1)S(1)}, bf16[192,40]{0,1:T(8,128)(2,1)}, u32[]{:S(2)}) copy-start(bf16[192,40]{0,1:T(8,128)(2,1)} %param.20) | copy-start | bytes 46084
  35.4 62.8 %collective-permute-start.5 = (bf16[2,192,1280]{2,1,0:T(8,128)(2,1)}, bf16[2,192,1280]{2,1,0:T(8,128)(2,1)S(1)}, u32[]{:S(2)}, u32[]{:S(2)}) collective-permute-start(bf16[2,192,1280]{2,1,0:T(8,128)(2,1)} %pack_rows.6), channel_id=1, source_target_pairs={{0,4},{1,5},{2,6},{3,7},{4,0},{5,1},{6,2},{7,3},{8,12},{9,13},{10,... | collective-permute-start | bytes 2949128 | tf_op jit(solution)/shard_map/ppermute | solution.py:822
  39.0 59.2 %collective-permute-start.6 = (bf16[2,192,1280]{2,1,0:T(8,128)(2,1)}, bf16[2,192,1280]{2,1,0:T(8,128)(2,1)S(1)}, u32[]{:S(2)}, u32[]{:S(2)}) collective-permute-start(bf16[2,192,1280]{2,1,0:T(8,128)(2,1)} %pack_rows.7), channel_id=1, source_target_pairs={{0,1},{1,0},{2,3},{3,2},{4,5},{5,4},{6,7},{7,6},{8,9},{9,8},{10,11... | collective-permute-start | bytes 2949128 | tf_op jit(solution)/shard_map/ppermute | solution.py:822
  79.4 12.6 %collective-permute-start.2 = (bf16[784,256]{1,0:T(8,128)(2,1)}, bf16[784,256]{1,0:T(8,128)(2,1)}, u32[]{:S(2)}, u32[]{:S(2)}) collective-permute-start(bf16[784,256]{1,0:T(8,128)(2,1)} %collective-permute-done.rest_10_), channel_id=1, source_target_pairs={{8,16},{16,24},{9,17},{17,25},{10,18},{18,26},{11,19},{19,27},{12,... | collective-permute-start | bytes 1204232 | tf_op jit(solution)/shard_map/ppermute | solution.py:837
  92.0 10.1 %collective-permute-start.3 = (bf16[784,256]{1,0:T(8,128)(2,1)}, bf16[784,256]{1,0:T(8,128)(2,1)}, u32[]{:S(2)}, u32[]{:S(2)}) collective-permute-start(bf16[784,256]{1,0:T(8,128)(2,1)} %collective-permute-done.2.rest_11_), channel_id=1, source_target_pairs={{16,24},{17,25},{18,26},{19,27},{20,28},{21,29},{22,30},{23,31}} | collective-permute-start | bytes 1204232 | tf_op jit(solution)/shard_map/ppermute | solution.py:838
  96.8 10.2 %copy-start.6 = (bf16[192,5120]{1,0:T(8,128)(2,1)S(1)}, bf16[192,5120]{1,0:T(8,128)(2,1)}, u32[]{:S(2)}) copy-start(bf16[192,5120]{1,0:T(8,128)(2,1)} %rest_2_.3) | copy-start | bytes 5898244
  96.8 8.0 %collective-permute-start.1 = (bf16[1,192,1280]{2,1,0:T(8,128)(2,1)}, bf16[1,192,1280]{2,1,0:T(8,128)(2,1)S(1)}, u32[]{:S(2)}, u32[]{:S(2)}) collective-permute-start(bf16[1,192,1280]{2,1,0:T(8,128)(2,1)} %pack_rows.4), channel_id=1, source_target_pairs={{0,2},{1,3},{2,0},{3,1},{4,6},{5,7},{6,4},{7,5},{8,10},{9,11},{10,... | collective-permute-start | bytes 1474568 | tf_op jit(solution)/shard_map/ppermute | solution.py:822
  98.2 8.8 %copy-start = (bf16[2,192,1280]{2,1,0:T(8,128)(2,1)}, bf16[2,192,1280]{2,1,0:T(8,128)(2,1)S(1)}, u32[]{:S(2)}) copy-start(bf16[2,192,1280]{2,1,0:T(8,128)(2,1)S(1)} %collective-permute-done.5.rest_5_) | copy-start | bytes 2949124
  98.2 8.8 %copy-start.2 = (bf16[2,192,1280]{2,1,0:T(8,128)(2,1)}, bf16[2,192,1280]{2,1,0:T(8,128)(2,1)S(1)}, u32[]{:S(2)}) copy-start(bf16[2,192,1280]{2,1,0:T(8,128)(2,1)S(1)} %collective-permute-done.6.rest_6_) | copy-start | bytes 2949124
  102.1 3.5 %collective-permute-start.7 = (bf16[1,192,1280]{2,1,0:T(8,128)(2,1)S(1)}, bf16[1,192,1280]{2,1,0:T(8,128)(2,1)S(1)}, u32[]{:S(2)}, u32[]{:S(2)}) collective-permute-start(bf16[1,192,1280]{2,1,0:T(8,128)(2,1)S(1)} %slice.36), channel_id=1, source_target_pairs={{0,2},{1,3},{2,0},{3,1},{4,6},{5,7},{6,4},{7,5},{8,10},{9,11},{10,... | collective-permute-start | bytes 1474568 | tf_op jit(solution)/shard_map/ppermute | solution.py:822
  104.1 2.2 %collective-permute-start.8 = (bf16[1,192,1280]{2,1,0:T(8,128)(2,1)S(1)}, bf16[1,192,1280]{2,1,0:T(8,128)(2,1)S(1)}, u32[]{:S(2)}, u32[]{:S(2)}) collective-permute-start(bf16[1,192,1280]{2,1,0:T(8,128)(2,1)S(1)} %slice.37), channel_id=1, source_target_pairs={{0,2},{1,3},{2,0},{3,1},{4,6},{5,7},{6,4},{7,5},{8,10},{9,11},{10,... | collective-permute-start | bytes 1474568 | tf_op jit(solution)/shard_map/ppermute | solution.py:822
  104.2 2.7 %collective-permute-start.9 = (bf16[1,192,1280]{2,1,0:T(8,128)(2,1)S(1)}, bf16[1,192,1280]{2,1,0:T(8,128)(2,1)S(1)}, u32[]{:S(2)}, u32[]{:S(2)}) collective-permute-start(bf16[1,192,1280]{2,1,0:T(8,128)(2,1)S(1)} %slice.38), channel_id=1, source_target_pairs={{0,2},{1,3},{2,0},{3,1},{4,6},{5,7},{6,4},{7,5},{8,10},{9,11},{10,... | collective-permute-start | bytes 1474568 | tf_op jit(solution)/shard_map/ppermute | solution.py:822
  107.0 21.2 %copy-start.10 = (bf16[192,5120]{1,0:T(8,128)(2,1)S(1)}, bf16[192,5120]{1,0:T(8,128)(2,1)}, u32[]{:S(2)}) copy-start(bf16[192,5120]{1,0:T(8,128)(2,1)} %rest_1_.3) | copy-start | bytes 5898244
  123.0 15.7 %collective-permute-start.10 = (bf16[784,256]{1,0:T(8,128)(2,1)S(1)}, bf16[784,256]{1,0:T(8,128)(2,1)S(1)}, u32[]{:S(2)}, u32[]{:S(2)}) collective-permute-start(bf16[784,256]{1,0:T(8,128)(2,1)S(1)} %get-tuple-element.390), channel_id=1, source_target_pairs={{24,0},{25,1},{26,2},{27,3},{28,4},{29,5},{30,6},{31,7}} | collective-permute-start | bytes 1204232 | tf_op jit(solution)/shard_map/ppermute | solution.py:846
  123.6 27.1 %collective-permute-start.11 = (bf16[784,256]{1,0:T(8,128)(2,1)S(1)}, bf16[784,256]{1,0:T(8,128)(2,1)S(1)}, u32[]{:S(2)}, u32[]{:S(2)}) collective-permute-start(bf16[784,256]{1,0:T(8,128)(2,1)S(1)} %get-tuple-element.391), channel_id=1, source_target_pairs={{16,0},{24,8},{17,1},{25,9},{18,2},{26,10},{19,3},{27,11},{20,4},{... | collective-permute-start | bytes 1204232 | tf_op jit(solution)/shard_map/ppermute | solution.py:846
  125.0 34.4 %collective-permute-start.12 = (bf16[784,256]{1,0:T(8,128)(2,1)S(1)}, bf16[784,256]{1,0:T(8,128)(2,1)S(1)}, u32[]{:S(2)}, u32[]{:S(2)}) collective-permute-start(bf16[784,256]{1,0:T(8,128)(2,1)S(1)} %get-tuple-element.392), channel_id=1, source_target_pairs={{8,0},{16,8},{24,16},{9,1},{17,9},{25,17},{10,2},{18,10},{26,18},{... | collective-permute-start | bytes 1204232 | tf_op jit(solution)/shard_map/ppermute | solution.py:846
  126.9 1.3 collective-permute-start.13
  128.2 1.2 copy-start.1
  129.4 1.2 copy-start.3
  175.6 28.4 %all-to-all-start.23 = ((bf16[8,192,640]{2,1,0:T(8,128)(2,1)}), bf16[8,192,640]{2,1,0:T(8,128)(2,1)}, u32[]{:S(2)}, u32[]{:S(2)}) async-start(bf16[8,192,640]{2,1,0:T(8,128)(2,1)} %get-tuple-element.395), calls=%async_computation.23 | async-start | bytes 3932160 | tf_op jit(solution)/shard_map/all_to_all | solution.py:851
  185.2 21.7 %copy-start.7 = (bf16[192,5120]{1,0:T(8,128)(2,1)S(1)}, bf16[192,5120]{1,0:T(8,128)(2,1)}, u32[]{:S(2)}) copy-start(bf16[192,5120]{1,0:T(8,128)(2,1)} %rest_2_.3) | copy-start | bytes 5898244
  185.2 21.7 %copy-start.14 = (bf16[192,1024]{1,0:T(8,128)(2,1)S(1)}, bf16[192,1024]{1,0:T(8,128)(2,1)}, u32[]{:S(2)}) copy-start(bf16[192,1024]{1,0:T(8,128)(2,1)} %k_ref.1) | copy-start | bytes 1179652
  185.2 21.7 %copy-start.15 = (bf16[192,1024]{1,0:T(8,128)(2,1)S(1)}, bf16[192,1024]{1,0:T(8,128)(2,1)}, u32[]{:S(2)}) copy-start(bf16[192,1024]{1,0:T(8,128)(2,1)} %v_ref.1) | copy-start | bytes 1179652
  185.2 21.7 %copy-start.16 = (bf16[192,8,128]{2,0,1:T(8,128)(2,1)S(1)}, bf16[192,8,128]{2,0,1:T(8,128)(2,1)}, u32[]{:S(2)}) copy-start(bf16[192,8,128]{2,0,1:T(8,128)(2,1)} %get-tuple-element.605) | copy-start | bytes 1179652
  185.2 21.7 %copy-start.17 = (bf16[192,8,128]{2,0,1:T(8,128)(2,1)S(1)}, bf16[192,8,128]{2,0,1:T(8,128)(2,1)}, u32[]{:S(2)}) copy-start(bf16[192,8,128]{2,0,1:T(8,128)(2,1)} %get-tuple-element.606) | copy-start | bytes 1179652
  185.2 21.7 %copy-start.20 = (s32[192]{0:T(256)S(1)}, s32[192]{0:T(256)}, u32[]{:S(2)}) copy-start(s32[192]{0:T(256)} %param.21) | copy-start | bytes 2308

commit v2 on v1

--- a/solution.py
+++ b/solution.py
@@ -213,6 +213,8 @@
 ROW_TILE = 128
 INFO_ROWS = 16
 AUX_LANES = 256
+COUNT_ROW = 5
+DELTA_ROW = 8
 SMEM = pl.BlockSpec(memory_space=pltpu.SMEM)
 VMEM = pl.BlockSpec(memory_space=pltpu.VMEM)
 HBM = pl.BlockSpec(memory_space=pltpu.HBM)
@@ -224,30 +226,47 @@
 PASS_ROWS = (256, 512, 768)
 
 
-def pack_pairs_kernel(limit, ranks_ref, k_ref, v_ref, out_ref):
+def pack_pairs_kernel(limit, ranks_ref, lse_ref, k_ref, v_ref, do_ref, o_ref, out_ref, columns, lanes):
     home_rows = k_ref.shape[0]
+    columns[...] = jnp.zeros_like(columns)
+    for g in range(KEY_VALUE_HEADS):
+        columns[:, 16 * g : 16 * g + GROUP] = lse_ref[:, g * GROUP : (g + 1) * GROUP].astype(
+            jnp.float32
+        )
+    for h in range(QUERY_HEADS):
+        head = slice(h * HEAD_SIZE, (h + 1) * HEAD_SIZE)
+        product = do_ref[:, head].astype(jnp.float32) * o_ref[:, head].astype(jnp.float32)
+        column = 16 * (h // GROUP) + DELTA_ROW + h % GROUP
+        columns[:, column : column + 1] = jnp.sum(product, axis=1, keepdims=True)
+    lanes[...] = jnp.zeros_like(lanes)
+    lanes[:, :home_rows] = columns[...].T
     live = jnp.where(ranks_ref[...] < limit, 1.0, 0.0)
-    info = jnp.broadcast_to(
-        jnp.sum(live, axis=1, keepdims=True), (INFO_ROWS, 2 * HEAD_SIZE)
-    ).astype(out_ref.dtype)
+    count = jnp.sum(live, axis=1, keepdims=True)
+    line = lax.broadcasted_iota(jnp.int32, (INFO_ROWS, 2 * HEAD_SIZE), 0)
     for g in range(KEY_VALUE_HEADS):
-        columns = slice(g * HEAD_SIZE, (g + 1) * HEAD_SIZE)
-        out_ref[g, :home_rows, :HEAD_SIZE] = k_ref[:, columns]
-        out_ref[g, :home_rows, HEAD_SIZE:] = v_ref[:, columns]
-        out_ref[g, home_rows:, :] = info
-
-
-def pack_pairs(limit, ranks, keys, values):
+        head = slice(g * HEAD_SIZE, (g + 1) * HEAD_SIZE)
+        out_ref[g, :home_rows, :HEAD_SIZE] = k_ref[:, head]
+        out_ref[g, :home_rows, HEAD_SIZE:] = v_ref[:, head]
+        info = jnp.where(line == COUNT_ROW, count, lanes[16 * g : 16 * g + INFO_ROWS, :])
+        out_ref[g, home_rows:, :] = info.astype(out_ref.dtype)
+
+
+def pack_pairs(limit, ranks, lse, keys, values, output_gradient, outputs):
     home_rows = keys.shape[0]
     return pl.pallas_call(
         functools.partial(pack_pairs_kernel, limit),
         out_shape=jax.ShapeDtypeStruct(
             (KEY_VALUE_HEADS, home_rows + INFO_ROWS, 2 * HEAD_SIZE), keys.dtype
         ),
-        in_specs=[VMEM] * 3,
+        in_specs=[VMEM] * 6,
         out_specs=VMEM,
+        scratch_shapes=[
+            pltpu.VMEM((home_rows, HEAD_SIZE), jnp.float32),
+            pltpu.VMEM((HEAD_SIZE, AUX_LANES), jnp.float32),
+        ],
+        compiler_params=pltpu.CompilerParams(vmem_limit_bytes=32 * 1024 * 1024),
         name="pack_pairs",
-    )(ranks.reshape(1, home_rows), keys, values)
+    )(ranks.reshape(1, home_rows), lse, keys, values, output_gradient, outputs)
 
 
 def pack_rows_kernel(partners, me_ref, q_hbm, do_hbm, out, sems):
@@ -280,41 +299,7 @@
     )(me, queries, output_gradient)
 
 
-def pack_small_kernel(lse_ref, do_ref, o_ref, out, columns, lanes):
-    home_rows = do_ref.shape[0]
-    columns[...] = jnp.zeros_like(columns)
-    for g in range(KEY_VALUE_HEADS):
-        columns[:, 16 * g : 16 * g + GROUP] = lse_ref[:, g * GROUP : (g + 1) * GROUP].astype(
-            jnp.float32
-        )
-    for h in range(QUERY_HEADS):
-        head = slice(h * HEAD_SIZE, (h + 1) * HEAD_SIZE)
-        product = do_ref[:, head].astype(jnp.float32) * o_ref[:, head].astype(jnp.float32)
-        column = 16 * (h // GROUP) + 8 + h % GROUP
-        columns[:, column : column + 1] = jnp.sum(product, axis=1, keepdims=True)
-    lanes[...] = jnp.zeros_like(lanes)
-    lanes[:, :home_rows] = columns[...].T
-    for g in range(KEY_VALUE_HEADS):
-        out[g] = lanes[16 * g : 16 * g + INFO_ROWS, :].astype(out.dtype)
-
-
-def pack_small(lse, output_gradient, outputs):
-    f32 = jnp.float32
-    return pl.pallas_call(
-        pack_small_kernel,
-        out_shape=jax.ShapeDtypeStruct((KEY_VALUE_HEADS, INFO_ROWS, AUX_LANES), jnp.bfloat16),
-        in_specs=[VMEM] * 3,
-        out_specs=VMEM,
-        scratch_shapes=[
-            pltpu.VMEM((lse.shape[0], HEAD_SIZE), f32),
-            pltpu.VMEM((HEAD_SIZE, AUX_LANES), f32),
-        ],
-        compiler_params=pltpu.CompilerParams(vmem_limit_bytes=32 * 1024 * 1024),
-        name="pack_small",
-    )(lse, output_gradient, outputs)
-
-
-def compact_kernel(arrived, out, counts_ref):
+def compact_kernel(arrived, out, small, counts_ref):
     home_rows = arrived.shape[1] - INFO_ROWS
     capacity = out.shape[0] - INFO_ROWS
     row = lax.broadcasted_iota(jnp.int32, (capacity, home_rows), 0)
@@ -322,7 +307,9 @@
     total = jnp.int32(0)
     picked = []
     for block in range(KEY_VALUE_HEADS):
-        count = jnp.max(arrived[block, home_rows:, :].astype(jnp.float32)).astype(jnp.int32)
+        info = arrived[block, home_rows:, :]
+        small[block] = info
+        count = jnp.max(info[COUNT_ROW : COUNT_ROW + 1].astype(jnp.float32)).astype(jnp.int32)
         counts_ref[block] = count
         hit = (row == within + total) & (within < count)
         picked.append(jnp.where(hit, 1.0, 0.0).astype(jnp.bfloat16))
@@ -348,10 +335,11 @@
         compact_kernel,
         out_shape=(
             jax.ShapeDtypeStruct((capacity + INFO_ROWS, columns), arrived.dtype),
+            jax.ShapeDtypeStruct((blocks, INFO_ROWS, columns), arrived.dtype),
             jax.ShapeDtypeStruct((blocks,), jnp.int32),
         ),
         in_specs=[VMEM],
-        out_specs=(VMEM, SMEM),
+        out_specs=(VMEM, VMEM, SMEM),
         compiler_params=pltpu.CompilerParams(vmem_limit_bytes=32 * 1024 * 1024),
         name="compact",
     )(arrived)
@@ -429,7 +417,7 @@
             for h in range(GROUP):
                 columns = slice(h * ROW_TILE, (h + 1) * ROW_TILE)
                 lse_s[row : row + 1, columns] = rows[h : h + 1] * LOG2E
-                delta_s[row : row + 1, columns] = rows[8 + h : 9 + h]
+                delta_s[row : row + 1, columns] = rows[DELTA_ROW + h : DELTA_ROW + 1 + h]
 
 
 def row_tile(tile, q_s, do_s, lse_s, delta_s):
@@ -821,22 +809,22 @@
     def swap(array, k):
         return lax.ppermute(array, plane, [(i, i ^ k) for i in range(blocks)])
 
-    sent = pack_pairs(surviving_tokens, ranks, keys, values)
+    sent = pack_pairs(
+        surviving_tokens, ranks, lse, keys, values, output_gradient, outputs
+    )
+    me, sent = lax.optimization_barrier((me, sent))
     arrived = lax.all_to_all(sent, plane, split_axis=0, concat_axis=0, tiled=True)
-    packed = [
-        pack_rows((chip, chip ^ CORE), me, queries, output_gradient) for chip in CHIPS
+    pairs = [
+        swap(pack_rows((chip, chip ^ CORE), me, queries, output_gradient), chip) for chip in CHIPS
     ]
-    pairs = [swap(rows, chip) for rows, chip in zip(packed, CHIPS)]
     beside = swap(pack_rows((CORE,), me, queries, output_gradient), CORE)
-    small = lax.all_to_all(
-        pack_small(lse, output_gradient, outputs), plane, split_axis=0, concat_axis=0, tiled=True
-    )
-    mine, counts = compact(arrived)
+    arrived, beside = lax.optimization_barrier((arrived, beside))
+    mine, small, counts = compact(arrived)
     up = [lax.ppermute(mine, "outer", [(i, i + 1) for i in range(planes - 1)])]
-    up[0], small = lax.optimization_barrier((up[0], small))
+    last = lax.ppermute(mine, "outer", [(0, planes - 1)])
     up.append(lax.ppermute(up[0], "outer", [(i, i + 1) for i in range(1, planes - 1)]))
-    up.append(lax.ppermute(up[1], "outer", [(i, i + 1) for i in range(2, planes - 1)]))
-    up[2], *pairs = lax.optimization_barrier((up[2], *pairs))
+    up.append(last)
+    up[1], up[2], *pairs = lax.optimization_barrier((up[1], up[2], *pairs))
     crossed = [swap(pair[1:], CORE) for pair in pairs]
     arrays = [queries, output_gradient, beside, *pairs, *crossed]
 
@@ -847,9 +835,9 @@
         for k in (3, 2, 1)
     ]
     dq, own = own_attention(me, counts, small, arrays, mine, dqt, note)
-    dq_home = unpack_rows(
-        lax.all_to_all(dq, plane, split_axis=0, concat_axis=0, tiled=True)
-    )
+    dq = lax.all_to_all(dq, plane, split_axis=0, concat_axis=0, tiled=True)
+    dq, own = lax.optimization_barrier((dq, own))
+    dq_home = unpack_rows(dq)
     kv_home = lax.all_to_all(
         combine(counts, own, backs, home_rows), plane, split_axis=0, concat_axis=0, tiled=True
     )

time: 219 us -> 174 us (0.79)
  blocking collectives: 67.5 us -> 0 us
  waiting for transfers between devices: 56.9 us -> 72.9 us
  starting transfers between devices: 23.7 us -> 30.7 us
    all_to_all x3 -> x0, blocking collectives: 67.5 us -> none  [the longest x1 35.7 us: plane_device(): lax.all_to_all(pack_small(lse, output_gradient, outputs), plane, split_ax...]
    ppermute x8, waiting for transfers between devices: 3.01 us -> 29.2 us  [swap(): return lax.ppermute(array, plane, [(i, i ^ k) for i in range(blocks)])]
    ppermute x1, waiting for transfers between devices: 10.6 us -> 0.01 us  [plane_device(): lax.ppermute(up[0], 'outer', [(i, i + 1) for i in range(1, planes - 1)])]
    all_to_all x1 -> x3, starting transfers between devices: 4.35 us -> 13.7 us  [the longest x1 4.7 us: plane_device(): dq = lax.all_to_all(dq, plane, split_axis=0, concat_axis=0, tiled=True)]
    ppermute x3, waiting for transfers between devices: 20.7 us -> 12.6 us  [plane_device(): lax.ppermute(down[k - 1], 'outer', [(i + k, i) for i in range(planes - k)])]
    ppermute x1, waiting for transfers between devices: 0.01 us -> 7.93 us  [plane_device(): up = [lax.ppermute(mine, 'outer', [(i, i + 1) for i in range(planes - 1)])]]
    all_to_all x1 -> x3, waiting for transfers between devices: 18.7 us -> 23.2 us  [the longest x1 19 us: plane_device(): dq = lax.all_to_all(dq, plane, split_axis=0, concat_axis=0, tiled=True)]
    ppermute x1, waiting for transfers between devices: 3.83 us -> 0.01 us  [plane_device(): last = lax.ppermute(mine, 'outer', [(0, planes - 1)])]
  transfers between devices with their start and end apart: 15 -> 17, of which waited for: 9 -> 12; matrix products, arithmetic and copies ran while one was open for 1% -> 2% of each run, Pallas kernels for 9% -> 7%
where the time goes in v2:
time: 174 us; the launch traced here: 171 us
  waiting for transfers between devices  72.9 us (42%)
  Pallas kernels  43 us (25%)
  starting transfers between devices  30.7 us (18%)
  between operations  16.9 us (10%)
  local copies, waits for them, and re-layouts  7.45 us (4%)
    ppermute x8, waiting for transfers between devices, swap(): return lax.ppermute(array, plane, [(i, i ^ k) for i in range(blocks)])  29.2 us
    all_to_all x1, waiting for transfers between devices, plane_device(): dq = lax.all_to_all(dq, plane, split_axis=0, concat_axis=0, tiled=True)  19 us
    pallas_call x1, Pallas kernels, far_attention(): pl.pallas_call(far_kernel, out_shape=(jax.ShapeDtypeStruct((rows, columns...  15.3 us
    ppermute x3, waiting for transfers between devices, plane_device(): lax.ppermute(down[k - 1], 'outer', [(i + k, i) for i in range(planes - k)])  12.6 us
    pallas_call x4, Pallas kernels, pack_rows(): pl.pallas_call(functools.partial(pack_rows_kernel, partners), out_shape=j...  8.4 us
    ppermute x1, waiting for transfers between devices, plane_device(): up = [lax.ppermute(mine, 'outer', [(i, i + 1) for i in range(planes - 1)])]  7.93 us
    pallas_call x1, Pallas kernels, own_attention(): pl.pallas_call(own_kernel, out_shape=(jax.ShapeDtypeStruct((blocks, plane...  7.91 us
    ppermute x3, starting transfers between devices, plane_device(): lax.ppermute(down[k - 1], 'outer', [(i + k, i) for i in range(planes - k)])  5 us
  transfers between devices with their start and end apart: 17, of which 12 were waited for; matrix products, arithmetic and copies ran while one was open for 2% of the time, Pallas kernels for 7%

profile of v2, /device:TPU:17, one launch (start us, length us, event | category | flops | bytes accessed | tf_op | source)
XLA Modules:
  0.0 170.9 jit_solution(14528576672003144051)
XLA Ops:
  7.2 0.8 copy.217.lse_ref
  8.0 0.0 copy-start.9
  8.0 4.8 %pack_pairs.1 = bf16[8,208,256]{2,1,0:T(8,128)(2,1)} custom-call(s32[1,192]{1,0:T(1,128)} %bitcast.283, bf16[192,40]{1,0:T(8,128)(2,1)S(1)} %copy.217.lse_ref, bf16[192,1024]{1,0:T(8,128)(2,1)} %k_ref.1, bf16[192,1024]{1,0:T(8,128)(2,1)} %v_ref.1, bf16[192,5120]{1,0:T(8,128)(2,1)} %rest_2_.3, bf16[192,5120]{1,0:T(8,128)(2,1)} %o_ref.1), custom_call_target="tpu_custom_call" | custom-call | tf_op jit(solution)/shard_map/pack_pairs/pallas_call | solution.py:256
  12.8 4.4 %all-to-all-start.20 = ((bf16[8,208,256]{2,1,0:T(8,128)(2,1)}), bf16[8,208,256]{2,1,0:T(8,128)(2,1)S(1)}, u32[]{:S(2)}, u32[]{:S(2)}) async-start(bf16[8,208,256]{2,1,0:T(8,128)(2,1)} %pack_pairs.1), calls=%async_computation.20 | async-start | bytes 1703936 | tf_op jit(solution)/shard_map/all_to_all | solution.py:816
  17.2 0.0 copy-done.9
  17.2 1.8 %pack_rows.4 = bf16[1,192,1280]{2,1,0:T(8,128)(2,1)} custom-call(s32[1]{0:T(128)} %bitcast.48.me_ref, bf16[192,5120]{1,0:T(8,128)(2,1)} %rest_1_.3, bf16[192,5120]{1,0:T(8,128)(2,1)S(1)} %copy-done.9), custom_call_target="tpu_custom_call" | custom-call | tf_op jit(solution)/shard_map/pack_rows/pallas_call | solution.py:292
  19.0 0.1 collective-permute-start
  19.0 2.1 %pack_rows.5 = bf16[2,192,1280]{2,1,0:T(8,128)(2,1)} custom-call(s32[1]{0:T(128)} %bitcast.48.me_ref, bf16[192,5120]{1,0:T(8,128)(2,1)} %rest_1_.3, bf16[192,5120]{1,0:T(8,128)(2,1)S(1)} %copy-done.9), custom_call_target="tpu_custom_call" | custom-call | tf_op jit(solution)/shard_map/pack_rows/pallas_call | solution.py:292
  21.1 2.7 %collective-permute-start.4 = (bf16[2,192,1280]{2,1,0:T(8,128)(2,1)}, bf16[2,192,1280]{2,1,0:T(8,128)(2,1)S(1)}, u32[]{:S(2)}, u32[]{:S(2)}) collective-permute-start(bf16[2,192,1280]{2,1,0:T(8,128)(2,1)} %pack_rows.5), channel_id=1, source_target_pairs={{0,5},{1,4},{2,7},{3,6},{4,1},{5,0},{6,3},{7,2},{8,13},{9,12},{10,... | collective-permute-start | bytes 2949128 | tf_op jit(solution)/shard_map/ppermute | solution.py:810
  23.8 2.3 %pack_rows.6 = bf16[2,192,1280]{2,1,0:T(8,128)(2,1)} custom-call(s32[1]{0:T(128)} %bitcast.48.me_ref, bf16[192,5120]{1,0:T(8,128)(2,1)} %rest_1_.3, bf16[192,5120]{1,0:T(8,128)(2,1)} %rest_2_.3), custom_call_target="tpu_custom_call" | custom-call | tf_op jit(solution)/shard_map/pack_rows/pallas_call | solution.py:292
  26.1 0.3 collective-permute-start.5
  26.5 2.3 %pack_rows.7 = bf16[2,192,1280]{2,1,0:T(8,128)(2,1)} custom-call(s32[1]{0:T(128)} %bitcast.48.me_ref, bf16[192,5120]{1,0:T(8,128)(2,1)} %rest_1_.3, bf16[192,5120]{1,0:T(8,128)(2,1)} %rest_2_.3), custom_call_target="tpu_custom_call" | custom-call | tf_op jit(solution)/shard_map/pack_rows/pallas_call | solution.py:292
  28.7 0.1 collective-permute-start.6
  28.8 0.0 collective-permute-done.rest_3_
  28.8 0.3 all-to-all-done.20.arrived
  29.2 1.1 compact.1
  30.3 3.2 %collective-permute-start.1 = (bf16[784,256]{1,0:T(8,128)(2,1)S(1)}, bf16[784,256]{1,0:T(8,128)(2,1)S(1)}, u32[]{:S(2)}, u32[]{:S(2)}) collective-permute-start(bf16[784,256]{1,0:T(8,128)(2,1)S(1)} %get-tuple-element.393.rest_10_), channel_id=1, source_target_pairs={{0,8},{8,16},{16,24},{1,9},{9,17},{17,25},{2,10},{10,18},{18,26},{... | collective-permute-start | bytes 1204232 | tf_op jit(solution)/shard_map/ppermute | solution.py:823
  33.5 0.7 collective-permute-start.3
  34.2 7.9 %collective-permute-done.1.rest_10_ = bf16[784,256]{1,0:T(8,128)(2,1)S(1)} collective-permute-done((bf16[784,256]{1,0:T(8,128)(2,1)S(1)}, bf16[784,256]{1,0:T(8,128)(2,1)S(1)}, u32[]{:S(2)}, u32[]{:S(2)}) %collective-permute-start.1) | collective-permute-done | bytes 401440 | tf_op jit(solution)/shard_map/ppermute | solution.py:823
  42.1 3.3 %collective-permute-start.2 = (bf16[784,256]{1,0:T(8,128)(2,1)S(1)}, bf16[784,256]{1,0:T(8,128)(2,1)S(1)}, u32[]{:S(2)}, u32[]{:S(2)}) collective-permute-start(bf16[784,256]{1,0:T(8,128)(2,1)S(1)} %collective-permute-done.1.rest_10_), channel_id=1, source_target_pairs={{8,16},{16,24},{9,17},{17,25},{10,18},{18,26},{11,19},{19,27},{12,... | collective-permute-start | bytes 1204232 | tf_op jit(solution)/shard_map/ppermute | solution.py:825
  45.5 5.3 %collective-permute-done.4.rest_4_ = bf16[2,192,1280]{2,1,0:T(8,128)(2,1)S(1)} collective-permute-done((bf16[2,192,1280]{2,1,0:T(8,128)(2,1)}, bf16[2,192,1280]{2,1,0:T(8,128)(2,1)S(1)}, u32[]{:S(2)}, u32[]{:S(2)}) %collective-permute-start.4) | collective-permute-done | bytes 983072 | tf_op jit(solution)/shard_map/ppermute | solution.py:810
  50.8 20.3 %collective-permute-done.5.rest_5_ = bf16[2,192,1280]{2,1,0:T(8,128)(2,1)S(1)} collective-permute-done((bf16[2,192,1280]{2,1,0:T(8,128)(2,1)}, bf16[2,192,1280]{2,1,0:T(8,128)(2,1)S(1)}, u32[]{:S(2)}, u32[]{:S(2)}) %collective-permute-start.5) | collective-permute-done | bytes 983072 | tf_op jit(solution)/shard_map/ppermute | solution.py:810
  71.1 1.2 collective-permute-done.6.rest_6_
  72.3 0.0 collective-permute-done.3.rest_12_
  72.3 0.0 collective-permute-done.2.rest_11_
  72.3 0.6 collective-permute-start.7
  72.9 0.1 collective-permute-start.8
  73.0 1.1 slice.38
  74.1 0.6 collective-permute-start.9
  74.6 0.0 collective-permute-done.7.rest_7_
  74.6 0.4 collective-permute-done.8.rest_8_
  75.1 1.0 collective-permute-done.9.rest_9_
  76.1 0.0 copy-done
  76.1 0.0 copy-done.10
  76.1 15.3 %far_attention.1 = (bf16[784,256]{1,0:T(8,128)(2,1)S(1)}, bf16[784,256]{1,0:T(8,128)(2,1)S(1)}, bf16[784,256]{1,0:T(8,128)(2,1)S(1)}, f32[12,128,640]{2,1,0:T(8,128)}, s32[1]{0:T(128)}) custom-call(s32[1]{0:T(128)} %bitcast.48.me_ref, s32[8]{0:T(128)S(1)} %get-tuple-element.390.counts_ref, bf16[8,16,256]{2,1,0:T(8,128)(2,1)S(1)} %get-tuple-element.391.rest_0_, ...), custom_call_target="tpu_custom_call" | custom-call | flops 10000000000 | bytes 12000000 | tf_op jit(solution)/shard_map/far_attention/pallas_call | solution.py:685
  91.5 0.8 copy-done.4
  92.3 0.7 copy-done.6
  93.0 0.4 collective-permute-start.13
  93.4 0.8 collective-permute-done.13.rest_12_
  94.2 1.2 copy-done.1
  95.4 7.9 %own_attention.1 = (bf16[8,192,640]{2,1,0:T(8,128)(2,1)}, f32[768,256]{1,0:T(8,128)S(1)}) custom-call(s32[1]{0:T(128)} %bitcast.48.me_ref, s32[8]{0:T(128)S(1)} %get-tuple-element.390.counts_ref, bf16[8,16,256]{2,1,0:T(8,128)(2,1)S(1)} %get-tuple-element.391.rest_0_, bf16[192,5120]{1,0:T(8,128)(2,1)S(1)} %copy-done.14, bf16[192,5120]{1,0:T(8,128)(2,1)S(1)} %copy-done.10, ...), custom_call_target="tpu_custom_call" | custom-call | flops 1000000 | bytes 100000 | tf_op jit(solution)/shard_map/own_attention/pallas_call | solution.py:722
  103.4 4.7 %all-to-all-start.21 = ((bf16[8,192,640]{2,1,0:T(8,128)(2,1)}), bf16[8,192,640]{2,1,0:T(8,128)(2,1)}, u32[]{:S(2)}, u32[]{:S(2)}) async-start(bf16[8,192,640]{2,1,0:T(8,128)(2,1)} %get-tuple-element.404), calls=%async_computation.21 | async-start | bytes 3932160 | tf_op jit(solution)/shard_map/all_to_all | solution.py:838
  108.1 0.7 collective-permute-start.10
  108.7 0.0 copy-done.5
  108.8 1.3 collective-permute-start.11
  110.1 3.0 %collective-permute-start.12 = (bf16[784,256]{1,0:T(8,128)(2,1)S(1)}, bf16[784,256]{1,0:T(8,128)(2,1)S(1)}, u32[]{:S(2)}, u32[]{:S(2)}) collective-permute-start(bf16[784,256]{1,0:T(8,128)(2,1)S(1)} %copy-done.3), channel_id=1, source_target_pairs={{8,0},{16,8},{24,16},{9,1},{17,9},{25,17},{10,2},{18,10},{26,18},{... | collective-permute-start | bytes 1204232 | tf_op jit(solution)/shard_map/ppermute | solution.py:834
  113.1 19.0 %all-to-all-done.21.parts = bf16[8,192,640]{2,1,0:T(8,128)(2,1)} async-done(((bf16[8,192,640]{2,1,0:T(8,128)(2,1)}), bf16[8,192,640]{2,1,0:T(8,128)(2,1)}, u32[]{:S(2)}, u32[]{:S(2)}) %all-to-all-start.21) | async-done | bytes 1966112 | tf_op jit(solution)/shard_map/all_to_all | solution.py:838
  132.1 0.0 collective-permute-done.10.rest_0_
  132.1 4.0 %collective-permute-done.11.rest_1_ = bf16[784,256]{1,0:T(8,128)(2,1)S(1)} collective-permute-done((bf16[784,256]{1,0:T(8,128)(2,1)S(1)}, bf16[784,256]{1,0:T(8,128)(2,1)S(1)}, u32[]{:S(2)}, u32[]{:S(2)}) %collective-permute-start.11) | collective-permute-done | bytes 401440 | tf_op jit(solution)/shard_map/ppermute | solution.py:834
  136.1 8.6 %collective-permute-done.12.rest_2_ = bf16[784,256]{1,0:T(8,128)(2,1)S(1)} collective-permute-done((bf16[784,256]{1,0:T(8,128)(2,1)S(1)}, bf16[784,256]{1,0:T(8,128)(2,1)S(1)}, u32[]{:S(2)}, u32[]{:S(2)}) %collective-permute-start.12) | collective-permute-done | bytes 401440 | tf_op jit(solution)/shard_map/ppermute | solution.py:834
  144.7 2.3 %combine.1 = bf16[8,192,256]{2,1,0:T(8,128)(2,1)} custom-call(s32[8]{0:T(128)S(1)} %get-tuple-element.390.counts_ref, f32[768,256]{1,0:T(8,128)S(1)} %get-tuple-element.406.own, bf16[784,256]{1,0:T(8,128)(2,1)S(1)} %collective-permute-done.10.rest_0_, bf16[784,256]{1,0:T(8,128)(2,1)S(1)} %collective-permute-done.11.rest_1_, ...), custom_call_target="tpu_custom_call" | custom-call | tf_op jit(solution)/shard_map/combine/pallas_call | solution.py:788
  147.0 4.6 %all-to-all-start.22 = ((bf16[8,192,256]{2,1,0:T(8,128)(2,1)}), bf16[8,192,256]{2,1,0:T(8,128)(2,1)S(1)}, u32[]{:S(2)}, u32[]{:S(2)}) async-start(bf16[8,192,256]{2,1,0:T(8,128)(2,1)} %combine.1), calls=%async_computation.22 | async-start | bytes 1572864 | tf_op jit(solution)/shard_map/all_to_all | solution.py:841
  152.2 0.5 slice.53
  153.4 0.5 slice.54
  154.6 0.5 slice.55
  155.7 0.0 copy-start.11
  155.8 0.0 copy-start.18
  155.8 0.0 copy-start.19
  155.8 0.0 copy-start.23
  155.8 3.1 %unpack_rows.1 = bf16[192,5120]{1,0:T(8,128)(2,1)} custom-call(bf16[8,192,640]{2,1,0:T(8,128)(2,1)} %all-to-all-done.21.parts), custom_call_target="tpu_custom_call" | custom-call | tf_op jit(solution)/shard_map/unpack_rows/pallas_call | solution.py:755
  158.9 3.9 %all-to-all-done.22 = bf16[8,192,256]{2,1,0:T(8,128)(2,1)S(1)} async-done(((bf16[8,192,256]{2,1,0:T(8,128)(2,1)}), bf16[8,192,256]{2,1,0:T(8,128)(2,1)S(1)}, u32[]{:S(2)}, u32[]{:S(2)}) %all-to-all-start.22) | async-done | bytes 786464 | tf_op jit(solution)/shard_map/all_to_all | solution.py:841
  162.8 0.2 slice_bitcast_fusion
  163.1 1.0 conditional.1
  163.1 1.0 copy_bitcast_fusion
  (21 shorter events, 0.1 us)
Async XLA Ops:
  8.0 9.2 %copy-start.9 = (bf16[192,5120]{1,0:T(8,128)(2,1)S(1)}, bf16[192,5120]{1,0:T(8,128)(2,1)}, u32[]{:S(2)}) copy-start(bf16[192,5120]{1,0:T(8,128)(2,1)} %rest_2_.3) | copy-start | bytes 5898244
  12.8 16.4 %all-to-all-start.20 = ((bf16[8,208,256]{2,1,0:T(8,128)(2,1)}), bf16[8,208,256]{2,1,0:T(8,128)(2,1)S(1)}, u32[]{:S(2)}, u32[]{:S(2)}) async-start(bf16[8,208,256]{2,1,0:T(8,128)(2,1)} %pack_pairs.1), calls=%async_computation.20 | async-start | bytes 1703936 | tf_op jit(solution)/shard_map/all_to_all | solution.py:816
  19.0 9.9 %collective-permute-start = (bf16[1,192,1280]{2,1,0:T(8,128)(2,1)}, bf16[1,192,1280]{2,1,0:T(8,128)(2,1)S(1)}, u32[]{:S(2)}, u32[]{:S(2)}) collective-permute-start(bf16[1,192,1280]{2,1,0:T(8,128)(2,1)} %pack_rows.4), channel_id=1, source_target_pairs={{0,2},{1,3},{2,0},{3,1},{4,6},{5,7},{6,4},{7,5},{8,10},{9,11},{10,... | collective-permute-start | bytes 1474568 | tf_op jit(solution)/shard_map/ppermute | solution.py:810
  21.1 29.7 %collective-permute-start.4 = (bf16[2,192,1280]{2,1,0:T(8,128)(2,1)}, bf16[2,192,1280]{2,1,0:T(8,128)(2,1)S(1)}, u32[]{:S(2)}, u32[]{:S(2)}) collective-permute-start(bf16[2,192,1280]{2,1,0:T(8,128)(2,1)} %pack_rows.5), channel_id=1, source_target_pairs={{0,5},{1,4},{2,7},{3,6},{4,1},{5,0},{6,3},{7,2},{8,13},{9,12},{10,... | collective-permute-start | bytes 2949128 | tf_op jit(solution)/shard_map/ppermute | solution.py:810
  26.1 44.9 %collective-permute-start.5 = (bf16[2,192,1280]{2,1,0:T(8,128)(2,1)}, bf16[2,192,1280]{2,1,0:T(8,128)(2,1)S(1)}, u32[]{:S(2)}, u32[]{:S(2)}) collective-permute-start(bf16[2,192,1280]{2,1,0:T(8,128)(2,1)} %pack_rows.6), channel_id=1, source_target_pairs={{0,4},{1,5},{2,6},{3,7},{4,0},{5,1},{6,2},{7,3},{8,12},{9,13},{10,... | collective-permute-start | bytes 2949128 | tf_op jit(solution)/shard_map/ppermute | solution.py:810
  28.7 43.5 %collective-permute-start.6 = (bf16[2,192,1280]{2,1,0:T(8,128)(2,1)}, bf16[2,192,1280]{2,1,0:T(8,128)(2,1)}, u32[]{:S(2)}, u32[]{:S(2)}) collective-permute-start(bf16[2,192,1280]{2,1,0:T(8,128)(2,1)} %pack_rows.7), channel_id=1, source_target_pairs={{0,1},{1,0},{2,3},{3,2},{4,5},{5,4},{6,7},{7,6},{8,9},{9,8},{10,11... | collective-permute-start | bytes 2949128 | tf_op jit(solution)/shard_map/ppermute | solution.py:810
  29.2 47.0 %copy-start.10 = (bf16[192,5120]{1,0:T(8,128)(2,1)S(1)}, bf16[192,5120]{1,0:T(8,128)(2,1)}, u32[]{:S(2)}) copy-start(bf16[192,5120]{1,0:T(8,128)(2,1)} %rest_2_.3) | copy-start | bytes 5898244
  30.3 11.8 %collective-permute-start.1 = (bf16[784,256]{1,0:T(8,128)(2,1)S(1)}, bf16[784,256]{1,0:T(8,128)(2,1)S(1)}, u32[]{:S(2)}, u32[]{:S(2)}) collective-permute-start(bf16[784,256]{1,0:T(8,128)(2,1)S(1)} %get-tuple-element.393.rest_10_), channel_id=1, source_target_pairs={{0,8},{8,16},{16,24},{1,9},{9,17},{17,25},{2,10},{10,18},{18,26},{... | collective-permute-start | bytes 1204232 | tf_op jit(solution)/shard_map/ppermute | solution.py:823
  33.5 38.8 %collective-permute-start.3 = (bf16[784,256]{1,0:T(8,128)(2,1)S(1)}, bf16[784,256]{1,0:T(8,128)(2,1)S(1)}, u32[]{:S(2)}, u32[]{:S(2)}) collective-permute-start(bf16[784,256]{1,0:T(8,128)(2,1)S(1)} %get-tuple-element.393.rest_10_), channel_id=1, source_target_pairs={{0,24},{1,25},{2,26},{3,27},{4,28},{5,29},{6,30},{7,31}} | collective-permute-start | bytes 1204232 | tf_op jit(solution)/shard_map/ppermute | solution.py:824
  42.1 30.2 %collective-permute-start.2 = (bf16[784,256]{1,0:T(8,128)(2,1)S(1)}, bf16[784,256]{1,0:T(8,128)(2,1)S(1)}, u32[]{:S(2)}, u32[]{:S(2)}) collective-permute-start(bf16[784,256]{1,0:T(8,128)(2,1)S(1)} %collective-permute-done.1.rest_10_), channel_id=1, source_target_pairs={{8,16},{16,24},{9,17},{17,25},{10,18},{18,26},{11,19},{19,27},{12,... | collective-permute-start | bytes 1204232 | tf_op jit(solution)/shard_map/ppermute | solution.py:825
  71.1 5.1 %copy-start = (bf16[2,192,1280]{2,1,0:T(8,128)(2,1)}, bf16[2,192,1280]{2,1,0:T(8,128)(2,1)S(1)}, u32[]{:S(2)}) copy-start(bf16[2,192,1280]{2,1,0:T(8,128)(2,1)S(1)} %collective-permute-done.5.rest_5_) | copy-start | bytes 2949124
  72.3 2.3 %collective-permute-start.7 = (bf16[1,192,1280]{2,1,0:T(8,128)(2,1)S(1)}, bf16[1,192,1280]{2,1,0:T(8,128)(2,1)S(1)}, u32[]{:S(2)}, u32[]{:S(2)}) collective-permute-start(bf16[1,192,1280]{2,1,0:T(8,128)(2,1)S(1)} %slice.36), channel_id=1, source_target_pairs={{0,2},{1,3},{2,0},{3,1},{4,6},{5,7},{6,4},{7,5},{8,10},{9,11},{10,... | collective-permute-start | bytes 1474568 | tf_op jit(solution)/shard_map/ppermute | solution.py:810
  72.9 2.2 %collective-permute-start.8 = (bf16[1,192,1280]{2,1,0:T(8,128)(2,1)S(1)}, bf16[1,192,1280]{2,1,0:T(8,128)(2,1)S(1)}, u32[]{:S(2)}, u32[]{:S(2)}) collective-permute-start(bf16[1,192,1280]{2,1,0:T(8,128)(2,1)S(1)} %slice.37), channel_id=1, source_target_pairs={{0,2},{1,3},{2,0},{3,1},{4,6},{5,7},{6,4},{7,5},{8,10},{9,11},{10,... | collective-permute-start | bytes 1474568 | tf_op jit(solution)/shard_map/ppermute | solution.py:810
  74.1 2.0 %collective-permute-start.9 = (bf16[1,192,1280]{2,1,0:T(8,128)(2,1)S(1)}, bf16[1,192,1280]{2,1,0:T(8,128)(2,1)S(1)}, u32[]{:S(2)}, u32[]{:S(2)}) collective-permute-start(bf16[1,192,1280]{2,1,0:T(8,128)(2,1)S(1)} %slice.38), channel_id=1, source_target_pairs={{0,2},{1,3},{2,0},{3,1},{4,6},{5,7},{6,4},{7,5},{8,10},{9,11},{10,... | collective-permute-start | bytes 1474568 | tf_op jit(solution)/shard_map/ppermute | solution.py:810
  76.1 18.1 %copy-start.14 = (bf16[192,5120]{1,0:T(8,128)(2,1)S(1)}, bf16[192,5120]{1,0:T(8,128)(2,1)}, u32[]{:S(2)}) copy-start(bf16[192,5120]{1,0:T(8,128)(2,1)} %rest_1_.3) | copy-start | bytes 5898244
  91.5 0.8 copy-start.4
  92.3 0.7 copy-start.6
  93.0 1.2 copy-start.2
  93.0 1.2 collective-permute-start.13
  94.2 1.2 copy-start.1
  103.3 4.7 %copy-start.7 = (bf16[784,256]{1,0:T(8,128)(2,1)S(1)}, bf16[784,256]{1,0:T(8,128)(2,1)}, u32[]{:S(2)}) copy-start(bf16[784,256]{1,0:T(8,128)(2,1)} %copy-done.6) | copy-start | bytes 1204228
  103.3 5.4 %copy-start.5 = (bf16[784,256]{1,0:T(8,128)(2,1)S(1)}, bf16[784,256]{1,0:T(8,128)(2,1)}, u32[]{:S(2)}) copy-start(bf16[784,256]{1,0:T(8,128)(2,1)} %copy-done.4) | copy-start | bytes 1204228
  103.3 6.7 %copy-start.3 = (bf16[784,256]{1,0:T(8,128)(2,1)S(1)}, bf16[784,256]{1,0:T(8,128)(2,1)}, u32[]{:S(2)}) copy-start(bf16[784,256]{1,0:T(8,128)(2,1)} %copy-done.2) | copy-start | bytes 1204228
  103.4 28.7 %all-to-all-start.21 = ((bf16[8,192,640]{2,1,0:T(8,128)(2,1)}), bf16[8,192,640]{2,1,0:T(8,128)(2,1)}, u32[]{:S(2)}, u32[]{:S(2)}) async-start(bf16[8,192,640]{2,1,0:T(8,128)(2,1)} %get-tuple-element.404), calls=%async_computation.21 | async-start | bytes 3932160 | tf_op jit(solution)/shard_map/all_to_all | solution.py:838
  108.1 24.0 %collective-permute-start.10 = (bf16[784,256]{1,0:T(8,128)(2,1)S(1)}, bf16[784,256]{1,0:T(8,128)(2,1)S(1)}, u32[]{:S(2)}, u32[]{:S(2)}) collective-permute-start(bf16[784,256]{1,0:T(8,128)(2,1)S(1)} %copy-done.7), channel_id=1, source_target_pairs={{24,0},{25,1},{26,2},{27,3},{28,4},{29,5},{30,6},{31,7}} | collective-permute-start | bytes 1204232 | tf_op jit(solution)/shard_map/ppermute | solution.py:834
  108.8 27.3 %collective-permute-start.11 = (bf16[784,256]{1,0:T(8,128)(2,1)S(1)}, bf16[784,256]{1,0:T(8,128)(2,1)S(1)}, u32[]{:S(2)}, u32[]{:S(2)}) collective-permute-start(bf16[784,256]{1,0:T(8,128)(2,1)S(1)} %copy-done.5), channel_id=1, source_target_pairs={{16,0},{24,8},{17,1},{25,9},{18,2},{26,10},{19,3},{27,11},{20,4},{... | collective-permute-start | bytes 1204232 | tf_op jit(solution)/shard_map/ppermute | solution.py:834
  110.1 34.6 %collective-permute-start.12 = (bf16[784,256]{1,0:T(8,128)(2,1)S(1)}, bf16[784,256]{1,0:T(8,128)(2,1)S(1)}, u32[]{:S(2)}, u32[]{:S(2)}) collective-permute-start(bf16[784,256]{1,0:T(8,128)(2,1)S(1)} %copy-done.3), channel_id=1, source_target_pairs={{8,0},{16,8},{24,16},{9,1},{17,9},{25,17},{10,2},{18,10},{26,18},{... | collective-permute-start | bytes 1204232 | tf_op jit(solution)/shard_map/ppermute | solution.py:834
  147.0 15.8 %all-to-all-start.22 = ((bf16[8,192,256]{2,1,0:T(8,128)(2,1)}), bf16[8,192,256]{2,1,0:T(8,128)(2,1)S(1)}, u32[]{:S(2)}, u32[]{:S(2)}) async-start(bf16[8,192,256]{2,1,0:T(8,128)(2,1)} %combine.1), calls=%async_computation.22 | async-start | bytes 1572864 | tf_op jit(solution)/shard_map/all_to_all | solution.py:841
  155.7 7.3 %copy-start.11 = (bf16[192,5120]{1,0:T(8,128)(2,1)S(1)}, bf16[192,5120]{1,0:T(8,128)(2,1)}, u32[]{:S(2)}) copy-start(bf16[192,5120]{1,0:T(8,128)(2,1)} %rest_2_.3) | copy-start | bytes 5898244
  155.8 7.3 %copy-start.18 = (bf16[192,1024]{1,0:T(8,128)(2,1)S(1)}, bf16[192,1024]{1,0:T(8,128)(2,1)}, u32[]{:S(2)}) copy-start(bf16[192,1024]{1,0:T(8,128)(2,1)} %k_ref.1) | copy-start | bytes 1179652
  155.8 7.3 %copy-start.19 = (bf16[192,1024]{1,0:T(8,128)(2,1)S(1)}, bf16[192,1024]{1,0:T(8,128)(2,1)}, u32[]{:S(2)}) copy-start(bf16[192,1024]{1,0:T(8,128)(2,1)} %v_ref.1) | copy-start | bytes 1179652
  155.8 7.3 %copy-start.23 = (s32[192]{0:T(256)S(1)}, s32[192]{0:T(256)}, u32[]{:S(2)}) copy-start(s32[192]{0:T(256)} %param.21) | copy-start | bytes 2308

commit v3 on v2

--- a/solution.py
+++ b/solution.py
@@ -443,21 +443,21 @@
     add_dq(jnp.dot(key_t, dscore, preferred_element_type=jnp.float32))
 
 
-def far_kernel(me_ref, counts_ref, *rest):
-    aux_s, arrays, kvs, rest = rest[0], rest[1:10], rest[10:13], rest[13:]
+def attention_kernel(me_ref, counts_ref, *rest):
+    aux_s, arrays, kv, kvs, rest = rest[0], rest[1:10], rest[10], rest[11:14], rest[14:]
     arrays = (*arrays[:3], arrays[3:6], arrays[6:9])
-    downs, dqt_out, full_ref, rest = rest[:3], rest[3], rest[4], rest[5:]
+    downs, dq_out, own_out, full_ref, rest = rest[:3], rest[3], rest[4], rest[5], rest[6:]
     (
         q_s, do_s, lse_s, delta_s, dqt, kv_s, acc_k, acc_v, tiles, starts, limits, sems, kv_sem,
-        down_sem, dq_sem, down_s,
+        down_sem, out_sem, down_s, dq_s, own,
     ) = rest
     capacity = downs[0].shape[0] - INFO_ROWS
     scale = HEAD_SIZE ** (-0.5)
     each = load_rows(me_ref[0], counts_ref, arrays, q_s, do_s, sems)
     each(lambda copy: copy.start())
     kv_copies = [
-        pltpu.make_async_copy(kvs[n], kv_s.at[n], kv_sem.at[n])
-        for n in range(3)
+        pltpu.make_async_copy(source, kv_s.at[n], kv_sem.at[n])
+        for n, source in enumerate((*kvs, kv))
     ]
     for copy in kv_copies:
         copy.start()
@@ -468,6 +468,7 @@
         return carry
 
     lax.fori_loop(0, length, zero_tile, 0)
+    own[...] = jnp.zeros_like(own)
     spread_lanes(aux_s, lse_s, delta_s)
     for copy in kv_copies:
         copy.wait()
@@ -544,64 +545,17 @@
     for copy in down_copies:
         copy.start()
 
-    def dq_copy(n):
-        tile = tiles[n]
-        return pltpu.make_async_copy(dqt.at[tile], dqt_out.at[tile], dq_sem.at[n])
-
-    def start_dq(n, carry):
-        dq_copy(n).start()
-        return carry
-
-    def wait_dq(n, carry):
-        dq_copy(n).wait()
-        return carry
-
-    lax.fori_loop(0, length, start_dq, 0)
-    for copy in down_copies:
-        copy.wait()
-    lax.fori_loop(0, length, wait_dq, 0)
-
-
-def own_kernel(me_ref, counts_ref, *rest):
-    aux_s, arrays, kv, dqt_in, rest = rest[0], rest[1:10], rest[10], rest[11], rest[13:]
-    arrays = (*arrays[:3], arrays[3:6], arrays[6:9])
-    dq_out, own, rest = rest[0], rest[1], rest[2:]
-    q_s, do_s, lse_s, delta_s, dqt, acc_k, acc_v, tiles, starts, sems, dq_sem, dq_s, out_sem = rest
-    capacity = kv.shape[0] - INFO_ROWS
-    home_rows = dq_out.shape[1]
-    scale = HEAD_SIZE ** (-0.5)
-    me = me_ref[0]
-    each = load_rows(me, counts_ref, arrays, q_s, do_s, sems)
-    each(lambda copy: copy.start())
-    length, total = list_tiles(counts_ref, tiles, starts)
     limit = jnp.minimum(total, capacity)
-
-    def dq_copy(n):
-        tile = tiles[n]
-        return pltpu.make_async_copy(dqt_in.at[tile], dqt.at[tile], dq_sem.at[n])
-
-    def start_dq(n, carry):
-        dq_copy(n).start()
-        return carry
-
-    def wait_dq(n, carry):
-        dq_copy(n).wait()
-        return carry
-
-    lax.fori_loop(0, length, start_dq, 0)
-    own[...] = jnp.zeros_like(own)
-    spread_lanes(aux_s, lse_s, delta_s)
-    each(lambda copy: copy.wait())
-    lax.fori_loop(0, length, wait_dq, 0)
-    lane = lax.broadcasted_iota(jnp.int32, (1, WIDTH), 1) % ROW_TILE
 
     def key_step(kt, carry):
         start = pl.multiple_of(kt * KEY_TILE, KEY_TILE)
-        key = kv[pl.ds(start, KEY_TILE), :HEAD_SIZE]
-        value = kv[pl.ds(start, KEY_TILE), HEAD_SIZE:]
+        key = kv_s[3, pl.ds(start, KEY_TILE), :HEAD_SIZE]
+        value = kv_s[3, pl.ds(start, KEY_TILE), HEAD_SIZE:]
         key_t = key.T
-        acc_k[...] = jnp.zeros_like(acc_k)
-        acc_v[...] = jnp.zeros_like(acc_v)
+        own_k = acc_k.at[pl.ds(0, KEY_TILE), :]
+        own_v = acc_v.at[pl.ds(0, KEY_TILE), :]
+        own_k[...] = jnp.zeros_like(own_k)
+        own_v[...] = jnp.zeros_like(own_v)
         position = start + lax.broadcasted_iota(jnp.int32, (KEY_TILE, 1), 0)
 
         def row_step(n, inner):
@@ -620,17 +574,19 @@
 
                 tile_step(
                     key, value, key_t, row_tile(tile, q_s, do_s, lse_s, delta_s), position, bound,
-                    acc_k, acc_v, add_dq,
+                    own_k, own_v, add_dq,
                 )
 
             return inner
 
         lax.fori_loop(0, length, row_step, 0)
-        own[pl.ds(start, KEY_TILE), :HEAD_SIZE] = acc_k[...] * scale
-        own[pl.ds(start, KEY_TILE), HEAD_SIZE:] = acc_v[...]
+        own[pl.ds(start, KEY_TILE), :HEAD_SIZE] = own_k[...] * scale
+        own[pl.ds(start, KEY_TILE), HEAD_SIZE:] = own_v[...]
         return carry
 
     lax.fori_loop(0, (limit + KEY_TILE - 1) // KEY_TILE, key_step, 0)
+    own_copy = pltpu.make_async_copy(own, own_out, down_sem.at[3])
+    own_copy.start()
 
     half = ROW_TILE // 2
     copies = []
@@ -659,7 +615,7 @@
         copy = pltpu.make_async_copy(dq_s.at[block], dq_out.at[block], out_sem.at[block])
         copy.start()
         copies.append(copy)
-    for copy in copies:
+    for copy in (*copies, *down_copies, own_copy):
         copy.wait()
 
 
@@ -675,75 +631,51 @@
     ]
 
 
-def far_attention(me, counts, small, arrays, kvs):
+def attention(me, counts, small, arrays, kv, kvs):
     bf16, f32 = jnp.bfloat16, jnp.float32
     blocks = KEY_VALUE_HEADS
-    rows = kvs[0].shape[0]
+    rows = kv.shape[0]
+    capacity = rows - INFO_ROWS
     columns = 2 * HEAD_SIZE
-    plane_rows = 2 * (rows - INFO_ROWS)
+    plane_rows = 2 * capacity
     tile_count = plane_rows // ROW_TILE
+    dq = (blocks, plane_rows // blocks, WIDTH)
     return pl.pallas_call(
-        far_kernel,
+        attention_kernel,
         out_shape=(jax.ShapeDtypeStruct((rows, columns), bf16),) * 3
         + (
-            jax.ShapeDtypeStruct((tile_count, HEAD_SIZE, WIDTH), f32),
+            jax.ShapeDtypeStruct(dq, bf16),
+            jax.ShapeDtypeStruct((capacity, columns), f32),
             jax.ShapeDtypeStruct((1,), jnp.int32),
         ),
-        in_specs=[SMEM] * 2 + [VMEM] + [HBM] * 12,
-        out_specs=[HBM] * 4 + [SMEM],
-        scratch_shapes=row_scratch(plane_rows)
-        + [
-            pltpu.VMEM((3, rows, columns), bf16),
-            pltpu.VMEM((rows - INFO_ROWS, HEAD_SIZE), f32),
-            pltpu.VMEM((rows - INFO_ROWS, HEAD_SIZE), f32),
+        in_specs=[SMEM] * 2 + [VMEM] + [HBM] * 13,
+        out_specs=[HBM] * 5 + [SMEM],
+        scratch_shapes=[
+            pltpu.VMEM((plane_rows, WIDTH), bf16),
+            pltpu.VMEM((plane_rows, WIDTH), bf16),
+            pltpu.VMEM((tile_count, WIDTH), f32),
+            pltpu.VMEM((tile_count, WIDTH), f32),
+            pltpu.VMEM((tile_count, HEAD_SIZE, WIDTH), f32),
+            pltpu.VMEM((4, rows, columns), bf16),
+            pltpu.VMEM((capacity, HEAD_SIZE), f32),
+            pltpu.VMEM((capacity, HEAD_SIZE), f32),
             pltpu.SMEM((tile_count + 1,), jnp.int32),
             pltpu.SMEM((blocks,), jnp.int32),
             pltpu.SMEM((3,), jnp.int32),
             pltpu.SemaphoreType.DMA((2 * blocks,)),
-            pltpu.SemaphoreType.DMA((3,)),
-            pltpu.SemaphoreType.DMA((3,)),
-            pltpu.SemaphoreType.DMA((tile_count,)),
+            pltpu.SemaphoreType.DMA((4,)),
+            pltpu.SemaphoreType.DMA((4,)),
+            pltpu.SemaphoreType.DMA((blocks,)),
             pltpu.VMEM((3, rows, columns), bf16),
+            pltpu.VMEM(dq, bf16),
+            pltpu.VMEM((capacity, columns), f32),
         ],
         compiler_params=pltpu.CompilerParams(vmem_limit_bytes=48 * 1024 * 1024),
         cost_estimate=pl.CostEstimate(
             flops=10_000_000_000, bytes_accessed=12_000_000, transcendentals=8_000_000
         ),
-        name="far_attention",
-    )(me, counts, small, *arrays, *kvs)
-
-
-def own_attention(me, counts, small, arrays, kv, dqt, note):
-    bf16, f32 = jnp.bfloat16, jnp.float32
-    blocks = KEY_VALUE_HEADS
-    capacity = kv.shape[0] - INFO_ROWS
-    plane_rows = 2 * capacity
-    tile_count = plane_rows // ROW_TILE
-    return pl.pallas_call(
-        own_kernel,
-        out_shape=(
-            jax.ShapeDtypeStruct((blocks, plane_rows // blocks, WIDTH), bf16),
-            jax.ShapeDtypeStruct((capacity, 2 * HEAD_SIZE), f32),
-        ),
-        in_specs=[SMEM] * 2 + [VMEM] + [HBM] * 9 + [VMEM, HBM, HBM],
-        out_specs=[HBM, VMEM],
-        scratch_shapes=row_scratch(plane_rows)
-        + [
-            pltpu.VMEM((KEY_TILE, HEAD_SIZE), f32),
-            pltpu.VMEM((KEY_TILE, HEAD_SIZE), f32),
-            pltpu.SMEM((tile_count + 1,), jnp.int32),
-            pltpu.SMEM((blocks,), jnp.int32),
-            pltpu.SemaphoreType.DMA((2 * blocks,)),
-            pltpu.SemaphoreType.DMA((tile_count,)),
-            pltpu.VMEM((blocks, plane_rows // blocks, WIDTH), bf16),
-            pltpu.SemaphoreType.DMA((blocks,)),
-        ],
-        compiler_params=pltpu.CompilerParams(vmem_limit_bytes=48 * 1024 * 1024),
-        cost_estimate=pl.CostEstimate(
-            flops=1_000_000, bytes_accessed=100_000, transcendentals=1_000
-        ),
-        name="own_attention",
-    )(me, counts, small, *arrays, kv, dqt, note)
+        name="attention",
+    )(me, counts, small, *arrays, kv, *kvs)
 
 
 def unpack_rows_kernel(parts, out):
@@ -814,9 +746,9 @@
     )
     me, sent = lax.optimization_barrier((me, sent))
     arrived = lax.all_to_all(sent, plane, split_axis=0, concat_axis=0, tiled=True)
-    pairs = [
-        swap(pack_rows((chip, chip ^ CORE), me, queries, output_gradient), chip) for chip in CHIPS
-    ]
+    packed = [pack_rows((chip, chip ^ CORE), me, queries, output_gradient) for chip in CHIPS]
+    me, packed[-1] = lax.optimization_barrier((me, packed[-1]))
+    pairs = [swap(rows, chip) for rows, chip in zip(packed, CHIPS)]
     beside = swap(pack_rows((CORE,), me, queries, output_gradient), CORE)
     arrived, beside = lax.optimization_barrier((arrived, beside))
     mine, small, counts = compact(arrived)
@@ -828,13 +760,11 @@
     crossed = [swap(pair[1:], CORE) for pair in pairs]
     arrays = [queries, output_gradient, beside, *pairs, *crossed]
 
-    *down, dqt, full = far_attention(me, counts, small, arrays, up)
-    note = swap(down[0][capacity:, :HEAD_SIZE], CORE)
+    *down, dq, own, full = attention(me, counts, small, arrays, mine, up)
     backs = [
         lax.ppermute(down[k - 1], "outer", [(i + k, i) for i in range(planes - k)])
         for k in (3, 2, 1)
     ]
-    dq, own = own_attention(me, counts, small, arrays, mine, dqt, note)
     dq = lax.all_to_all(dq, plane, split_axis=0, concat_axis=0, tiled=True)
     dq, own = lax.optimization_barrier((dq, own))
     dq_home = unpack_rows(dq)

time: 174 us -> 172 us (0.989)
  Pallas kernels: 43 us -> 46.3 us
  local copies, waits for them, and re-layouts: 7.45 us -> 5.09 us
  starting transfers between devices: 30.7 us -> 28.8 us
    pallas_call x2 -> x1, Pallas kernels: 23.3 us -> 27 us  [attention(): pl.pallas_call(attention_kernel, out_shape=(jax.ShapeDtypeStruct((rows, c...]
    unnamed x31 -> x17, local copies, waits for them, and re-layouts: 3.59 us -> 0.88 us
    ppermute x3, waiting for transfers between devices: 12.6 us -> 10.7 us  [plane_device(): lax.ppermute(down[k - 1], 'outer', [(i + k, i) for i in range(planes - k)])]
    ppermute x8 -> x7, starting transfers between devices: 4.78 us -> 4.4 us  [swap(): return lax.ppermute(array, plane, [(i, i ^ k) for i in range(blocks)])]
    ppermute x8 -> x7, waiting for transfers between devices: 29.2 us -> 28.8 us  [swap(): return lax.ppermute(array, plane, [(i, i ^ k) for i in range(blocks)])]
  transfers between devices with their start and end apart: 17 -> 16, of which waited for: 12 -> 12; matrix products, arithmetic and copies ran while one was open for 2% -> 1% of each run, Pallas kernels for 7% -> 7%
where the time goes in v3:
time: 172 us; the launch traced here: 169 us
  waiting for transfers between devices  72.3 us (42%)
  Pallas kernels  46.3 us (27%)
  starting transfers between devices  28.8 us (17%)
  between operations  16.9 us (10%)
  local copies, waits for them, and re-layouts  5.09 us (3%)
    ppermute x7, waiting for transfers between devices, swap(): return lax.ppermute(array, plane, [(i, i ^ k) for i in range(blocks)])  28.8 us
    pallas_call x1, Pallas kernels, attention(): pl.pallas_call(attention_kernel, out_shape=(jax.ShapeDtypeStruct((rows, c...  27 us
    all_to_all x1, waiting for transfers between devices, plane_device(): dq = lax.all_to_all(dq, plane, split_axis=0, concat_axis=0, tiled=True)  20.1 us
    ppermute x3, waiting for transfers between devices, plane_device(): lax.ppermute(down[k - 1], 'outer', [(i + k, i) for i in range(planes - k)])  10.7 us
    ppermute x1, waiting for transfers between devices, plane_device(): up = [lax.ppermute(mine, 'outer', [(i, i + 1) for i in range(planes - 1)])]  8.03 us
    pallas_call x4, Pallas kernels, pack_rows(): pl.pallas_call(functools.partial(pack_rows_kernel, partners), out_shape=j...  7.95 us
    pallas_call x1, Pallas kernels, pack_pairs(): pl.pallas_call(functools.partial(pack_pairs_kernel, limit), out_shape=jax...  4.78 us
    all_to_all x1, starting transfers between devices, plane_device(): dq = lax.all_to_all(dq, plane, split_axis=0, concat_axis=0, tiled=True)  4.57 us
  transfers between devices with their start and end apart: 16, of which 12 were waited for; matrix products, arithmetic and copies ran while one was open for 1% of the time, Pallas kernels for 7%

profile of v3, /device:TPU:17, one launch (start us, length us, event | category | flops | bytes accessed | tf_op | source)
XLA Modules:
  0.0 169.3 jit_solution(1089046400346103661)
XLA Ops:
  7.2 0.8 copy.217.lse_ref
  8.0 0.0 copy-start.3
  8.0 4.8 %pack_pairs.1 = bf16[8,208,256]{2,1,0:T(8,128)(2,1)} custom-call(s32[1,192]{1,0:T(1,128)} %bitcast.283, bf16[192,40]{1,0:T(8,128)(2,1)S(1)} %copy.217.lse_ref, bf16[192,1024]{1,0:T(8,128)(2,1)} %k_ref.1, bf16[192,1024]{1,0:T(8,128)(2,1)} %v_ref.1, bf16[192,5120]{1,0:T(8,128)(2,1)} %rest_2_.1, bf16[192,5120]{1,0:T(8,128)(2,1)} %o_ref.1), custom_call_target="tpu_custom_call" | custom-call | tf_op jit(solution)/shard_map/pack_pairs/pallas_call | solution.py:256
  12.8 4.4 %all-to-all-start.20 = ((bf16[8,208,256]{2,1,0:T(8,128)(2,1)}), bf16[8,208,256]{2,1,0:T(8,128)(2,1)S(1)}, u32[]{:S(2)}, u32[]{:S(2)}) async-start(bf16[8,208,256]{2,1,0:T(8,128)(2,1)} %pack_pairs.1), calls=%async_computation.20 | async-start | bytes 1703936 | tf_op jit(solution)/shard_map/all_to_all | solution.py:748
  17.2 0.0 copy-done.3
  17.2 2.1 %pack_rows.4 = bf16[2,192,1280]{2,1,0:T(8,128)(2,1)} custom-call(s32[1]{0:T(128)} %bitcast.48.me_ref, bf16[192,5120]{1,0:T(8,128)(2,1)} %rest_1_.1, bf16[192,5120]{1,0:T(8,128)(2,1)S(1)} %copy-done.3), custom_call_target="tpu_custom_call" | custom-call | tf_op jit(solution)/shard_map/pack_rows/pallas_call | solution.py:292
  19.3 1.8 %pack_rows.5 = bf16[1,192,1280]{2,1,0:T(8,128)(2,1)} custom-call(s32[1]{0:T(128)} %bitcast.48.me_ref, bf16[192,5120]{1,0:T(8,128)(2,1)} %rest_1_.1, bf16[192,5120]{1,0:T(8,128)(2,1)S(1)} %copy-done.3), custom_call_target="tpu_custom_call" | custom-call | tf_op jit(solution)/shard_map/pack_rows/pallas_call | solution.py:292
  21.0 0.1 collective-permute-start
  21.1 2.1 %pack_rows.6 = bf16[2,192,1280]{2,1,0:T(8,128)(2,1)} custom-call(s32[1]{0:T(128)} %bitcast.48.me_ref, bf16[192,5120]{1,0:T(8,128)(2,1)} %rest_1_.1, bf16[192,5120]{1,0:T(8,128)(2,1)S(1)} %copy-done.3), custom_call_target="tpu_custom_call" | custom-call | tf_op jit(solution)/shard_map/pack_rows/pallas_call | solution.py:292
  23.2 2.7 %collective-permute-start.4 = (bf16[2,192,1280]{2,1,0:T(8,128)(2,1)}, bf16[2,192,1280]{2,1,0:T(8,128)(2,1)}, u32[]{:S(2)}, u32[]{:S(2)}) collective-permute-start(bf16[2,192,1280]{2,1,0:T(8,128)(2,1)} %pack_rows.6), channel_id=1, source_target_pairs={{0,5},{1,4},{2,7},{3,6},{4,1},{5,0},{6,3},{7,2},{8,13},{9,12},{10,... | collective-permute-start | bytes 2949128 | tf_op jit(solution)/shard_map/ppermute | solution.py:742
  25.9 2.1 %pack_rows.7 = bf16[2,192,1280]{2,1,0:T(8,128)(2,1)} custom-call(s32[1]{0:T(128)} %bitcast.48.me_ref, bf16[192,5120]{1,0:T(8,128)(2,1)} %rest_1_.1, bf16[192,5120]{1,0:T(8,128)(2,1)S(1)} %copy-done.3), custom_call_target="tpu_custom_call" | custom-call | tf_op jit(solution)/shard_map/pack_rows/pallas_call | solution.py:292
  28.0 0.3 collective-permute-start.5
  28.3 0.1 collective-permute-start.6
  28.4 0.0 collective-permute-done.rest_3_
  28.4 0.8 all-to-all-done.20.arrived
  29.2 0.0 copy-start.4
  29.2 1.1 compact.1
  30.3 3.2 %collective-permute-start.1 = (bf16[784,256]{1,0:T(8,128)(2,1)S(1)}, bf16[784,256]{1,0:T(8,128)(2,1)S(1)}, u32[]{:S(2)}, u32[]{:S(2)}) collective-permute-start(bf16[784,256]{1,0:T(8,128)(2,1)S(1)} %get-tuple-element.395.rest_10_), channel_id=1, source_target_pairs={{0,8},{8,16},{16,24},{1,9},{9,17},{17,25},{2,10},{10,18},{18,26},{... | collective-permute-start | bytes 1204232 | tf_op jit(solution)/shard_map/ppermute | solution.py:755
  33.5 0.7 collective-permute-start.3
  34.2 8.0 %collective-permute-done.1.rest_11_ = bf16[784,256]{1,0:T(8,128)(2,1)S(1)} collective-permute-done((bf16[784,256]{1,0:T(8,128)(2,1)S(1)}, bf16[784,256]{1,0:T(8,128)(2,1)S(1)}, u32[]{:S(2)}, u32[]{:S(2)}) %collective-permute-start.1) | collective-permute-done | bytes 401440 | tf_op jit(solution)/shard_map/ppermute | solution.py:755
  42.2 3.3 %collective-permute-start.2 = (bf16[784,256]{1,0:T(8,128)(2,1)S(1)}, bf16[784,256]{1,0:T(8,128)(2,1)S(1)}, u32[]{:S(2)}, u32[]{:S(2)}) collective-permute-start(bf16[784,256]{1,0:T(8,128)(2,1)S(1)} %collective-permute-done.1.rest_11_), channel_id=1, source_target_pairs={{8,16},{16,24},{9,17},{17,25},{10,18},{18,26},{11,19},{19,27},{12,... | collective-permute-start | bytes 1204232 | tf_op jit(solution)/shard_map/ppermute | solution.py:757
  45.6 5.3 %collective-permute-done.4.rest_4_ = bf16[2,192,1280]{2,1,0:T(8,128)(2,1)} collective-permute-done((bf16[2,192,1280]{2,1,0:T(8,128)(2,1)}, bf16[2,192,1280]{2,1,0:T(8,128)(2,1)}, u32[]{:S(2)}, u32[]{:S(2)}) %collective-permute-start.4) | collective-permute-done | bytes 983072 | tf_op jit(solution)/shard_map/ppermute | solution.py:742
  50.9 20.1 %collective-permute-done.5.rest_5_ = bf16[2,192,1280]{2,1,0:T(8,128)(2,1)S(1)} collective-permute-done((bf16[2,192,1280]{2,1,0:T(8,128)(2,1)}, bf16[2,192,1280]{2,1,0:T(8,128)(2,1)S(1)}, u32[]{:S(2)}, u32[]{:S(2)}) %collective-permute-start.5) | collective-permute-done | bytes 983072 | tf_op jit(solution)/shard_map/ppermute | solution.py:742
  71.0 0.0 copy-start.12
  71.0 1.2 collective-permute-done.6.rest_6_
  72.2 0.0 collective-permute-done.3.rest_13_
  72.2 0.0 collective-permute-done.2.rest_12_
  72.2 1.4 slice.33
  73.6 0.6 collective-permute-start.7
  74.2 0.1 collective-permute-start.8
  74.3 0.6 collective-permute-start.9
  74.9 0.8 collective-permute-done.7.rest_7_
  75.7 0.7 collective-permute-done.8.rest_8_
  76.4 0.7 collective-permute-done.9.rest_9_
  77.1 0.0 copy-done.12
  77.1 0.0 copy-done.13
  77.1 0.0 copy-done.4
  77.1 27.0 %attention.1 = (bf16[784,256]{1,0:T(8,128)(2,1)S(1)}, bf16[784,256]{1,0:T(8,128)(2,1)S(1)}, bf16[784,256]{1,0:T(8,128)(2,1)S(1)}, bf16[8,192,640]{2,1,0:T(8,128)...) custom-call(s32[1]{0:T(128)} %bitcast.48.me_ref, s32[8]{0:T(128)S(1)} %get-tuple-element.392.counts_ref, ...), custom_call_target="tpu_custom_call" | custom-call | flops 10000000000 | bytes 12000000 | tf_op jit(solution)/shard_map/attention/pallas_call | solution.py:643
  104.1 4.6 %all-to-all-start.21 = ((bf16[8,192,640]{2,1,0:T(8,128)(2,1)}), bf16[8,192,640]{2,1,0:T(8,128)(2,1)}, u32[]{:S(2)}, u32[]{:S(2)}) async-start(bf16[8,192,640]{2,1,0:T(8,128)(2,1)} %get-tuple-element.406), calls=%async_computation.21 | async-start | bytes 3932160 | tf_op jit(solution)/shard_map/all_to_all | solution.py:768
  108.7 0.7 collective-permute-start.10
  109.3 1.3 collective-permute-start.11
  110.7 1.9 %collective-permute-start.12 = (bf16[784,256]{1,0:T(8,128)(2,1)S(1)}, bf16[784,256]{1,0:T(8,128)(2,1)S(1)}, u32[]{:S(2)}, u32[]{:S(2)}) collective-permute-start(bf16[784,256]{1,0:T(8,128)(2,1)S(1)} %get-tuple-element.405), channel_id=1, source_target_pairs={{8,0},{16,8},{24,16},{9,1},{17,9},{25,17},{10,2},{18,10},{26,18},{... | collective-permute-start | bytes 1204232 | tf_op jit(solution)/shard_map/ppermute | solution.py:765
  112.6 20.1 %all-to-all-done.21.parts = bf16[8,192,640]{2,1,0:T(8,128)(2,1)} async-done(((bf16[8,192,640]{2,1,0:T(8,128)(2,1)}), bf16[8,192,640]{2,1,0:T(8,128)(2,1)}, u32[]{:S(2)}, u32[]{:S(2)}) %all-to-all-start.21) | async-done | bytes 1966112 | tf_op jit(solution)/shard_map/all_to_all | solution.py:768
  132.7 0.0 collective-permute-done.10.rest_0_
  132.7 2.1 %collective-permute-done.11.rest_1_ = bf16[784,256]{1,0:T(8,128)(2,1)S(1)} collective-permute-done((bf16[784,256]{1,0:T(8,128)(2,1)S(1)}, bf16[784,256]{1,0:T(8,128)(2,1)S(1)}, u32[]{:S(2)}, u32[]{:S(2)}) %collective-permute-start.11) | collective-permute-done | bytes 401440 | tf_op jit(solution)/shard_map/ppermute | solution.py:765
  134.7 8.6 %collective-permute-done.12.rest_2_ = bf16[784,256]{1,0:T(8,128)(2,1)S(1)} collective-permute-done((bf16[784,256]{1,0:T(8,128)(2,1)S(1)}, bf16[784,256]{1,0:T(8,128)(2,1)S(1)}, u32[]{:S(2)}, u32[]{:S(2)}) %collective-permute-start.12) | collective-permute-done | bytes 401440 | tf_op jit(solution)/shard_map/ppermute | solution.py:765
  143.3 2.3 %combine.1 = bf16[8,192,256]{2,1,0:T(8,128)(2,1)} custom-call(s32[8]{0:T(128)S(1)} %get-tuple-element.392.counts_ref, f32[768,256]{1,0:T(8,128)S(1)} %get-tuple-element.408.own, bf16[784,256]{1,0:T(8,128)(2,1)S(1)} %collective-permute-done.10.rest_0_, bf16[784,256]{1,0:T(8,128)(2,1)S(1)} %collective-permute-done.11.rest_1_, ...), custom_call_target="tpu_custom_call" | custom-call | tf_op jit(solution)/shard_map/combine/pallas_call | solution.py:720
  145.6 4.3 %all-to-all-start.22 = ((bf16[8,192,256]{2,1,0:T(8,128)(2,1)}), bf16[8,192,256]{2,1,0:T(8,128)(2,1)S(1)}, u32[]{:S(2)}, u32[]{:S(2)}) async-start(bf16[8,192,256]{2,1,0:T(8,128)(2,1)} %combine.1), calls=%async_computation.22 | async-start | bytes 1572864 | tf_op jit(solution)/shard_map/all_to_all | solution.py:771
  150.6 0.5 slice.49
  151.8 0.5 slice.50
  152.9 0.5 slice.51
  154.1 0.0 copy-start.5
  154.1 0.0 copy-start.9
  154.1 0.0 copy-start.10
  154.2 0.0 copy-start.16
  154.2 3.1 %unpack_rows.1 = bf16[192,5120]{1,0:T(8,128)(2,1)} custom-call(bf16[8,192,640]{2,1,0:T(8,128)(2,1)} %all-to-all-done.21.parts), custom_call_target="tpu_custom_call" | custom-call | tf_op jit(solution)/shard_map/unpack_rows/pallas_call | solution.py:687
  157.3 3.9 %all-to-all-done.22 = bf16[8,192,256]{2,1,0:T(8,128)(2,1)S(1)} async-done(((bf16[8,192,256]{2,1,0:T(8,128)(2,1)}), bf16[8,192,256]{2,1,0:T(8,128)(2,1)S(1)}, u32[]{:S(2)}, u32[]{:S(2)}) %all-to-all-start.22) | async-done | bytes 786464 | tf_op jit(solution)/shard_map/all_to_all | solution.py:771
  161.2 0.2 slice_bitcast_fusion
  161.4 0.0 copy-done.5
  161.4 0.0 copy-done.9
  161.4 0.0 copy-done.10
  161.4 0.0 copy-done.16
  161.4 1.0 conditional.1
  161.5 1.0 copy_bitcast_fusion
  (3 shorter events, 0.1 us)
Async XLA Ops:
  8.0 9.2 %copy-start.3 = (bf16[192,5120]{1,0:T(8,128)(2,1)S(1)}, bf16[192,5120]{1,0:T(8,128)(2,1)}, u32[]{:S(2)}) copy-start(bf16[192,5120]{1,0:T(8,128)(2,1)} %rest_2_.1) | copy-start | bytes 5898244
  12.8 16.4 %all-to-all-start.20 = ((bf16[8,208,256]{2,1,0:T(8,128)(2,1)}), bf16[8,208,256]{2,1,0:T(8,128)(2,1)S(1)}, u32[]{:S(2)}, u32[]{:S(2)}) async-start(bf16[8,208,256]{2,1,0:T(8,128)(2,1)} %pack_pairs.1), calls=%async_computation.20 | async-start | bytes 1703936 | tf_op jit(solution)/shard_map/all_to_all | solution.py:748
  21.0 7.4 %collective-permute-start = (bf16[1,192,1280]{2,1,0:T(8,128)(2,1)}, bf16[1,192,1280]{2,1,0:T(8,128)(2,1)S(1)}, u32[]{:S(2)}, u32[]{:S(2)}) collective-permute-start(bf16[1,192,1280]{2,1,0:T(8,128)(2,1)} %pack_rows.5), channel_id=1, source_target_pairs={{0,2},{1,3},{2,0},{3,1},{4,6},{5,7},{6,4},{7,5},{8,10},{9,11},{10,... | collective-permute-start | bytes 1474568 | tf_op jit(solution)/shard_map/ppermute | solution.py:742
  23.2 27.7 %collective-permute-start.4 = (bf16[2,192,1280]{2,1,0:T(8,128)(2,1)}, bf16[2,192,1280]{2,1,0:T(8,128)(2,1)}, u32[]{:S(2)}, u32[]{:S(2)}) collective-permute-start(bf16[2,192,1280]{2,1,0:T(8,128)(2,1)} %pack_rows.6), channel_id=1, source_target_pairs={{0,5},{1,4},{2,7},{3,6},{4,1},{5,0},{6,3},{7,2},{8,13},{9,12},{10,... | collective-permute-start | bytes 2949128 | tf_op jit(solution)/shard_map/ppermute | solution.py:742
  28.0 43.0 %collective-permute-start.5 = (bf16[2,192,1280]{2,1,0:T(8,128)(2,1)}, bf16[2,192,1280]{2,1,0:T(8,128)(2,1)S(1)}, u32[]{:S(2)}, u32[]{:S(2)}) collective-permute-start(bf16[2,192,1280]{2,1,0:T(8,128)(2,1)} %pack_rows.7), channel_id=1, source_target_pairs={{0,4},{1,5},{2,6},{3,7},{4,0},{5,1},{6,2},{7,3},{8,12},{9,13},{10,... | collective-permute-start | bytes 2949128 | tf_op jit(solution)/shard_map/ppermute | solution.py:742
  28.3 43.9 %collective-permute-start.6 = (bf16[2,192,1280]{2,1,0:T(8,128)(2,1)}, bf16[2,192,1280]{2,1,0:T(8,128)(2,1)S(1)}, u32[]{:S(2)}, u32[]{:S(2)}) collective-permute-start(bf16[2,192,1280]{2,1,0:T(8,128)(2,1)} %pack_rows.4), channel_id=1, source_target_pairs={{0,1},{1,0},{2,3},{3,2},{4,5},{5,4},{6,7},{7,6},{8,9},{9,8},{10,11... | collective-permute-start | bytes 2949128 | tf_op jit(solution)/shard_map/ppermute | solution.py:742
  29.2 47.9 %copy-start.4 = (bf16[192,5120]{1,0:T(8,128)(2,1)S(1)}, bf16[192,5120]{1,0:T(8,128)(2,1)}, u32[]{:S(2)}) copy-start(bf16[192,5120]{1,0:T(8,128)(2,1)} %rest_2_.1) | copy-start | bytes 5898244
  30.3 11.9 %collective-permute-start.1 = (bf16[784,256]{1,0:T(8,128)(2,1)S(1)}, bf16[784,256]{1,0:T(8,128)(2,1)S(1)}, u32[]{:S(2)}, u32[]{:S(2)}) collective-permute-start(bf16[784,256]{1,0:T(8,128)(2,1)S(1)} %get-tuple-element.395.rest_10_), channel_id=1, source_target_pairs={{0,8},{8,16},{16,24},{1,9},{9,17},{17,25},{2,10},{10,18},{18,26},{... | collective-permute-start | bytes 1204232 | tf_op jit(solution)/shard_map/ppermute | solution.py:755
  33.5 38.7 %collective-permute-start.3 = (bf16[784,256]{1,0:T(8,128)(2,1)S(1)}, bf16[784,256]{1,0:T(8,128)(2,1)S(1)}, u32[]{:S(2)}, u32[]{:S(2)}) collective-permute-start(bf16[784,256]{1,0:T(8,128)(2,1)S(1)} %get-tuple-element.395.rest_10_), channel_id=1, source_target_pairs={{0,24},{1,25},{2,26},{3,27},{4,28},{5,29},{6,30},{7,31}} | collective-permute-start | bytes 1204232 | tf_op jit(solution)/shard_map/ppermute | solution.py:756
  42.2 30.0 %collective-permute-start.2 = (bf16[784,256]{1,0:T(8,128)(2,1)S(1)}, bf16[784,256]{1,0:T(8,128)(2,1)S(1)}, u32[]{:S(2)}, u32[]{:S(2)}) collective-permute-start(bf16[784,256]{1,0:T(8,128)(2,1)S(1)} %collective-permute-done.1.rest_11_), channel_id=1, source_target_pairs={{8,16},{16,24},{9,17},{17,25},{10,18},{18,26},{11,19},{19,27},{12,... | collective-permute-start | bytes 1204232 | tf_op jit(solution)/shard_map/ppermute | solution.py:757
  71.0 6.1 %copy-start.12 = (bf16[2,192,1280]{2,1,0:T(8,128)(2,1)}, bf16[2,192,1280]{2,1,0:T(8,128)(2,1)S(1)}, u32[]{:S(2)}) copy-start(bf16[2,192,1280]{2,1,0:T(8,128)(2,1)S(1)} %collective-permute-done.5.rest_5_) | copy-start | bytes 2949124
  72.2 4.9 %copy-start.13 = (bf16[2,192,1280]{2,1,0:T(8,128)(2,1)}, bf16[2,192,1280]{2,1,0:T(8,128)(2,1)S(1)}, u32[]{:S(2)}) copy-start(bf16[2,192,1280]{2,1,0:T(8,128)(2,1)S(1)} %collective-permute-done.6.rest_6_) | copy-start | bytes 2949124
  73.6 2.0 %collective-permute-start.7 = (bf16[1,192,1280]{2,1,0:T(8,128)(2,1)S(1)}, bf16[1,192,1280]{2,1,0:T(8,128)(2,1)S(1)}, u32[]{:S(2)}, u32[]{:S(2)}) collective-permute-start(bf16[1,192,1280]{2,1,0:T(8,128)(2,1)S(1)} %slice.33), channel_id=1, source_target_pairs={{0,2},{1,3},{2,0},{3,1},{4,6},{5,7},{6,4},{7,5},{8,10},{9,11},{10,... | collective-permute-start | bytes 1474568 | tf_op jit(solution)/shard_map/ppermute | solution.py:742
  74.2 2.2 %collective-permute-start.8 = (bf16[1,192,1280]{2,1,0:T(8,128)(2,1)S(1)}, bf16[1,192,1280]{2,1,0:T(8,128)(2,1)S(1)}, u32[]{:S(2)}, u32[]{:S(2)}) collective-permute-start(bf16[1,192,1280]{2,1,0:T(8,128)(2,1)S(1)} %slice.34), channel_id=1, source_target_pairs={{0,2},{1,3},{2,0},{3,1},{4,6},{5,7},{6,4},{7,5},{8,10},{9,11},{10,... | collective-permute-start | bytes 1474568 | tf_op jit(solution)/shard_map/ppermute | solution.py:742
  74.3 2.7 %collective-permute-start.9 = (bf16[1,192,1280]{2,1,0:T(8,128)(2,1)S(1)}, bf16[1,192,1280]{2,1,0:T(8,128)(2,1)S(1)}, u32[]{:S(2)}, u32[]{:S(2)}) collective-permute-start(bf16[1,192,1280]{2,1,0:T(8,128)(2,1)S(1)} %slice.35), channel_id=1, source_target_pairs={{0,2},{1,3},{2,0},{3,1},{4,6},{5,7},{6,4},{7,5},{8,10},{9,11},{10,... | collective-permute-start | bytes 1474568 | tf_op jit(solution)/shard_map/ppermute | solution.py:742
  104.1 28.6 %all-to-all-start.21 = ((bf16[8,192,640]{2,1,0:T(8,128)(2,1)}), bf16[8,192,640]{2,1,0:T(8,128)(2,1)}, u32[]{:S(2)}, u32[]{:S(2)}) async-start(bf16[8,192,640]{2,1,0:T(8,128)(2,1)} %get-tuple-element.406), calls=%async_computation.21 | async-start | bytes 3932160 | tf_op jit(solution)/shard_map/all_to_all | solution.py:768
  108.7 24.0 %collective-permute-start.10 = (bf16[784,256]{1,0:T(8,128)(2,1)S(1)}, bf16[784,256]{1,0:T(8,128)(2,1)S(1)}, u32[]{:S(2)}, u32[]{:S(2)}) collective-permute-start(bf16[784,256]{1,0:T(8,128)(2,1)S(1)} %get-tuple-element.403), channel_id=1, source_target_pairs={{24,0},{25,1},{26,2},{27,3},{28,4},{29,5},{30,6},{31,7}} | collective-permute-start | bytes 1204232 | tf_op jit(solution)/shard_map/ppermute | solution.py:765
  109.3 25.4 %collective-permute-start.11 = (bf16[784,256]{1,0:T(8,128)(2,1)S(1)}, bf16[784,256]{1,0:T(8,128)(2,1)S(1)}, u32[]{:S(2)}, u32[]{:S(2)}) collective-permute-start(bf16[784,256]{1,0:T(8,128)(2,1)S(1)} %get-tuple-element.404), channel_id=1, source_target_pairs={{16,0},{24,8},{17,1},{25,9},{18,2},{26,10},{19,3},{27,11},{20,4},{... | collective-permute-start | bytes 1204232 | tf_op jit(solution)/shard_map/ppermute | solution.py:765
  110.7 32.7 %collective-permute-start.12 = (bf16[784,256]{1,0:T(8,128)(2,1)S(1)}, bf16[784,256]{1,0:T(8,128)(2,1)S(1)}, u32[]{:S(2)}, u32[]{:S(2)}) collective-permute-start(bf16[784,256]{1,0:T(8,128)(2,1)S(1)} %get-tuple-element.405), channel_id=1, source_target_pairs={{8,0},{16,8},{24,16},{9,1},{17,9},{25,17},{10,2},{18,10},{26,18},{... | collective-permute-start | bytes 1204232 | tf_op jit(solution)/shard_map/ppermute | solution.py:765
  145.6 15.6 %all-to-all-start.22 = ((bf16[8,192,256]{2,1,0:T(8,128)(2,1)}), bf16[8,192,256]{2,1,0:T(8,128)(2,1)S(1)}, u32[]{:S(2)}, u32[]{:S(2)}) async-start(bf16[8,192,256]{2,1,0:T(8,128)(2,1)} %combine.1), calls=%async_computation.22 | async-start | bytes 1572864 | tf_op jit(solution)/shard_map/all_to_all | solution.py:771
  154.1 7.3 %copy-start.5 = (bf16[192,5120]{1,0:T(8,128)(2,1)S(1)}, bf16[192,5120]{1,0:T(8,128)(2,1)}, u32[]{:S(2)}) copy-start(bf16[192,5120]{1,0:T(8,128)(2,1)} %rest_2_.1) | copy-start | bytes 5898244
  154.1 7.3 %copy-start.9 = (bf16[192,1024]{1,0:T(8,128)(2,1)S(1)}, bf16[192,1024]{1,0:T(8,128)(2,1)}, u32[]{:S(2)}) copy-start(bf16[192,1024]{1,0:T(8,128)(2,1)} %k_ref.1) | copy-start | bytes 1179652
  154.1 7.3 %copy-start.10 = (bf16[192,1024]{1,0:T(8,128)(2,1)S(1)}, bf16[192,1024]{1,0:T(8,128)(2,1)}, u32[]{:S(2)}) copy-start(bf16[192,1024]{1,0:T(8,128)(2,1)} %v_ref.1) | copy-start | bytes 1179652
  154.2 7.3 %copy-start.16 = (s32[192]{0:T(256)S(1)}, s32[192]{0:T(256)}, u32[]{:S(2)}) copy-start(s32[192]{0:T(256)} %param.21) | copy-start | bytes 2308

commit v4 on v3

--- a/solution.py
+++ b/solution.py
@@ -443,52 +443,73 @@
     add_dq(jnp.dot(key_t, dscore, preferred_element_type=jnp.float32))
 
 
-def attention_kernel(me_ref, counts_ref, *rest):
-    aux_s, arrays, kv, kvs, rest = rest[0], rest[1:10], rest[10], rest[11:14], rest[14:]
+def attention_kernel(first, me_ref, counts_ref, *rest):
+    aux_s, arrays, kvs, rest = rest[0], rest[1:10], rest[10:12], rest[12:]
     arrays = (*arrays[:3], arrays[3:6], arrays[6:9])
-    downs, dq_out, own_out, full_ref, rest = rest[:3], rest[3], rest[4], rest[5], rest[6:]
+    if first:
+        far, downs, dqt_out, full_ref, rest = 2, rest[:2], rest[2], rest[3], rest[4:]
+    else:
+        dqt_in, far, downs, rest = rest[0], 1, rest[1:2], rest[2:]
+        dq_out, own_out, full_ref, rest = rest[0], rest[1], rest[2], rest[3:]
     (
         q_s, do_s, lse_s, delta_s, dqt, kv_s, acc_k, acc_v, tiles, starts, limits, sems, kv_sem,
-        down_sem, out_sem, down_s, dq_s, own,
-    ) = rest
+        down_sem, dqt_sem, down_s,
+    ) = rest[:16]
+    if not first:
+        out_sem, dq_s, own = rest[16:]
     capacity = downs[0].shape[0] - INFO_ROWS
     scale = HEAD_SIZE ** (-0.5)
     each = load_rows(me_ref[0], counts_ref, arrays, q_s, do_s, sems)
     each(lambda copy: copy.start())
     kv_copies = [
         pltpu.make_async_copy(source, kv_s.at[n], kv_sem.at[n])
-        for n, source in enumerate((*kvs, kv))
+        for n, source in enumerate(kvs)
     ]
     for copy in kv_copies:
         copy.start()
     length, total = list_tiles(counts_ref, tiles, starts)
 
-    def zero_tile(n, carry):
-        dqt[tiles[n]] = jnp.zeros(dqt.shape[1:], jnp.float32)
-        return carry
-
-    lax.fori_loop(0, length, zero_tile, 0)
-    own[...] = jnp.zeros_like(own)
+    def each_tile(act):
+        def step(n, carry):
+            act(n, tiles[n])
+            return carry
+
+        lax.fori_loop(0, length, step, 0)
+
+    if first:
+
+        def zero_tile(n, tile):
+            dqt[tile] = jnp.zeros(dqt.shape[1:], jnp.float32)
+
+        each_tile(zero_tile)
+    else:
+
+        def load(n, tile):
+            return pltpu.make_async_copy(dqt_in.at[tile], dqt.at[tile], dqt_sem.at[n])
+
+        each_tile(lambda n, tile: load(n, tile).start())
+        own[...] = jnp.zeros_like(own)
     spread_lanes(aux_s, lse_s, delta_s)
     for copy in kv_copies:
         copy.wait()
     most = total
-    for n in range(3):
+    for n in range(far):
         info = kv_s[n, capacity:, :].astype(jnp.float32)
         limit = (jnp.max(info[0:1]) * 64.0 + jnp.max(info[1:2])).astype(jnp.int32)
         limits[n] = jnp.minimum(limit, capacity)
         most = jnp.maximum(most, limit)
-    full = most > capacity
-    full_ref[0] = full.astype(jnp.int32)
-    for n in range(3):
+    full_ref[0] = (most > capacity).astype(jnp.int32)
+    for n in range(far):
         down_s[n, capacity:, :] = jnp.full(
-            (INFO_ROWS, 2 * HEAD_SIZE), jnp.where(full, 1.0, 0.0)
+            (INFO_ROWS, 2 * HEAD_SIZE), jnp.where(most > capacity, 1.0, 0.0)
         ).astype(jnp.bfloat16)
     each(lambda copy: copy.wait())
+    if not first:
+        each_tile(lambda n, tile: load(n, tile).wait())
     lane = lax.broadcasted_iota(jnp.int32, (1, WIDTH), 1) % ROW_TILE
 
     def block_step(step, carry):
-        index = 2 - step
+        index = far - 1 - step
         limit = limits[index]
 
         def run(rows):
@@ -538,19 +559,30 @@
 
         return carry
 
-    lax.fori_loop(0, 3, block_step, 0)
+    lax.fori_loop(0, far, block_step, 0)
     down_copies = [
-        pltpu.make_async_copy(down_s.at[n], downs[n], down_sem.at[n]) for n in range(3)
+        pltpu.make_async_copy(down_s.at[n], downs[n], down_sem.at[n]) for n in range(far)
     ]
     for copy in down_copies:
         copy.start()
 
+    if first:
+
+        def save(n, tile):
+            return pltpu.make_async_copy(dqt.at[tile], dqt_out.at[tile], dqt_sem.at[n])
+
+        each_tile(lambda n, tile: save(n, tile).start())
+        for copy in down_copies:
+            copy.wait()
+        each_tile(lambda n, tile: save(n, tile).wait())
+        return
+
     limit = jnp.minimum(total, capacity)
 
     def key_step(kt, carry):
         start = pl.multiple_of(kt * KEY_TILE, KEY_TILE)
-        key = kv_s[3, pl.ds(start, KEY_TILE), :HEAD_SIZE]
-        value = kv_s[3, pl.ds(start, KEY_TILE), HEAD_SIZE:]
+        key = kv_s[1, pl.ds(start, KEY_TILE), :HEAD_SIZE]
+        value = kv_s[1, pl.ds(start, KEY_TILE), HEAD_SIZE:]
         key_t = key.T
         own_k = acc_k.at[pl.ds(0, KEY_TILE), :]
         own_v = acc_v.at[pl.ds(0, KEY_TILE), :]
@@ -585,7 +617,7 @@
         return carry
 
     lax.fori_loop(0, (limit + KEY_TILE - 1) // KEY_TILE, key_step, 0)
-    own_copy = pltpu.make_async_copy(own, own_out, down_sem.at[3])
+    own_copy = pltpu.make_async_copy(own, own_out, down_sem.at[1])
     own_copy.start()
 
     half = ROW_TILE // 2
@@ -631,51 +663,59 @@
     ]
 
 
-def attention(me, counts, small, arrays, kv, kvs):
+def attention(first, me, counts, small, arrays, kvs, *before):
     bf16, f32 = jnp.bfloat16, jnp.float32
     blocks = KEY_VALUE_HEADS
-    rows = kv.shape[0]
+    rows = kvs[0].shape[0]
     capacity = rows - INFO_ROWS
     columns = 2 * HEAD_SIZE
     plane_rows = 2 * capacity
     tile_count = plane_rows // ROW_TILE
     dq = (blocks, plane_rows // blocks, WIDTH)
+    dqt = (tile_count, HEAD_SIZE, WIDTH)
+    down = jax.ShapeDtypeStruct((rows, columns), bf16)
+    flag = jax.ShapeDtypeStruct((1,), jnp.int32)
+    if first:
+        outs = (down, down, jax.ShapeDtypeStruct(dqt, f32), flag)
+        more = []
+    else:
+        own = jax.ShapeDtypeStruct((capacity, columns), f32)
+        outs = (down, jax.ShapeDtypeStruct(dq, bf16), own, flag)
+        more = [
+            pltpu.SemaphoreType.DMA((blocks,)),
+            pltpu.VMEM(dq, bf16),
+            pltpu.VMEM((capacity, columns), f32),
+        ]
     return pl.pallas_call(
-        attention_kernel,
-        out_shape=(jax.ShapeDtypeStruct((rows, columns), bf16),) * 3
-        + (
-            jax.ShapeDtypeStruct(dq, bf16),
-            jax.ShapeDtypeStruct((capacity, columns), f32),
-            jax.ShapeDtypeStruct((1,), jnp.int32),
-        ),
-        in_specs=[SMEM] * 2 + [VMEM] + [HBM] * 13,
-        out_specs=[HBM] * 5 + [SMEM],
+        functools.partial(attention_kernel, first),
+        out_shape=outs,
+        in_specs=[SMEM] * 2 + [VMEM] + [HBM] * (11 + len(before)),
+        out_specs=[HBM] * 3 + [SMEM],
         scratch_shapes=[
             pltpu.VMEM((plane_rows, WIDTH), bf16),
             pltpu.VMEM((plane_rows, WIDTH), bf16),
             pltpu.VMEM((tile_count, WIDTH), f32),
             pltpu.VMEM((tile_count, WIDTH), f32),
-            pltpu.VMEM((tile_count, HEAD_SIZE, WIDTH), f32),
-            pltpu.VMEM((4, rows, columns), bf16),
+            pltpu.VMEM(dqt, f32),
+            pltpu.VMEM((2, rows, columns), bf16),
             pltpu.VMEM((capacity, HEAD_SIZE), f32),
             pltpu.VMEM((capacity, HEAD_SIZE), f32),
             pltpu.SMEM((tile_count + 1,), jnp.int32),
             pltpu.SMEM((blocks,), jnp.int32),
-            pltpu.SMEM((3,), jnp.int32),
+            pltpu.SMEM((2,), jnp.int32),
             pltpu.SemaphoreType.DMA((2 * blocks,)),
-            pltpu.SemaphoreType.DMA((4,)),
-            pltpu.SemaphoreType.DMA((4,)),
-            pltpu.SemaphoreType.DMA((blocks,)),
-            pltpu.VMEM((3, rows, columns), bf16),
-            pltpu.VMEM(dq, bf16),
-            pltpu.VMEM((capacity, columns), f32),
+            pltpu.SemaphoreType.DMA((2,)),
+            pltpu.SemaphoreType.DMA((2,)),
+            pltpu.SemaphoreType.DMA((tile_count,)),
+            pltpu.VMEM((2, rows, columns), bf16),
+            *more,
         ],
         compiler_params=pltpu.CompilerParams(vmem_limit_bytes=48 * 1024 * 1024),
         cost_estimate=pl.CostEstimate(
-            flops=10_000_000_000, bytes_accessed=12_000_000, transcendentals=8_000_000
+            flops=5_000_000_000, bytes_accessed=12_000_000, transcendentals=4_000_000
         ),
         name="attention",
-    )(me, counts, small, *arrays, kv, *kvs)
+    )(me, counts, small, *arrays, *kvs, *before)
 
 
 def unpack_rows_kernel(parts, out):
@@ -760,18 +800,21 @@
     crossed = [swap(pair[1:], CORE) for pair in pairs]
     arrays = [queries, output_gradient, beside, *pairs, *crossed]
 
-    *down, dq, own, full = attention(me, counts, small, arrays, mine, up)
-    backs = [
-        lax.ppermute(down[k - 1], "outer", [(i + k, i) for i in range(planes - k)])
-        for k in (3, 2, 1)
-    ]
+    def lower(rows, k):
+        return lax.ppermute(rows, "outer", [(i + k, i) for i in range(planes - k)])
+
+    down2, down3, dqt, full1 = attention(True, me, counts, small, arrays, [up[1], up[2]])
+    back2 = lower(down2, 2)
+    down1, dq, own, full2 = attention(False, me, counts, small, arrays, [up[0], mine], dqt)
+    dq, back2 = lax.optimization_barrier((dq, back2))
+    backs = [lower(down3, 3), back2, lower(down1, 1)]
     dq = lax.all_to_all(dq, plane, split_axis=0, concat_axis=0, tiled=True)
     dq, own = lax.optimization_barrier((dq, own))
     dq_home = unpack_rows(dq)
     kv_home = lax.all_to_all(
         combine(counts, own, backs, home_rows), plane, split_axis=0, concat_axis=0, tiled=True
     )
-    full = full[0] > 0
+    full = (full1[0] + full2[0]) > 0
     for back in backs:
         full = full | (back[capacity, 0] > 0)
     dk = kv_home[:, :, :HEAD_SIZE].transpose(1, 0, 2).reshape(home_rows, blocks * HEAD_SIZE)

time: 172 us -> 165 us (0.959)
  the two profiles are of different devices: /device:TPU:17 before, /device:TPU:0 now
where the time goes in v4:
time: 165 us; the launch traced here: 164 us
  waiting for transfers between devices  73.5 us (45%)
  Pallas kernels  38 us (23%)
  starting transfers between devices  29.5 us (18%)
  between operations  17.6 us (11%)
  local copies, waits for them, and re-layouts  5.6 us (3%)
    ppermute x7, waiting for transfers between devices, swap(): return lax.ppermute(array, plane, [(i, i ^ k) for i in range(blocks)])  29.5 us
    all_to_all x1, waiting for transfers between devices, plane_device(): dq = lax.all_to_all(dq, plane, split_axis=0, concat_axis=0, tiled=True)  21.8 us
    pallas_call x2, Pallas kernels, attention(): pl.pallas_call(functools.partial(attention_kernel, first), out_shape=outs...  18.2 us
    ppermute x3, waiting for transfers between devices, lower(): return lax.ppermute(rows, 'outer', [(i + k, i) for i in range(planes - k)])  12.2 us
    pallas_call x4, Pallas kernels, pack_rows(): pl.pallas_call(functools.partial(pack_rows_kernel, partners), out_shape=j...  8.56 us
    ppermute x1, waiting for transfers between devices, plane_device(): up = [lax.ppermute(mine, 'outer', [(i, i + 1) for i in range(planes - 1)])]  6.37 us
    all_to_all x1, starting transfers between devices, plane_device(): lax.all_to_all(sent, plane, split_axis=0, concat_axis=0, tiled=True)  5.17 us
    ppermute x7, starting transfers between devices, swap(): return lax.ppermute(array, plane, [(i, i ^ k) for i in range(blocks)])  4.91 us
  transfers between devices with their start and end apart: 16, of which 11 were waited for; matrix products, arithmetic and copies ran while one was open for 2% of the time, Pallas kernels for 16%

profile of v4, /device:TPU:0, one launch (start us, length us, event | category | flops | bytes accessed | tf_op | source)
XLA Modules:
  0.0 164.2 jit_solution(9450159117610222103)
XLA Ops:
  7.2 0.8 copy.217.lse_ref
  8.0 4.7 %pack_pairs.1 = bf16[8,208,256]{2,1,0:T(8,128)(2,1)} custom-call(s32[1,192]{1,0:T(1,128)} %bitcast.283, bf16[192,40]{1,0:T(8,128)(2,1)S(1)} %copy.217.lse_ref, bf16[192,1024]{1,0:T(8,128)(2,1)} %k_ref.1, bf16[192,1024]{1,0:T(8,128)(2,1)} %v_ref.1, bf16[192,5120]{1,0:T(8,128)(2,1)} %rest_2_.3, bf16[192,5120]{1,0:T(8,128)(2,1)} %o_ref.1), custom_call_target="tpu_custom_call" | custom-call | tf_op jit(solution)/shard_map/pack_pairs/pallas_call | solution.py:256
  12.7 5.2 %all-to-all-start.20 = ((bf16[8,208,256]{2,1,0:T(8,128)(2,1)}), bf16[8,208,256]{2,1,0:T(8,128)(2,1)S(1)}, u32[]{:S(2)}, u32[]{:S(2)}) async-start(bf16[8,208,256]{2,1,0:T(8,128)(2,1)} %pack_pairs.1), calls=%async_computation.20 | async-start | bytes 1703936 | tf_op jit(solution)/shard_map/all_to_all | solution.py:788
  17.8 2.5 %pack_rows.4 = bf16[2,192,1280]{2,1,0:T(8,128)(2,1)} custom-call(s32[1]{0:T(128)} %bitcast.48.me_ref, bf16[192,5120]{1,0:T(8,128)(2,1)} %rest_1_.3, bf16[192,5120]{1,0:T(8,128)(2,1)} %rest_2_.3), custom_call_target="tpu_custom_call" | custom-call | tf_op jit(solution)/shard_map/pack_rows/pallas_call | solution.py:292
  20.3 0.0 copy-done.7
  20.3 1.8 %pack_rows.5 = bf16[1,192,1280]{2,1,0:T(8,128)(2,1)} custom-call(s32[1]{0:T(128)} %bitcast.48.me_ref, bf16[192,5120]{1,0:T(8,128)(2,1)} %rest_1_.3, bf16[192,5120]{1,0:T(8,128)(2,1)S(1)} %copy-done.7), custom_call_target="tpu_custom_call" | custom-call | tf_op jit(solution)/shard_map/pack_rows/pallas_call | solution.py:292
  22.1 0.6 collective-permute-start
  22.7 2.0 %pack_rows.6 = bf16[2,192,1280]{2,1,0:T(8,128)(2,1)} custom-call(s32[1]{0:T(128)} %bitcast.48.me_ref, bf16[192,5120]{1,0:T(8,128)(2,1)} %rest_1_.3, bf16[192,5120]{1,0:T(8,128)(2,1)S(1)} %copy-done.7), custom_call_target="tpu_custom_call" | custom-call | tf_op jit(solution)/shard_map/pack_rows/pallas_call | solution.py:292
  24.7 2.6 %collective-permute-start.4 = (bf16[2,192,1280]{2,1,0:T(8,128)(2,1)}, bf16[2,192,1280]{2,1,0:T(8,128)(2,1)S(1)}, u32[]{:S(2)}, u32[]{:S(2)}) collective-permute-start(bf16[2,192,1280]{2,1,0:T(8,128)(2,1)} %pack_rows.6), channel_id=1, source_target_pairs={{0,5},{1,4},{2,7},{3,6},{4,1},{5,0},{6,3},{7,2},{8,13},{9,12},{10,... | collective-permute-start | bytes 2949128 | tf_op jit(solution)/shard_map/ppermute | solution.py:782
  27.4 2.3 %pack_rows.7 = bf16[2,192,1280]{2,1,0:T(8,128)(2,1)} custom-call(s32[1]{0:T(128)} %bitcast.48.me_ref, bf16[192,5120]{1,0:T(8,128)(2,1)} %rest_1_.3, bf16[192,5120]{1,0:T(8,128)(2,1)} %rest_2_.3), custom_call_target="tpu_custom_call" | custom-call | tf_op jit(solution)/shard_map/pack_rows/pallas_call | solution.py:292
  29.7 0.6 collective-permute-start.5
  30.3 0.3 collective-permute-start.6
  30.6 0.0 collective-permute-done.rest_3_
  30.6 0.1 all-to-all-done.20.arrived
  30.8 1.1 compact.1
  31.9 3.5 %collective-permute-start.1 = (bf16[784,256]{1,0:T(8,128)(2,1)S(1)}, bf16[784,256]{1,0:T(8,128)(2,1)S(1)}, u32[]{:S(2)}, u32[]{:S(2)}) collective-permute-start(bf16[784,256]{1,0:T(8,128)(2,1)S(1)} %get-tuple-element.399.rest_11_), channel_id=1, source_target_pairs={{0,8},{8,16},{16,24},{1,9},{9,17},{17,25},{2,10},{10,18},{18,26},{... | collective-permute-start | bytes 1204232 | tf_op jit(solution)/shard_map/ppermute | solution.py:795
  35.4 3.3 %collective-permute-start.3 = (bf16[784,256]{1,0:T(8,128)(2,1)S(1)}, bf16[784,256]{1,0:T(8,128)(2,1)S(1)}, u32[]{:S(2)}, u32[]{:S(2)}) collective-permute-start(bf16[784,256]{1,0:T(8,128)(2,1)S(1)} %get-tuple-element.399.rest_11_), channel_id=1, source_target_pairs={{0,24},{1,25},{2,26},{3,27},{4,28},{5,29},{6,30},{7,31}} | collective-permute-start | bytes 1204232 | tf_op jit(solution)/shard_map/ppermute | solution.py:796
  38.7 6.4 %collective-permute-done.1.rest_10_ = bf16[784,256]{1,0:T(8,128)(2,1)S(1)} collective-permute-done((bf16[784,256]{1,0:T(8,128)(2,1)S(1)}, bf16[784,256]{1,0:T(8,128)(2,1)S(1)}, u32[]{:S(2)}, u32[]{:S(2)}) %collective-permute-start.1) | collective-permute-done | bytes 401440 | tf_op jit(solution)/shard_map/ppermute | solution.py:795
  45.1 0.7 collective-permute-start.2
  45.8 7.0 %collective-permute-done.4.rest_4_ = bf16[2,192,1280]{2,1,0:T(8,128)(2,1)S(1)} collective-permute-done((bf16[2,192,1280]{2,1,0:T(8,128)(2,1)}, bf16[2,192,1280]{2,1,0:T(8,128)(2,1)S(1)}, u32[]{:S(2)}, u32[]{:S(2)}) %collective-permute-start.4) | collective-permute-done | bytes 983072 | tf_op jit(solution)/shard_map/ppermute | solution.py:782
  52.8 19.7 %collective-permute-done.5.rest_5_ = bf16[2,192,1280]{2,1,0:T(8,128)(2,1)S(1)} collective-permute-done((bf16[2,192,1280]{2,1,0:T(8,128)(2,1)}, bf16[2,192,1280]{2,1,0:T(8,128)(2,1)S(1)}, u32[]{:S(2)}, u32[]{:S(2)}) %collective-permute-start.5) | collective-permute-done | bytes 983072 | tf_op jit(solution)/shard_map/ppermute | solution.py:782
  72.5 1.0 collective-permute-done.6.rest_6_
  73.4 0.0 collective-permute-done.3.rest_11_
  73.4 0.0 collective-permute-done.2.rest_10_
  73.5 0.1 collective-permute-start.7
  73.6 0.6 collective-permute-start.8
  74.1 1.1 slice.35
  75.2 0.1 collective-permute-start.9
  75.3 0.1 collective-permute-done.7.rest_7_
  75.4 0.7 collective-permute-done.8.rest_8_
  76.1 1.0 collective-permute-done.9.rest_9_
  77.1 0.0 copy-done.8
  77.1 4.5 %attention.2 = (bf16[784,256]{1,0:T(8,128)(2,1)S(1)}, bf16[784,256]{1,0:T(8,128)(2,1)S(1)}, f32[12,128,640]{2,1,0:T(8,128)}, s32[1]{0:T(128)}) custom-call(s32[1]{0:T(128)} %bitcast.48.me_ref, s32[8]{0:T(128)S(1)} %get-tuple-element.396.counts_ref, bf16[8,16,256]{2,1,0:T(8,128)(2,1)S(1)} %get-tuple-element.397.rest_0_, bf16[192,5120]{1,0:T(8,128)(2,1)} %rest_1_.3, ...), custom_call_target="tpu_custom_call" | custom-call | flops 5000000000 | bytes 12000000 | tf_op jit(solution)/shard_map/attention/pallas_call | solution.py:689
  81.6 0.0 copy-start
  81.6 1.3 collective-permute-start.11
  82.9 0.0 copy-done.10
  82.9 13.8 %attention.3 = (bf16[784,256]{1,0:T(8,128)(2,1)S(1)}, bf16[8,192,640]{2,1,0:T(8,128)(2,1)}, f32[768,256]{1,0:T(8,128)S(1)}, s32[1]{0:T(128)}) custom-call(s32[1]{0:T(128)} %bitcast.48.me_ref, s32[8]{0:T(128)S(1)} %get-tuple-element.396.counts_ref, bf16[8,16,256]{2,1,0:T(8,128)(2,1)S(1)} %get-tuple-element.397.rest_0_, bf16[192,5120]{1,0:T(8,128)(2,1)S(1)} %copy-done.10, ...), custom_call_target="tpu_custom_call" | custom-call | flops 5000000000 | bytes 12000000 | tf_op jit(solution)/shard_map/attention/pallas_call | solution.py:689
  96.7 0.0 copy-done
  96.7 0.0 copy-start.2
  96.7 0.7 copy-done.2
  97.5 12.2 %collective-permute-done.11.rest_1_ = bf16[784,256]{1,0:T(8,128)(2,1)S(1)} collective-permute-done((bf16[784,256]{1,0:T(8,128)(2,1)S(1)}, bf16[784,256]{1,0:T(8,128)(2,1)S(1)}, u32[]{:S(2)}, u32[]{:S(2)}) %collective-permute-start.11) | collective-permute-done | bytes 401440 | tf_op jit(solution)/shard_map/ppermute | solution.py:804
  109.7 4.5 %all-to-all-start.21 = ((bf16[8,192,640]{2,1,0:T(8,128)(2,1)}), bf16[8,192,640]{2,1,0:T(8,128)(2,1)}, u32[]{:S(2)}, u32[]{:S(2)}) async-start(bf16[8,192,640]{2,1,0:T(8,128)(2,1)} %get-tuple-element.414), calls=%async_computation.21 | async-start | bytes 3932160 | tf_op jit(solution)/shard_map/all_to_all | solution.py:811
  114.2 0.0 copy-done.1
  114.2 1.3 collective-permute-start.10
  115.5 0.0 copy-done.3
  115.5 1.3 collective-permute-start.12
  116.8 21.8 %all-to-all-done.21.parts = bf16[8,192,640]{2,1,0:T(8,128)(2,1)} async-done(((bf16[8,192,640]{2,1,0:T(8,128)(2,1)}), bf16[8,192,640]{2,1,0:T(8,128)(2,1)}, u32[]{:S(2)}, u32[]{:S(2)}) %all-to-all-start.21) | async-done | bytes 1966112 | tf_op jit(solution)/shard_map/all_to_all | solution.py:811
  138.5 0.0 collective-permute-done.10.rest_0_
  138.5 0.0 collective-permute-done.12.rest_2_
  138.5 2.3 %combine.1 = bf16[8,192,256]{2,1,0:T(8,128)(2,1)} custom-call(s32[8]{0:T(128)S(1)} %get-tuple-element.396.counts_ref, f32[768,256]{1,0:T(8,128)S(1)} %get-tuple-element.416.own, bf16[784,256]{1,0:T(8,128)(2,1)S(1)} %collective-permute-done.10.rest_0_, bf16[784,256]{1,0:T(8,128)(2,1)S(1)} %collective-permute-done.11.rest_1_, ...), custom_call_target="tpu_custom_call" | custom-call | tf_op jit(solution)/shard_map/combine/pallas_call | solution.py:760
  140.9 3.5 %all-to-all-start.22 = ((bf16[8,192,256]{2,1,0:T(8,128)(2,1)}), bf16[8,192,256]{2,1,0:T(8,128)(2,1)S(1)}, u32[]{:S(2)}, u32[]{:S(2)}) async-start(bf16[8,192,256]{2,1,0:T(8,128)(2,1)} %combine.1), calls=%async_computation.22 | async-start | bytes 1572864 | tf_op jit(solution)/shard_map/all_to_all | solution.py:814
  145.7 0.6 slice.37
  146.3 0.5 slice.49
  148.1 0.6 slice.50
  149.4 0.0 copy-start.9
  149.4 0.0 copy-start.14
  149.4 0.0 copy-start.15
  149.4 0.0 copy-start.19
  149.4 3.1 %unpack_rows.1 = bf16[192,5120]{1,0:T(8,128)(2,1)} custom-call(bf16[8,192,640]{2,1,0:T(8,128)(2,1)} %all-to-all-done.21.parts), custom_call_target="tpu_custom_call" | custom-call | tf_op jit(solution)/shard_map/unpack_rows/pallas_call | solution.py:727
  152.5 3.5 %all-to-all-done.22 = bf16[8,192,256]{2,1,0:T(8,128)(2,1)S(1)} async-done(((bf16[8,192,256]{2,1,0:T(8,128)(2,1)}), bf16[8,192,256]{2,1,0:T(8,128)(2,1)S(1)}, u32[]{:S(2)}, u32[]{:S(2)}) %all-to-all-start.22) | async-done | bytes 786464 | tf_op jit(solution)/shard_map/all_to_all | solution.py:814
  156.1 0.2 slice_bitcast_fusion
  156.3 0.0 copy-done.9
  156.3 1.0 conditional.1
  156.3 1.0 copy_bitcast_fusion
  (10 shorter events, 0.1 us)
Async XLA Ops:
  12.7 18.1 %all-to-all-start.20 = ((bf16[8,208,256]{2,1,0:T(8,128)(2,1)}), bf16[8,208,256]{2,1,0:T(8,128)(2,1)S(1)}, u32[]{:S(2)}, u32[]{:S(2)}) async-start(bf16[8,208,256]{2,1,0:T(8,128)(2,1)} %pack_pairs.1), calls=%async_computation.20 | async-start | bytes 1703936 | tf_op jit(solution)/shard_map/all_to_all | solution.py:788
  17.8 2.5 %copy-start.7 = (bf16[192,5120]{1,0:T(8,128)(2,1)S(1)}, bf16[192,5120]{1,0:T(8,128)(2,1)}, u32[]{:S(2)}) copy-start(bf16[192,5120]{1,0:T(8,128)(2,1)} %rest_2_.3) | copy-start | bytes 5898244
  22.1 8.5 %collective-permute-start = (bf16[1,192,1280]{2,1,0:T(8,128)(2,1)}, bf16[1,192,1280]{2,1,0:T(8,128)(2,1)}, u32[]{:S(2)}, u32[]{:S(2)}) collective-permute-start(bf16[1,192,1280]{2,1,0:T(8,128)(2,1)} %pack_rows.5), channel_id=1, source_target_pairs={{0,2},{1,3},{2,0},{3,1},{4,6},{5,7},{6,4},{7,5},{8,10},{9,11},{10,... | collective-permute-start | bytes 1474568 | tf_op jit(solution)/shard_map/ppermute | solution.py:782
  24.7 28.1 %collective-permute-start.4 = (bf16[2,192,1280]{2,1,0:T(8,128)(2,1)}, bf16[2,192,1280]{2,1,0:T(8,128)(2,1)S(1)}, u32[]{:S(2)}, u32[]{:S(2)}) collective-permute-start(bf16[2,192,1280]{2,1,0:T(8,128)(2,1)} %pack_rows.6), channel_id=1, source_target_pairs={{0,5},{1,4},{2,7},{3,6},{4,1},{5,0},{6,3},{7,2},{8,13},{9,12},{10,... | collective-permute-start | bytes 2949128 | tf_op jit(solution)/shard_map/ppermute | solution.py:782
  29.7 42.8 %collective-permute-start.5 = (bf16[2,192,1280]{2,1,0:T(8,128)(2,1)}, bf16[2,192,1280]{2,1,0:T(8,128)(2,1)S(1)}, u32[]{:S(2)}, u32[]{:S(2)}) collective-permute-start(bf16[2,192,1280]{2,1,0:T(8,128)(2,1)} %pack_rows.7), channel_id=1, source_target_pairs={{0,4},{1,5},{2,6},{3,7},{4,0},{5,1},{6,2},{7,3},{8,12},{9,13},{10,... | collective-permute-start | bytes 2949128 | tf_op jit(solution)/shard_map/ppermute | solution.py:782
  30.3 43.1 %collective-permute-start.6 = (bf16[2,192,1280]{2,1,0:T(8,128)(2,1)}, bf16[2,192,1280]{2,1,0:T(8,128)(2,1)}, u32[]{:S(2)}, u32[]{:S(2)}) collective-permute-start(bf16[2,192,1280]{2,1,0:T(8,128)(2,1)} %pack_rows.4), channel_id=1, source_target_pairs={{0,1},{1,0},{2,3},{3,2},{4,5},{5,4},{6,7},{7,6},{8,9},{9,8},{10,11... | collective-permute-start | bytes 2949128 | tf_op jit(solution)/shard_map/ppermute | solution.py:782
  30.8 46.4 %copy-start.8 = (bf16[192,5120]{1,0:T(8,128)(2,1)S(1)}, bf16[192,5120]{1,0:T(8,128)(2,1)}, u32[]{:S(2)}) copy-start(bf16[192,5120]{1,0:T(8,128)(2,1)} %rest_2_.3) | copy-start | bytes 5898244
  31.9 13.2 %collective-permute-start.1 = (bf16[784,256]{1,0:T(8,128)(2,1)S(1)}, bf16[784,256]{1,0:T(8,128)(2,1)S(1)}, u32[]{:S(2)}, u32[]{:S(2)}) collective-permute-start(bf16[784,256]{1,0:T(8,128)(2,1)S(1)} %get-tuple-element.399.rest_11_), channel_id=1, source_target_pairs={{0,8},{8,16},{16,24},{1,9},{9,17},{17,25},{2,10},{10,18},{18,26},{... | collective-permute-start | bytes 1204232 | tf_op jit(solution)/shard_map/ppermute | solution.py:795
  35.4 38.0 %collective-permute-start.3 = (bf16[784,256]{1,0:T(8,128)(2,1)S(1)}, bf16[784,256]{1,0:T(8,128)(2,1)S(1)}, u32[]{:S(2)}, u32[]{:S(2)}) collective-permute-start(bf16[784,256]{1,0:T(8,128)(2,1)S(1)} %get-tuple-element.399.rest_11_), channel_id=1, source_target_pairs={{0,24},{1,25},{2,26},{3,27},{4,28},{5,29},{6,30},{7,31}} | collective-permute-start | bytes 1204232 | tf_op jit(solution)/shard_map/ppermute | solution.py:796
  45.1 28.3 %collective-permute-start.2 = (bf16[784,256]{1,0:T(8,128)(2,1)S(1)}, bf16[784,256]{1,0:T(8,128)(2,1)S(1)}, u32[]{:S(2)}, u32[]{:S(2)}) collective-permute-start(bf16[784,256]{1,0:T(8,128)(2,1)S(1)} %collective-permute-done.1.rest_10_), channel_id=1, source_target_pairs={{8,16},{16,24},{9,17},{17,25},{10,18},{18,26},{11,19},{19,27},{12,... | collective-permute-start | bytes 1204232 | tf_op jit(solution)/shard_map/ppermute | solution.py:797
  73.5 1.9 %collective-permute-start.7 = (bf16[1,192,1280]{2,1,0:T(8,128)(2,1)S(1)}, bf16[1,192,1280]{2,1,0:T(8,128)(2,1)S(1)}, u32[]{:S(2)}, u32[]{:S(2)}) collective-permute-start(bf16[1,192,1280]{2,1,0:T(8,128)(2,1)S(1)} %slice.33), channel_id=1, source_target_pairs={{0,2},{1,3},{2,0},{3,1},{4,6},{5,7},{6,4},{7,5},{8,10},{9,11},{10,... | collective-permute-start | bytes 1474568 | tf_op jit(solution)/shard_map/ppermute | solution.py:782
  73.6 2.5 %collective-permute-start.8 = (bf16[1,192,1280]{2,1,0:T(8,128)(2,1)S(1)}, bf16[1,192,1280]{2,1,0:T(8,128)(2,1)S(1)}, u32[]{:S(2)}, u32[]{:S(2)}) collective-permute-start(bf16[1,192,1280]{2,1,0:T(8,128)(2,1)S(1)} %slice.34), channel_id=1, source_target_pairs={{0,2},{1,3},{2,0},{3,1},{4,6},{5,7},{6,4},{7,5},{8,10},{9,11},{10,... | collective-permute-start | bytes 1474568 | tf_op jit(solution)/shard_map/ppermute | solution.py:782
  75.2 1.9 %collective-permute-start.9 = (bf16[1,192,1280]{2,1,0:T(8,128)(2,1)S(1)}, bf16[1,192,1280]{2,1,0:T(8,128)(2,1)S(1)}, u32[]{:S(2)}, u32[]{:S(2)}) collective-permute-start(bf16[1,192,1280]{2,1,0:T(8,128)(2,1)S(1)} %slice.35), channel_id=1, source_target_pairs={{0,2},{1,3},{2,0},{3,1},{4,6},{5,7},{6,4},{7,5},{8,10},{9,11},{10,... | collective-permute-start | bytes 1474568 | tf_op jit(solution)/shard_map/ppermute | solution.py:782
  77.1 5.8 %copy-start.10 = (bf16[192,5120]{1,0:T(8,128)(2,1)S(1)}, bf16[192,5120]{1,0:T(8,128)(2,1)}, u32[]{:S(2)}) copy-start(bf16[192,5120]{1,0:T(8,128)(2,1)} %rest_1_.3) | copy-start | bytes 5898244
  81.6 15.1 %copy-start = (bf16[784,256]{1,0:T(8,128)(2,1)}, bf16[784,256]{1,0:T(8,128)(2,1)S(1)}, u32[]{:S(2)}) copy-start(bf16[784,256]{1,0:T(8,128)(2,1)S(1)} %get-tuple-element.409) | copy-start | bytes 1204228
  81.6 28.1 %collective-permute-start.11 = (bf16[784,256]{1,0:T(8,128)(2,1)S(1)}, bf16[784,256]{1,0:T(8,128)(2,1)S(1)}, u32[]{:S(2)}, u32[]{:S(2)}) collective-permute-start(bf16[784,256]{1,0:T(8,128)(2,1)S(1)} %get-tuple-element.411), channel_id=1, source_target_pairs={{16,0},{24,8},{17,1},{25,9},{18,2},{26,10},{19,3},{27,11},{20,4},{... | collective-permute-start | bytes 1204232 | tf_op jit(solution)/shard_map/ppermute | solution.py:804
  96.7 0.7 copy-start.2
  109.7 4.5 %copy-start.1 = (bf16[784,256]{1,0:T(8,128)(2,1)S(1)}, bf16[784,256]{1,0:T(8,128)(2,1)}, u32[]{:S(2)}) copy-start(bf16[784,256]{1,0:T(8,128)(2,1)} %copy-done) | copy-start | bytes 1204228
  109.7 5.8 %copy-start.3 = (bf16[784,256]{1,0:T(8,128)(2,1)S(1)}, bf16[784,256]{1,0:T(8,128)(2,1)}, u32[]{:S(2)}) copy-start(bf16[784,256]{1,0:T(8,128)(2,1)} %copy-done.2) | copy-start | bytes 1204228
  109.7 28.9 %all-to-all-start.21 = ((bf16[8,192,640]{2,1,0:T(8,128)(2,1)}), bf16[8,192,640]{2,1,0:T(8,128)(2,1)}, u32[]{:S(2)}, u32[]{:S(2)}) async-start(bf16[8,192,640]{2,1,0:T(8,128)(2,1)} %get-tuple-element.414), calls=%async_computation.21 | async-start | bytes 3932160 | tf_op jit(solution)/shard_map/all_to_all | solution.py:811
  114.2 24.4 %collective-permute-start.10 = (bf16[784,256]{1,0:T(8,128)(2,1)S(1)}, bf16[784,256]{1,0:T(8,128)(2,1)S(1)}, u32[]{:S(2)}, u32[]{:S(2)}) collective-permute-start(bf16[784,256]{1,0:T(8,128)(2,1)S(1)} %copy-done.1), channel_id=1, source_target_pairs={{24,0},{25,1},{26,2},{27,3},{28,4},{29,5},{30,6},{31,7}} | collective-permute-start | bytes 1204232 | tf_op jit(solution)/shard_map/ppermute | solution.py:804
  115.5 23.1 %collective-permute-start.12 = (bf16[784,256]{1,0:T(8,128)(2,1)S(1)}, bf16[784,256]{1,0:T(8,128)(2,1)S(1)}, u32[]{:S(2)}, u32[]{:S(2)}) collective-permute-start(bf16[784,256]{1,0:T(8,128)(2,1)S(1)} %copy-done.3), channel_id=1, source_target_pairs={{8,0},{16,8},{24,16},{9,1},{17,9},{25,17},{10,2},{18,10},{26,18},{... | collective-permute-start | bytes 1204232 | tf_op jit(solution)/shard_map/ppermute | solution.py:804
  140.9 15.2 %all-to-all-start.22 = ((bf16[8,192,256]{2,1,0:T(8,128)(2,1)}), bf16[8,192,256]{2,1,0:T(8,128)(2,1)S(1)}, u32[]{:S(2)}, u32[]{:S(2)}) async-start(bf16[8,192,256]{2,1,0:T(8,128)(2,1)} %combine.1), calls=%async_computation.22 | async-start | bytes 1572864 | tf_op jit(solution)/shard_map/all_to_all | solution.py:814
  149.4 6.9 %copy-start.9 = (bf16[192,5120]{1,0:T(8,128)(2,1)S(1)}, bf16[192,5120]{1,0:T(8,128)(2,1)}, u32[]{:S(2)}) copy-start(bf16[192,5120]{1,0:T(8,128)(2,1)} %rest_2_.3) | copy-start | bytes 5898244
  149.4 6.9 %copy-start.14 = (bf16[192,1024]{1,0:T(8,128)(2,1)S(1)}, bf16[192,1024]{1,0:T(8,128)(2,1)}, u32[]{:S(2)}) copy-start(bf16[192,1024]{1,0:T(8,128)(2,1)} %k_ref.1) | copy-start | bytes 1179652
  149.4 6.9 %copy-start.15 = (bf16[192,1024]{1,0:T(8,128)(2,1)S(1)}, bf16[192,1024]{1,0:T(8,128)(2,1)}, u32[]{:S(2)}) copy-start(bf16[192,1024]{1,0:T(8,128)(2,1)} %v_ref.1) | copy-start | bytes 1179652
  149.4 6.9 %copy-start.19 = (s32[192]{0:T(256)S(1)}, s32[192]{0:T(256)}, u32[]{:S(2)}) copy-start(s32[192]{0:T(256)} %param.21) | copy-start | bytes 2308

commit v5 on v4

--- a/solution.py
+++ b/solution.py
@@ -213,7 +213,6 @@
 ROW_TILE = 128
 INFO_ROWS = 16
 AUX_LANES = 256
-COUNT_ROW = 5
 DELTA_ROW = 8
 SMEM = pl.BlockSpec(memory_space=pltpu.SMEM)
 VMEM = pl.BlockSpec(memory_space=pltpu.VMEM)
@@ -226,80 +225,82 @@
 PASS_ROWS = (256, 512, 768)
 
 
-def pack_pairs_kernel(limit, ranks_ref, lse_ref, k_ref, v_ref, do_ref, o_ref, out_ref, columns, lanes):
+def pack_pairs_kernel(limit, ranks_ref, k_ref, v_ref, out_ref):
     home_rows = k_ref.shape[0]
-    columns[...] = jnp.zeros_like(columns)
-    for g in range(KEY_VALUE_HEADS):
-        columns[:, 16 * g : 16 * g + GROUP] = lse_ref[:, g * GROUP : (g + 1) * GROUP].astype(
-            jnp.float32
-        )
-    for h in range(QUERY_HEADS):
-        head = slice(h * HEAD_SIZE, (h + 1) * HEAD_SIZE)
-        product = do_ref[:, head].astype(jnp.float32) * o_ref[:, head].astype(jnp.float32)
-        column = 16 * (h // GROUP) + DELTA_ROW + h % GROUP
-        columns[:, column : column + 1] = jnp.sum(product, axis=1, keepdims=True)
-    lanes[...] = jnp.zeros_like(lanes)
-    lanes[:, :home_rows] = columns[...].T
     live = jnp.where(ranks_ref[...] < limit, 1.0, 0.0)
-    count = jnp.sum(live, axis=1, keepdims=True)
-    line = lax.broadcasted_iota(jnp.int32, (INFO_ROWS, 2 * HEAD_SIZE), 0)
+    info = jnp.broadcast_to(
+        jnp.sum(live, axis=1, keepdims=True), (INFO_ROWS, 2 * HEAD_SIZE)
+    ).astype(out_ref.dtype)
     for g in range(KEY_VALUE_HEADS):
         head = slice(g * HEAD_SIZE, (g + 1) * HEAD_SIZE)
         out_ref[g, :home_rows, :HEAD_SIZE] = k_ref[:, head]
         out_ref[g, :home_rows, HEAD_SIZE:] = v_ref[:, head]
-        info = jnp.where(line == COUNT_ROW, count, lanes[16 * g : 16 * g + INFO_ROWS, :])
-        out_ref[g, home_rows:, :] = info.astype(out_ref.dtype)
-
-
-def pack_pairs(limit, ranks, lse, keys, values, output_gradient, outputs):
+        out_ref[g, home_rows:, :] = info
+
+
+def pack_pairs(limit, ranks, keys, values):
     home_rows = keys.shape[0]
     return pl.pallas_call(
         functools.partial(pack_pairs_kernel, limit),
         out_shape=jax.ShapeDtypeStruct(
             (KEY_VALUE_HEADS, home_rows + INFO_ROWS, 2 * HEAD_SIZE), keys.dtype
         ),
-        in_specs=[VMEM] * 6,
+        in_specs=[VMEM] * 3,
         out_specs=VMEM,
+        name="pack_pairs",
+    )(ranks.reshape(1, home_rows), keys, values)
+
+
+def pack_rows_kernel(me_ref, lse_ref, q_ref, do_ref, o_ref, *rest):
+    outs, small_ref, columns, lanes = rest[:4], rest[4], rest[5], rest[6]
+    home_rows = q_ref.shape[0]
+    me = me_ref[0]
+    columns[...] = jnp.zeros_like(columns)
+    for h in range(QUERY_HEADS):
+        head = slice(h * HEAD_SIZE, (h + 1) * HEAD_SIZE)
+        product = do_ref[:, head].astype(jnp.float32) * o_ref[:, head].astype(jnp.float32)
+        column = INFO_ROWS * (h // GROUP) + DELTA_ROW + h % GROUP
+        columns[:, column : column + 1] = jnp.sum(product, axis=1, keepdims=True)
+    lanes[...] = jnp.zeros_like(lanes)
+    lanes[:, :home_rows] = columns[...].T
+    lse = lse_ref[...].astype(jnp.float32)
+    for g in range(KEY_VALUE_HEADS):
+        lanes[INFO_ROWS * g : INFO_ROWS * g + GROUP, :home_rows] = lse[g * GROUP : (g + 1) * GROUP]
+
+    def small(to):
+        rows = pl.ds(pl.multiple_of(to * INFO_ROWS, INFO_ROWS), INFO_ROWS)
+        return lanes[rows, :].astype(jnp.bfloat16)
+
+    small_ref[...] = small(me)
+    for out, partners in zip(outs, [(chip, chip ^ CORE) for chip in CHIPS] + [(CORE,)]):
+        for n, partner in enumerate(partners):
+            to = me ^ partner
+            start = pl.multiple_of(to * WIDTH, HEAD_SIZE)
+            out[n, :home_rows, :WIDTH] = q_ref[:, pl.ds(start, WIDTH)]
+            out[n, :home_rows, WIDTH:] = do_ref[:, pl.ds(start, WIDTH)]
+            out[n, home_rows:, :AUX_LANES] = small(to)
+
+
+def pack_rows(me, lse, queries, output_gradient, outputs):
+    home_rows = queries.shape[0]
+    bf16, f32 = jnp.bfloat16, jnp.float32
+    pair = jax.ShapeDtypeStruct((2, home_rows + INFO_ROWS, 2 * WIDTH), bf16)
+    beside = jax.ShapeDtypeStruct((1, home_rows + INFO_ROWS, 2 * WIDTH), bf16)
+    return pl.pallas_call(
+        pack_rows_kernel,
+        out_shape=(pair, pair, pair, beside, jax.ShapeDtypeStruct((INFO_ROWS, AUX_LANES), bf16)),
+        in_specs=[SMEM] + [VMEM] * 4,
+        out_specs=[VMEM] * 5,
         scratch_shapes=[
-            pltpu.VMEM((home_rows, HEAD_SIZE), jnp.float32),
-            pltpu.VMEM((HEAD_SIZE, AUX_LANES), jnp.float32),
+            pltpu.VMEM((home_rows, HEAD_SIZE), f32),
+            pltpu.VMEM((HEAD_SIZE, AUX_LANES), f32),
         ],
         compiler_params=pltpu.CompilerParams(vmem_limit_bytes=32 * 1024 * 1024),
-        name="pack_pairs",
-    )(ranks.reshape(1, home_rows), lse, keys, values, output_gradient, outputs)
-
-
-def pack_rows_kernel(partners, me_ref, q_hbm, do_hbm, out, sems):
-    copies = []
-    for n, partner in enumerate(partners):
-        start = pl.multiple_of((me_ref[0] ^ partner) * WIDTH, HEAD_SIZE)
-        for m, source in enumerate((q_hbm, do_hbm)):
-            copies.append(
-                pltpu.make_async_copy(
-                    source.at[:, pl.ds(start, WIDTH)],
-                    out.at[n, :, pl.ds(m * WIDTH, WIDTH)],
-                    sems.at[2 * n + m],
-                )
-            )
-    for copy in copies:
-        copy.start()
-    for copy in copies:
-        copy.wait()
-
-
-def pack_rows(partners, me, queries, output_gradient):
-    home_rows = queries.shape[0]
-    return pl.pallas_call(
-        functools.partial(pack_rows_kernel, partners),
-        out_shape=jax.ShapeDtypeStruct((len(partners), home_rows, 2 * WIDTH), queries.dtype),
-        in_specs=[SMEM, HBM, HBM],
-        out_specs=VMEM,
-        scratch_shapes=[pltpu.SemaphoreType.DMA((2 * len(partners),))],
         name="pack_rows",
-    )(me, queries, output_gradient)
-
-
-def compact_kernel(arrived, out, small, counts_ref):
+    )(me, lse.T, queries, output_gradient, outputs)
+
+
+def compact_kernel(arrived, out, counts_ref):
     home_rows = arrived.shape[1] - INFO_ROWS
     capacity = out.shape[0] - INFO_ROWS
     row = lax.broadcasted_iota(jnp.int32, (capacity, home_rows), 0)
@@ -307,9 +308,8 @@
     total = jnp.int32(0)
     picked = []
     for block in range(KEY_VALUE_HEADS):
-        info = arrived[block, home_rows:, :]
-        small[block] = info
-        count = jnp.max(info[COUNT_ROW : COUNT_ROW + 1].astype(jnp.float32)).astype(jnp.int32)
+        info = arrived[block, home_rows:, :].astype(jnp.float32)
+        count = jnp.max(info[0:8]).astype(jnp.int32)
         counts_ref[block] = count
         hit = (row == within + total) & (within < count)
         picked.append(jnp.where(hit, 1.0, 0.0).astype(jnp.bfloat16))
@@ -335,30 +335,34 @@
         compact_kernel,
         out_shape=(
             jax.ShapeDtypeStruct((capacity + INFO_ROWS, columns), arrived.dtype),
-            jax.ShapeDtypeStruct((blocks, INFO_ROWS, columns), arrived.dtype),
             jax.ShapeDtypeStruct((blocks,), jnp.int32),
         ),
         in_specs=[VMEM],
-        out_specs=(VMEM, VMEM, SMEM),
+        out_specs=(VMEM, SMEM),
         compiler_params=pltpu.CompilerParams(vmem_limit_bytes=32 * 1024 * 1024),
         name="compact",
     )(arrived)
 
 
-def load_rows(me, counts_ref, arrays, q_s, do_s, sems):
+def load_rows(me, counts_ref, arrays, q_s, do_s, aux_s, sems):
     home_rows = q_s.shape[0] // KEY_VALUE_HEADS
-    q_hbm, do_hbm, beside, pairs, crossed = arrays
-    column = pl.multiple_of(me * WIDTH, HEAD_SIZE)
-    left, right = pl.ds(0, WIDTH), pl.ds(WIDTH, WIDTH)
-    sources = [
-        (0, q_hbm.at[:, pl.ds(column, WIDTH)], do_hbm.at[:, pl.ds(column, WIDTH)]),
-        (CORE, beside.at[0, :, left], beside.at[0, :, right]),
-    ]
+    q_hbm, do_hbm, small, beside, pairs, crossed = arrays
+    column = pl.ds(pl.multiple_of(me * WIDTH, HEAD_SIZE), WIDTH)
+
+    def parts(partner, payload):
+        rows = pl.ds(0, home_rows)
+        return (
+            partner,
+            payload.at[0, rows, pl.ds(0, WIDTH)],
+            payload.at[0, rows, pl.ds(WIDTH, WIDTH)],
+            payload.at[0, pl.ds(home_rows, INFO_ROWS), pl.ds(0, AUX_LANES)],
+        )
+
+    sources = [(0, q_hbm.at[:, column], do_hbm.at[:, column], small), parts(CORE, beside)]
     for chip, pair, cross in zip(CHIPS, pairs, crossed):
-        sources.append((chip, pair.at[0, :, left], pair.at[0, :, right]))
-        sources.append((chip ^ CORE, cross.at[0, :, left], cross.at[0, :, right]))
+        sources += [parts(chip, pair), parts(chip ^ CORE, cross)]
     plans = []
-    for n, (partner, q, do) in enumerate(sources):
+    for n, (partner, q, do, lanes) in enumerate(sources):
         source = me ^ partner
         rows = pl.ds(pl.multiple_of(source * home_rows, 64), home_rows)
         shard = counts_ref[source & ~1] + counts_ref[source | 1]
@@ -367,8 +371,9 @@
             (
                 needed,
                 [
-                    pltpu.make_async_copy(q, q_s.at[rows, :], sems.at[2 * n]),
-                    pltpu.make_async_copy(do, do_s.at[rows, :], sems.at[2 * n + 1]),
+                    pltpu.make_async_copy(q, q_s.at[rows, :], sems.at[3 * n]),
+                    pltpu.make_async_copy(do, do_s.at[rows, :], sems.at[3 * n + 1]),
+                    pltpu.make_async_copy(lanes, aux_s.at[source], sems.at[3 * n + 2]),
                 ],
             )
         )
@@ -444,22 +449,22 @@
 
 
 def attention_kernel(first, me_ref, counts_ref, *rest):
-    aux_s, arrays, kvs, rest = rest[0], rest[1:10], rest[10:12], rest[12:]
-    arrays = (*arrays[:3], arrays[3:6], arrays[6:9])
+    arrays, kvs, rest = rest[:10], rest[10:12], rest[12:]
+    arrays = (*arrays[:4], arrays[4:7], arrays[7:10])
     if first:
         far, downs, dqt_out, full_ref, rest = 2, rest[:2], rest[2], rest[3], rest[4:]
     else:
         dqt_in, far, downs, rest = rest[0], 1, rest[1:2], rest[2:]
         dq_out, own_out, full_ref, rest = rest[0], rest[1], rest[2], rest[3:]
     (
-        q_s, do_s, lse_s, delta_s, dqt, kv_s, acc_k, acc_v, tiles, starts, limits, sems, kv_sem,
-        down_sem, dqt_sem, down_s,
-    ) = rest[:16]
+        q_s, do_s, aux_s, lse_s, delta_s, dqt, kv_s, acc_k, acc_v, tiles, starts, limits, sems,
+        kv_sem, down_sem, dqt_sem, down_s,
+    ) = rest[:17]
     if not first:
-        out_sem, dq_s, own = rest[16:]
+        out_sem, dq_s, own, before = rest[17:]
     capacity = downs[0].shape[0] - INFO_ROWS
     scale = HEAD_SIZE ** (-0.5)
-    each = load_rows(me_ref[0], counts_ref, arrays, q_s, do_s, sems)
+    each = load_rows(me_ref[0], counts_ref, arrays, q_s, do_s, aux_s, sems)
     each(lambda copy: copy.start())
     kv_copies = [
         pltpu.make_async_copy(source, kv_s.at[n], kv_sem.at[n])
@@ -476,20 +481,17 @@
 
         lax.fori_loop(0, length, step, 0)
 
-    if first:
-
-        def zero_tile(n, tile):
-            dqt[tile] = jnp.zeros(dqt.shape[1:], jnp.float32)
-
-        each_tile(zero_tile)
-    else:
+    def zero_tile(n, tile):
+        dqt[tile] = jnp.zeros(dqt.shape[1:], jnp.float32)
+
+    each_tile(zero_tile)
+    if not first:
 
         def load(n, tile):
-            return pltpu.make_async_copy(dqt_in.at[tile], dqt.at[tile], dqt_sem.at[n])
+            return pltpu.make_async_copy(dqt_in.at[tile], before.at[tile], dqt_sem.at[n])
 
         each_tile(lambda n, tile: load(n, tile).start())
         own[...] = jnp.zeros_like(own)
-    spread_lanes(aux_s, lse_s, delta_s)
     for copy in kv_copies:
         copy.wait()
     most = total
@@ -504,8 +506,7 @@
             (INFO_ROWS, 2 * HEAD_SIZE), jnp.where(most > capacity, 1.0, 0.0)
         ).astype(jnp.bfloat16)
     each(lambda copy: copy.wait())
-    if not first:
-        each_tile(lambda n, tile: load(n, tile).wait())
+    spread_lanes(aux_s, lse_s, delta_s)
     lane = lax.broadcasted_iota(jnp.int32, (1, WIDTH), 1) % ROW_TILE
 
     def block_step(step, carry):
@@ -619,6 +620,7 @@
     lax.fori_loop(0, (limit + KEY_TILE - 1) // KEY_TILE, key_step, 0)
     own_copy = pltpu.make_async_copy(own, own_out, down_sem.at[1])
     own_copy.start()
+    each_tile(lambda n, tile: load(n, tile).wait())
 
     half = ROW_TILE // 2
     copies = []
@@ -637,7 +639,8 @@
             def _():
                 for h in range(GROUP):
                     columns = slice(h * HEAD_SIZE, (h + 1) * HEAD_SIZE)
-                    part = (dqt[SHARD_TILES * shard + t, :, columns] * scale).T
+                    tile = SHARD_TILES * shard + t
+                    part = ((dqt[tile, :, columns] + before[tile, :, columns]) * scale).T
                     dq_s[block, rows, columns] = part[first : first + size].astype(jnp.bfloat16)
 
             @pl.when(jnp.logical_not(live))
@@ -663,7 +666,7 @@
     ]
 
 
-def attention(first, me, counts, small, arrays, kvs, *before):
+def attention(first, me, counts, arrays, kvs, *before):
     bf16, f32 = jnp.bfloat16, jnp.float32
     blocks = KEY_VALUE_HEADS
     rows = kvs[0].shape[0]
@@ -685,15 +688,17 @@
             pltpu.SemaphoreType.DMA((blocks,)),
             pltpu.VMEM(dq, bf16),
             pltpu.VMEM((capacity, columns), f32),
+            pltpu.VMEM(dqt, f32),
         ]
     return pl.pallas_call(
         functools.partial(attention_kernel, first),
         out_shape=outs,
-        in_specs=[SMEM] * 2 + [VMEM] + [HBM] * (11 + len(before)),
+        in_specs=[SMEM] * 2 + [HBM] * (12 + len(before)),
         out_specs=[HBM] * 3 + [SMEM],
         scratch_shapes=[
             pltpu.VMEM((plane_rows, WIDTH), bf16),
             pltpu.VMEM((plane_rows, WIDTH), bf16),
+            pltpu.VMEM((blocks, INFO_ROWS, AUX_LANES), bf16),
             pltpu.VMEM((tile_count, WIDTH), f32),
             pltpu.VMEM((tile_count, WIDTH), f32),
             pltpu.VMEM(dqt, f32),
@@ -703,7 +708,7 @@
             pltpu.SMEM((tile_count + 1,), jnp.int32),
             pltpu.SMEM((blocks,), jnp.int32),
             pltpu.SMEM((2,), jnp.int32),
-            pltpu.SemaphoreType.DMA((2 * blocks,)),
+            pltpu.SemaphoreType.DMA((3 * blocks,)),
             pltpu.SemaphoreType.DMA((2,)),
             pltpu.SemaphoreType.DMA((2,)),
             pltpu.SemaphoreType.DMA((tile_count,)),
@@ -715,7 +720,7 @@
             flops=5_000_000_000, bytes_accessed=12_000_000, transcendentals=4_000_000
         ),
         name="attention",
-    )(me, counts, small, *arrays, *kvs, *before)
+    )(me, counts, *arrays, *kvs, *before)
 
 
 def unpack_rows_kernel(parts, out):
@@ -781,39 +786,35 @@
     def swap(array, k):
         return lax.ppermute(array, plane, [(i, i ^ k) for i in range(blocks)])
 
-    sent = pack_pairs(
-        surviving_tokens, ranks, lse, keys, values, output_gradient, outputs
-    )
+    sent = pack_pairs(surviving_tokens, ranks, keys, values)
     me, sent = lax.optimization_barrier((me, sent))
     arrived = lax.all_to_all(sent, plane, split_axis=0, concat_axis=0, tiled=True)
-    packed = [pack_rows((chip, chip ^ CORE), me, queries, output_gradient) for chip in CHIPS]
-    me, packed[-1] = lax.optimization_barrier((me, packed[-1]))
+    *packed, beside, small = pack_rows(me, lse, queries, output_gradient, outputs)
     pairs = [swap(rows, chip) for rows, chip in zip(packed, CHIPS)]
-    beside = swap(pack_rows((CORE,), me, queries, output_gradient), CORE)
+    beside = swap(beside, CORE)
     arrived, beside = lax.optimization_barrier((arrived, beside))
-    mine, small, counts = compact(arrived)
+    mine, counts = compact(arrived)
     up = [lax.ppermute(mine, "outer", [(i, i + 1) for i in range(planes - 1)])]
     last = lax.ppermute(mine, "outer", [(0, planes - 1)])
     up.append(lax.ppermute(up[0], "outer", [(i, i + 1) for i in range(1, planes - 1)]))
     up.append(last)
     up[1], up[2], *pairs = lax.optimization_barrier((up[1], up[2], *pairs))
     crossed = [swap(pair[1:], CORE) for pair in pairs]
-    arrays = [queries, output_gradient, beside, *pairs, *crossed]
+    arrays = [queries, output_gradient, small, beside, *pairs, *crossed]
 
     def lower(rows, k):
         return lax.ppermute(rows, "outer", [(i + k, i) for i in range(planes - k)])
 
-    down2, down3, dqt, full1 = attention(True, me, counts, small, arrays, [up[1], up[2]])
+    down2, down3, dqt, full1 = attention(True, me, counts, arrays, [up[1], up[2]])
     back2 = lower(down2, 2)
-    down1, dq, own, full2 = attention(False, me, counts, small, arrays, [up[0], mine], dqt)
+    down1, dq, own, full2 = attention(False, me, counts, arrays, [up[0], mine], dqt)
     dq, back2 = lax.optimization_barrier((dq, back2))
     backs = [lower(down3, 3), back2, lower(down1, 1)]
     dq = lax.all_to_all(dq, plane, split_axis=0, concat_axis=0, tiled=True)
-    dq, own = lax.optimization_barrier((dq, own))
+    spread = combine(counts, own, backs, home_rows)
+    dq, spread = lax.optimization_barrier((dq, spread))
     dq_home = unpack_rows(dq)
-    kv_home = lax.all_to_all(
-        combine(counts, own, backs, home_rows), plane, split_axis=0, concat_axis=0, tiled=True
-    )
+    kv_home = lax.all_to_all(spread, plane, split_axis=0, concat_axis=0, tiled=True)
     full = (full1[0] + full2[0]) > 0
     for back in backs:
         full = full | (back[capacity, 0] > 0)

time: 165 us -> 164 us (level)
  the two profiles are of different devices: /device:TPU:0 before, /device:TPU:17 now
where the time goes in v5:
time: 164 us; the launch traced here: 166 us
  waiting for transfers between devices  70.7 us (43%)
  starting transfers between devices  37.3 us (23%)
  Pallas kernels  36.5 us (22%)
  between operations  17.2 us (10%)
  local copies, waits for them, and re-layouts  4.67 us (3%)
    ppermute x7, waiting for transfers between devices, swap(): return lax.ppermute(array, plane, [(i, i ^ k) for i in range(blocks)])  29.8 us
    ppermute x3, waiting for transfers between devices, lower(): return lax.ppermute(rows, 'outer', [(i + k, i) for i in range(planes - k)])  25.8 us
    pallas_call x2, Pallas kernels, attention(): pl.pallas_call(functools.partial(attention_kernel, first), out_shape=outs...  22.1 us
    ppermute x3, starting transfers between devices, lower(): return lax.ppermute(rows, 'outer', [(i + k, i) for i in range(planes - k)])  12 us
    ppermute x1, waiting for transfers between devices, plane_device(): up = [lax.ppermute(mine, 'outer', [(i, i + 1) for i in range(planes - 1)])]  8.48 us
    pallas_call x1, Pallas kernels, pack_rows(): pl.pallas_call(pack_rows_kernel, out_shape=(pair, pair, pair, beside, jax...  5.65 us
    all_to_all x1, starting transfers between devices, plane_device(): dq = lax.all_to_all(dq, plane, split_axis=0, concat_axis=0, tiled=True)  4.75 us
    all_to_all x1, starting transfers between devices, plane_device(): lax.all_to_all(spread, plane, split_axis=0, concat_axis=0, tiled=True)  4.58 us
  transfers between devices with their start and end apart: 16, of which 8 were waited for; matrix products, arithmetic and copies ran while one was open for 2% of the time, Pallas kernels for 15%

profile of v5, /device:TPU:17, one launch (start us, length us, event | category | flops | bytes accessed | tf_op | source)
XLA Modules:
  0.0 166.4 jit_solution(10143195407227185875)
XLA Ops:
  7.2 0.0 copy-start.18
  7.2 2.2 %pack_pairs.1 = bf16[8,208,256]{2,1,0:T(8,128)(2,1)} custom-call(s32[1,192]{1,0:T(1,128)} %bitcast.287, bf16[192,1024]{1,0:T(8,128)(2,1)} %k_ref.1, bf16[192,1024]{1,0:T(8,128)(2,1)} %v_ref.1), custom_call_target="tpu_custom_call" | custom-call | tf_op jit(solution)/shard_map/pack_pairs/pallas_call | solution.py:243
  9.4 4.4 %all-to-all-start.20 = ((bf16[8,208,256]{2,1,0:T(8,128)(2,1)}), bf16[8,208,256]{2,1,0:T(8,128)(2,1)S(1)}, u32[]{:S(2)}, u32[]{:S(2)}) async-start(bf16[8,208,256]{2,1,0:T(8,128)(2,1)} %pack_pairs.1), calls=%async_computation.20 | async-start | bytes 1703936 | tf_op jit(solution)/shard_map/all_to_all | solution.py:791
  13.8 0.0 copy-done.18
  13.8 5.7 %pack_rows.1 = (bf16[2,208,1280]{2,1,0:T(8,128)(2,1)}, bf16[2,208,1280]{2,1,0:T(8,128)(2,1)}, bf16[2,208,1280]{2,1,0:T(8,128)(2,1)}, bf16[1,208,1280]{2,1,0:T(8,128)(2,1)S(1)}, bf16[16,256]{1,0:T(8,128)(2,1)S(1)}) custom-call(s32[1]{0:T(128)} %bitcast.48.me_ref, bf16[40,192]{1,0:T(8,128)(2,1)S(1)} %bitcast.285, bf16[192,5120]{1,0:T(8,128)(2,1)} %rest_0_.3, ...), custom_call_target="tpu_custom_call" | custom-call | tf_op jit(solution)/shard_map/pack_rows/pallas_call | solution.py:289
  19.4 0.0 collective-permute-start
  19.4 2.6 %collective-permute-start.4 = (bf16[2,208,1280]{2,1,0:T(8,128)(2,1)}, bf16[2,208,1280]{2,1,0:T(8,128)(2,1)S(1)}, u32[]{:S(2)}, u32[]{:S(2)}) collective-permute-start(bf16[2,208,1280]{2,1,0:T(8,128)(2,1)} %get-tuple-element.402), channel_id=1, source_target_pairs={{0,5},{1,4},{2,7},{3,6},{4,1},{5,0},{6,3},{7,2},{8,13},{9,12},{10,... | collective-permute-start | bytes 3194888 | tf_op jit(solution)/shard_map/ppermute | solution.py:787
  22.1 0.3 collective-permute-start.5
  22.4 0.0 collective-permute-start.6
  22.4 0.0 collective-permute-done.rest_3_
  22.4 0.8 copy-done.1
  23.2 3.0 %all-to-all-done.20.arrived = bf16[8,208,256]{2,1,0:T(8,128)(2,1)S(1)} async-done(((bf16[8,208,256]{2,1,0:T(8,128)(2,1)}), bf16[8,208,256]{2,1,0:T(8,128)(2,1)S(1)}, u32[]{:S(2)}, u32[]{:S(2)}) %all-to-all-start.20) | async-done | bytes 852000 | tf_op jit(solution)/shard_map/all_to_all | solution.py:791
  26.1 1.1 compact.1
  27.3 3.2 %collective-permute-start.1 = (bf16[784,256]{1,0:T(8,128)(2,1)S(1)}, bf16[784,256]{1,0:T(8,128)(2,1)S(1)}, u32[]{:S(2)}, u32[]{:S(2)}) collective-permute-start(bf16[784,256]{1,0:T(8,128)(2,1)S(1)} %get-tuple-element.401.rest_11_), channel_id=1, source_target_pairs={{0,8},{8,16},{16,24},{1,9},{9,17},{17,25},{2,10},{10,18},{18,26},{... | collective-permute-start | bytes 1204232 | tf_op jit(solution)/shard_map/ppermute | solution.py:797
  30.5 0.7 collective-permute-start.3
  31.2 8.5 %collective-permute-done.1.rest_10_ = bf16[784,256]{1,0:T(8,128)(2,1)S(1)} collective-permute-done((bf16[784,256]{1,0:T(8,128)(2,1)S(1)}, bf16[784,256]{1,0:T(8,128)(2,1)S(1)}, u32[]{:S(2)}, u32[]{:S(2)}) %collective-permute-start.1) | collective-permute-done | bytes 401440 | tf_op jit(solution)/shard_map/ppermute | solution.py:797
  39.6 3.3 %collective-permute-start.2 = (bf16[784,256]{1,0:T(8,128)(2,1)S(1)}, bf16[784,256]{1,0:T(8,128)(2,1)S(1)}, u32[]{:S(2)}, u32[]{:S(2)}) collective-permute-start(bf16[784,256]{1,0:T(8,128)(2,1)S(1)} %collective-permute-done.1.rest_10_), channel_id=1, source_target_pairs={{8,16},{16,24},{9,17},{17,25},{10,18},{18,26},{11,19},{19,27},{12,... | collective-permute-start | bytes 1204232 | tf_op jit(solution)/shard_map/ppermute | solution.py:799
  42.9 6.2 %collective-permute-done.4.rest_4_ = bf16[2,208,1280]{2,1,0:T(8,128)(2,1)S(1)} collective-permute-done((bf16[2,208,1280]{2,1,0:T(8,128)(2,1)}, bf16[2,208,1280]{2,1,0:T(8,128)(2,1)S(1)}, u32[]{:S(2)}, u32[]{:S(2)}) %collective-permute-start.4) | collective-permute-done | bytes 1064992 | tf_op jit(solution)/shard_map/ppermute | solution.py:787
  49.1 22.0 %collective-permute-done.5.rest_5_ = bf16[2,208,1280]{2,1,0:T(8,128)(2,1)S(1)} collective-permute-done((bf16[2,208,1280]{2,1,0:T(8,128)(2,1)}, bf16[2,208,1280]{2,1,0:T(8,128)(2,1)S(1)}, u32[]{:S(2)}, u32[]{:S(2)}) %collective-permute-start.5) | collective-permute-done | bytes 1064992 | tf_op jit(solution)/shard_map/ppermute | solution.py:787
  71.1 0.0 collective-permute-done.6.rest_6_
  71.1 0.0 collective-permute-done.3.rest_11_
  71.2 0.0 collective-permute-done.2.rest_10_
  71.2 0.8 collective-permute-start.7
  72.1 0.1 collective-permute-start.8
  72.2 1.1 slice.35
  73.2 0.6 collective-permute-start.9
  73.8 0.0 collective-permute-done.7.rest_7_
  73.8 0.5 collective-permute-done.8.rest_8_
  74.4 1.0 collective-permute-done.9.rest_9_
  75.4 0.0 copy-done.2
  75.4 0.0 copy-done.12
  75.4 8.7 %attention.2 = (bf16[784,256]{1,0:T(8,128)(2,1)S(1)}, bf16[784,256]{1,0:T(8,128)(2,1)S(1)}, f32[12,128,640]{2,1,0:T(8,128)}, s32[1]{0:T(128)}) custom-call(s32[1]{0:T(128)} %bitcast.48.me_ref, s32[8]{0:T(128)S(1)} %get-tuple-element.398.counts_ref, bf16[192,5120]{1,0:T(8,128)(2,1)S(1)} %copy-done.12, bf16[192,5120]{1,0:T(8,128)(2,1)} %rest_1_.3, ...), custom_call_target="tpu_custom_call" | custom-call | flops 5000000000 | bytes 12000000 | tf_op jit(solution)/shard_map/attention/pallas_call | solution.py:693
  84.1 0.0 copy-done
  84.1 0.0 copy-start.3
  84.1 1.3 collective-permute-start.11
  85.4 0.0 copy-done.14
  85.4 13.4 %attention.3 = (bf16[784,256]{1,0:T(8,128)(2,1)S(1)}, bf16[8,192,640]{2,1,0:T(8,128)(2,1)}, f32[768,256]{1,0:T(8,128)S(1)}, s32[1]{0:T(128)}) custom-call(s32[1]{0:T(128)} %bitcast.48.me_ref, s32[8]{0:T(128)S(1)} %get-tuple-element.398.counts_ref, bf16[192,5120]{1,0:T(8,128)(2,1)S(1)} %copy-done.12, bf16[192,5120]{1,0:T(8,128)(2,1)S(1)} %copy-done.14, ...), custom_call_target="tpu_custom_call" | custom-call | flops 5000000000 | bytes 12000000 | tf_op jit(solution)/shard_map/attention/pallas_call | solution.py:693
  98.8 0.0 copy-done.3
  98.8 0.0 collective-permute-done.11.rest_1_
  98.8 0.0 copy-start.4
  98.8 4.7 %all-to-all-start.21 = ((bf16[8,192,640]{2,1,0:T(8,128)(2,1)}), bf16[8,192,640]{2,1,0:T(8,128)(2,1)}, u32[]{:S(2)}, u32[]{:S(2)}) async-start(bf16[8,192,640]{2,1,0:T(8,128)(2,1)} %get-tuple-element.418), calls=%async_computation.21 | async-start | bytes 3932160 | tf_op jit(solution)/shard_map/all_to_all | solution.py:813
  103.6 0.0 copy-done.4
  103.6 0.7 collective-permute-start.10
  104.3 10.0 %collective-permute-start.12 = (bf16[784,256]{1,0:T(8,128)(2,1)S(1)}, bf16[784,256]{1,0:T(8,128)(2,1)S(1)}, u32[]{:S(2)}, u32[]{:S(2)}) collective-permute-start(bf16[784,256]{1,0:T(8,128)(2,1)S(1)} %get-tuple-element.417), channel_id=1, source_target_pairs={{8,0},{16,8},{24,16},{9,1},{17,9},{25,17},{10,2},{18,10},{26,18},{... | collective-permute-start | bytes 1204232 | tf_op jit(solution)/shard_map/ppermute | solution.py:806
  114.3 0.0 collective-permute-done.10.rest_0_
  114.3 25.8 %collective-permute-done.12.rest_2_ = bf16[784,256]{1,0:T(8,128)(2,1)S(1)} collective-permute-done((bf16[784,256]{1,0:T(8,128)(2,1)S(1)}, bf16[784,256]{1,0:T(8,128)(2,1)S(1)}, u32[]{:S(2)}, u32[]{:S(2)}) %collective-permute-start.12) | collective-permute-done | bytes 401440 | tf_op jit(solution)/shard_map/ppermute | solution.py:806
  140.1 2.3 %combine.1 = bf16[8,192,256]{2,1,0:T(8,128)(2,1)} custom-call(s32[8]{0:T(128)S(1)} %get-tuple-element.398.counts_ref, f32[768,256]{1,0:T(8,128)S(1)} %get-tuple-element.419.own, bf16[784,256]{1,0:T(8,128)(2,1)S(1)} %collective-permute-done.10.rest_0_, bf16[784,256]{1,0:T(8,128)(2,1)S(1)} %collective-permute-done.11.rest_1_, ...), custom_call_target="tpu_custom_call" | custom-call | tf_op jit(solution)/shard_map/combine/pallas_call | solution.py:765
  142.4 0.0 all-to-all-done.21.parts
  142.4 4.6 %all-to-all-start.22 = ((bf16[8,192,256]{2,1,0:T(8,128)(2,1)}), bf16[8,192,256]{2,1,0:T(8,128)(2,1)S(1)}, u32[]{:S(2)}, u32[]{:S(2)}) async-start(bf16[8,192,256]{2,1,0:T(8,128)(2,1)} %combine.1), calls=%async_computation.22 | async-start | bytes 1572864 | tf_op jit(solution)/shard_map/all_to_all | solution.py:817
  148.2 0.5 slice.37
  148.7 0.5 slice.49
  150.4 0.5 slice.50
  151.5 0.0 copy-start.13
  151.5 0.0 copy-start.15
  151.5 0.0 copy-start.16
  151.5 0.0 copy-start.21
  151.5 3.1 %unpack_rows.1 = bf16[192,5120]{1,0:T(8,128)(2,1)} custom-call(bf16[8,192,640]{2,1,0:T(8,128)(2,1)} %all-to-all-done.21.parts), custom_call_target="tpu_custom_call" | custom-call | tf_op jit(solution)/shard_map/unpack_rows/pallas_call | solution.py:732
  154.6 3.6 %all-to-all-done.22 = bf16[8,192,256]{2,1,0:T(8,128)(2,1)S(1)} async-done(((bf16[8,192,256]{2,1,0:T(8,128)(2,1)}), bf16[8,192,256]{2,1,0:T(8,128)(2,1)S(1)}, u32[]{:S(2)}, u32[]{:S(2)}) %all-to-all-start.22) | async-done | bytes 786464 | tf_op jit(solution)/shard_map/all_to_all | solution.py:817
  158.3 0.2 slice_bitcast_fusion
  158.5 0.0 copy-done.13
  158.5 0.0 copy-done.15
  158.5 0.0 copy-done.16
  158.5 1.0 conditional.1
  158.5 1.0 copy_bitcast_fusion
  (8 shorter events, 0.1 us)
Async XLA Ops:
  7.2 6.6 %copy-start.18 = (bf16[192,40]{0,1:T(8,128)(2,1)S(1)}, bf16[192,40]{0,1:T(8,128)(2,1)}, u32[]{:S(2)}) copy-start(bf16[192,40]{0,1:T(8,128)(2,1)} %param.20) | copy-start | bytes 46084
  9.4 16.7 %all-to-all-start.20 = ((bf16[8,208,256]{2,1,0:T(8,128)(2,1)}), bf16[8,208,256]{2,1,0:T(8,128)(2,1)S(1)}, u32[]{:S(2)}, u32[]{:S(2)}) async-start(bf16[8,208,256]{2,1,0:T(8,128)(2,1)} %pack_pairs.1), calls=%async_computation.20 | async-start | bytes 1703936 | tf_op jit(solution)/shard_map/all_to_all | solution.py:791
  19.4 2.9 %collective-permute-start = (bf16[1,208,1280]{2,1,0:T(8,128)(2,1)S(1)}, bf16[1,208,1280]{2,1,0:T(8,128)(2,1)S(1)}, u32[]{:S(2)}, u32[]{:S(2)}) collective-permute-start(bf16[1,208,1280]{2,1,0:T(8,128)(2,1)S(1)} %get-tuple-element.396), channel_id=1, source_target_pairs={{0,2},{1,3},{2,0},{3,1},{4,6},{5,7},{6,4},{7,5},{8,10},{9,11},{10,... | collective-permute-start | bytes 1597448 | tf_op jit(solution)/shard_map/ppermute | solution.py:787
  19.4 29.7 %collective-permute-start.4 = (bf16[2,208,1280]{2,1,0:T(8,128)(2,1)}, bf16[2,208,1280]{2,1,0:T(8,128)(2,1)S(1)}, u32[]{:S(2)}, u32[]{:S(2)}) collective-permute-start(bf16[2,208,1280]{2,1,0:T(8,128)(2,1)} %get-tuple-element.402), channel_id=1, source_target_pairs={{0,5},{1,4},{2,7},{3,6},{4,1},{5,0},{6,3},{7,2},{8,13},{9,12},{10,... | collective-permute-start | bytes 3194888 | tf_op jit(solution)/shard_map/ppermute | solution.py:787
  22.1 49.1 %collective-permute-start.5 = (bf16[2,208,1280]{2,1,0:T(8,128)(2,1)}, bf16[2,208,1280]{2,1,0:T(8,128)(2,1)S(1)}, u32[]{:S(2)}, u32[]{:S(2)}) collective-permute-start(bf16[2,208,1280]{2,1,0:T(8,128)(2,1)} %get-tuple-element.403), channel_id=1, source_target_pairs={{0,4},{1,5},{2,6},{3,7},{4,0},{5,1},{6,2},{7,3},{8,12},{9,13},{10,... | collective-permute-start | bytes 3194888 | tf_op jit(solution)/shard_map/ppermute | solution.py:787
  22.4 48.8 %collective-permute-start.6 = (bf16[2,208,1280]{2,1,0:T(8,128)(2,1)}, bf16[2,208,1280]{2,1,0:T(8,128)(2,1)}, u32[]{:S(2)}, u32[]{:S(2)}) collective-permute-start(bf16[2,208,1280]{2,1,0:T(8,128)(2,1)} %get-tuple-element.404), channel_id=1, source_target_pairs={{0,1},{1,0},{2,3},{3,2},{4,5},{5,4},{6,7},{7,6},{8,9},{9,8},{10,11... | collective-permute-start | bytes 3194888 | tf_op jit(solution)/shard_map/ppermute | solution.py:787
  22.4 0.8 copy-start.1
  26.1 49.2 %copy-start.2 = (bf16[1,208,1280]{2,1,0:T(8,128)(2,1)S(1)}, bf16[1,208,1280]{2,1,0:T(8,128)(2,1)}, u32[]{:S(2)}) copy-start(bf16[1,208,1280]{2,1,0:T(8,128)(2,1)} %copy-done.1) | copy-start | bytes 1597444
  26.1 49.2 %copy-start.12 = (bf16[192,5120]{1,0:T(8,128)(2,1)S(1)}, bf16[192,5120]{1,0:T(8,128)(2,1)}, u32[]{:S(2)}) copy-start(bf16[192,5120]{1,0:T(8,128)(2,1)} %rest_0_.3) | copy-start | bytes 5898244
  27.3 12.4 %collective-permute-start.1 = (bf16[784,256]{1,0:T(8,128)(2,1)S(1)}, bf16[784,256]{1,0:T(8,128)(2,1)S(1)}, u32[]{:S(2)}, u32[]{:S(2)}) collective-permute-start(bf16[784,256]{1,0:T(8,128)(2,1)S(1)} %get-tuple-element.401.rest_11_), channel_id=1, source_target_pairs={{0,8},{8,16},{16,24},{1,9},{9,17},{17,25},{2,10},{10,18},{18,26},{... | collective-permute-start | bytes 1204232 | tf_op jit(solution)/shard_map/ppermute | solution.py:797
  30.5 40.7 %collective-permute-start.3 = (bf16[784,256]{1,0:T(8,128)(2,1)S(1)}, bf16[784,256]{1,0:T(8,128)(2,1)S(1)}, u32[]{:S(2)}, u32[]{:S(2)}) collective-permute-start(bf16[784,256]{1,0:T(8,128)(2,1)S(1)} %get-tuple-element.401.rest_11_), channel_id=1, source_target_pairs={{0,24},{1,25},{2,26},{3,27},{4,28},{5,29},{6,30},{7,31}} | collective-permute-start | bytes 1204232 | tf_op jit(solution)/shard_map/ppermute | solution.py:798
  39.6 31.5 %collective-permute-start.2 = (bf16[784,256]{1,0:T(8,128)(2,1)S(1)}, bf16[784,256]{1,0:T(8,128)(2,1)S(1)}, u32[]{:S(2)}, u32[]{:S(2)}) collective-permute-start(bf16[784,256]{1,0:T(8,128)(2,1)S(1)} %collective-permute-done.1.rest_10_), channel_id=1, source_target_pairs={{8,16},{16,24},{9,17},{17,25},{10,18},{18,26},{11,19},{19,27},{12,... | collective-permute-start | bytes 1204232 | tf_op jit(solution)/shard_map/ppermute | solution.py:799
  71.1 12.9 %copy-start = (bf16[2,208,1280]{2,1,0:T(8,128)(2,1)}, bf16[2,208,1280]{2,1,0:T(8,128)(2,1)S(1)}, u32[]{:S(2)}) copy-start(bf16[2,208,1280]{2,1,0:T(8,128)(2,1)S(1)} %collective-permute-done.5.rest_5_) | copy-start | bytes 3194884
  71.2 2.6 %collective-permute-start.7 = (bf16[1,208,1280]{2,1,0:T(8,128)(2,1)S(1)}, bf16[1,208,1280]{2,1,0:T(8,128)(2,1)S(1)}, u32[]{:S(2)}, u32[]{:S(2)}) collective-permute-start(bf16[1,208,1280]{2,1,0:T(8,128)(2,1)S(1)} %slice.33), channel_id=1, source_target_pairs={{0,2},{1,3},{2,0},{3,1},{4,6},{5,7},{6,4},{7,5},{8,10},{9,11},{10,... | collective-permute-start | bytes 1597448 | tf_op jit(solution)/shard_map/ppermute | solution.py:787
  72.1 2.3 %collective-permute-start.8 = (bf16[1,208,1280]{2,1,0:T(8,128)(2,1)S(1)}, bf16[1,208,1280]{2,1,0:T(8,128)(2,1)S(1)}, u32[]{:S(2)}, u32[]{:S(2)}) collective-permute-start(bf16[1,208,1280]{2,1,0:T(8,128)(2,1)S(1)} %slice.34), channel_id=1, source_target_pairs={{0,2},{1,3},{2,0},{3,1},{4,6},{5,7},{6,4},{7,5},{8,10},{9,11},{10,... | collective-permute-start | bytes 1597448 | tf_op jit(solution)/shard_map/ppermute | solution.py:787
  73.2 2.1 %collective-permute-start.9 = (bf16[1,208,1280]{2,1,0:T(8,128)(2,1)S(1)}, bf16[1,208,1280]{2,1,0:T(8,128)(2,1)S(1)}, u32[]{:S(2)}, u32[]{:S(2)}) collective-permute-start(bf16[1,208,1280]{2,1,0:T(8,128)(2,1)S(1)} %slice.35), channel_id=1, source_target_pairs={{0,2},{1,3},{2,0},{3,1},{4,6},{5,7},{6,4},{7,5},{8,10},{9,11},{10,... | collective-permute-start | bytes 1597448 | tf_op jit(solution)/shard_map/ppermute | solution.py:787
  75.4 10.1 %copy-start.14 = (bf16[192,5120]{1,0:T(8,128)(2,1)S(1)}, bf16[192,5120]{1,0:T(8,128)(2,1)}, u32[]{:S(2)}) copy-start(bf16[192,5120]{1,0:T(8,128)(2,1)} %rest_1_.3) | copy-start | bytes 5898244
  84.1 14.7 %copy-start.3 = (bf16[784,256]{1,0:T(8,128)(2,1)}, bf16[784,256]{1,0:T(8,128)(2,1)S(1)}, u32[]{:S(2)}) copy-start(bf16[784,256]{1,0:T(8,128)(2,1)S(1)} %get-tuple-element.413) | copy-start | bytes 1204228
  84.1 14.7 %collective-permute-start.11 = (bf16[784,256]{1,0:T(8,128)(2,1)S(1)}, bf16[784,256]{1,0:T(8,128)(2,1)S(1)}, u32[]{:S(2)}, u32[]{:S(2)}) collective-permute-start(bf16[784,256]{1,0:T(8,128)(2,1)S(1)} %get-tuple-element.415), channel_id=1, source_target_pairs={{16,0},{24,8},{17,1},{25,9},{18,2},{26,10},{19,3},{27,11},{20,4},{... | collective-permute-start | bytes 1204232 | tf_op jit(solution)/shard_map/ppermute | solution.py:806
  98.8 4.8 %copy-start.4 = (bf16[784,256]{1,0:T(8,128)(2,1)S(1)}, bf16[784,256]{1,0:T(8,128)(2,1)}, u32[]{:S(2)}) copy-start(bf16[784,256]{1,0:T(8,128)(2,1)} %copy-done.3) | copy-start | bytes 1204228
  98.8 43.6 %all-to-all-start.21 = ((bf16[8,192,640]{2,1,0:T(8,128)(2,1)}), bf16[8,192,640]{2,1,0:T(8,128)(2,1)}, u32[]{:S(2)}, u32[]{:S(2)}) async-start(bf16[8,192,640]{2,1,0:T(8,128)(2,1)} %get-tuple-element.418), calls=%async_computation.21 | async-start | bytes 3932160 | tf_op jit(solution)/shard_map/all_to_all | solution.py:813
  103.6 10.7 %collective-permute-start.10 = (bf16[784,256]{1,0:T(8,128)(2,1)S(1)}, bf16[784,256]{1,0:T(8,128)(2,1)S(1)}, u32[]{:S(2)}, u32[]{:S(2)}) collective-permute-start(bf16[784,256]{1,0:T(8,128)(2,1)S(1)} %copy-done.4), channel_id=1, source_target_pairs={{24,0},{25,1},{26,2},{27,3},{28,4},{29,5},{30,6},{31,7}} | collective-permute-start | bytes 1204232 | tf_op jit(solution)/shard_map/ppermute | solution.py:806
  104.3 35.8 %collective-permute-start.12 = (bf16[784,256]{1,0:T(8,128)(2,1)S(1)}, bf16[784,256]{1,0:T(8,128)(2,1)S(1)}, u32[]{:S(2)}, u32[]{:S(2)}) collective-permute-start(bf16[784,256]{1,0:T(8,128)(2,1)S(1)} %get-tuple-element.417), channel_id=1, source_target_pairs={{8,0},{16,8},{24,16},{9,1},{17,9},{25,17},{10,2},{18,10},{26,18},{... | collective-permute-start | bytes 1204232 | tf_op jit(solution)/shard_map/ppermute | solution.py:806
  142.4 15.8 %all-to-all-start.22 = ((bf16[8,192,256]{2,1,0:T(8,128)(2,1)}), bf16[8,192,256]{2,1,0:T(8,128)(2,1)S(1)}, u32[]{:S(2)}, u32[]{:S(2)}) async-start(bf16[8,192,256]{2,1,0:T(8,128)(2,1)} %combine.1), calls=%async_computation.22 | async-start | bytes 1572864 | tf_op jit(solution)/shard_map/all_to_all | solution.py:817
  151.5 7.0 %copy-start.13 = (bf16[192,5120]{1,0:T(8,128)(2,1)S(1)}, bf16[192,5120]{1,0:T(8,128)(2,1)}, u32[]{:S(2)}) copy-start(bf16[192,5120]{1,0:T(8,128)(2,1)} %rest_0_.3) | copy-start | bytes 5898244
  151.5 7.0 %copy-start.15 = (bf16[192,1024]{1,0:T(8,128)(2,1)S(1)}, bf16[192,1024]{1,0:T(8,128)(2,1)}, u32[]{:S(2)}) copy-start(bf16[192,1024]{1,0:T(8,128)(2,1)} %k_ref.1) | copy-start | bytes 1179652
  151.5 7.0 %copy-start.16 = (bf16[192,1024]{1,0:T(8,128)(2,1)S(1)}, bf16[192,1024]{1,0:T(8,128)(2,1)}, u32[]{:S(2)}) copy-start(bf16[192,1024]{1,0:T(8,128)(2,1)} %v_ref.1) | copy-start | bytes 1179652
  151.5 7.0 %copy-start.21 = (s32[192]{0:T(256)S(1)}, s32[192]{0:T(256)}, u32[]{:S(2)}) copy-start(s32[192]{0:T(256)} %param.21) | copy-start | bytes 2308

commit v6 on v4

--- a/solution.py
+++ b/solution.py
@@ -213,7 +213,6 @@
 ROW_TILE = 128
 INFO_ROWS = 16
 AUX_LANES = 256
-COUNT_ROW = 5
 DELTA_ROW = 8
 SMEM = pl.BlockSpec(memory_space=pltpu.SMEM)
 VMEM = pl.BlockSpec(memory_space=pltpu.VMEM)
@@ -226,29 +225,26 @@
 PASS_ROWS = (256, 512, 768)
 
 
-def pack_pairs_kernel(limit, ranks_ref, lse_ref, k_ref, v_ref, do_ref, o_ref, out_ref, columns, lanes):
+def pack_pairs_kernel(limit, ranks_ref, lse_ref, k_ref, v_ref, do_ref, o_ref, out_ref, columns):
     home_rows = k_ref.shape[0]
     columns[...] = jnp.zeros_like(columns)
-    for g in range(KEY_VALUE_HEADS):
-        columns[:, 16 * g : 16 * g + GROUP] = lse_ref[:, g * GROUP : (g + 1) * GROUP].astype(
-            jnp.float32
-        )
     for h in range(QUERY_HEADS):
         head = slice(h * HEAD_SIZE, (h + 1) * HEAD_SIZE)
         product = do_ref[:, head].astype(jnp.float32) * o_ref[:, head].astype(jnp.float32)
-        column = 16 * (h // GROUP) + DELTA_ROW + h % GROUP
+        column = 8 * (h // GROUP) + h % GROUP
         columns[:, column : column + 1] = jnp.sum(product, axis=1, keepdims=True)
-    lanes[...] = jnp.zeros_like(lanes)
-    lanes[:, :home_rows] = columns[...].T
+    delta = columns[...].T
+    lse = lse_ref[...].astype(jnp.float32)
     live = jnp.where(ranks_ref[...] < limit, 1.0, 0.0)
-    count = jnp.sum(live, axis=1, keepdims=True)
-    line = lax.broadcasted_iota(jnp.int32, (INFO_ROWS, 2 * HEAD_SIZE), 0)
+    count = jnp.broadcast_to(jnp.sum(live, axis=1, keepdims=True), (8 - GROUP, home_rows))
     for g in range(KEY_VALUE_HEADS):
         head = slice(g * HEAD_SIZE, (g + 1) * HEAD_SIZE)
         out_ref[g, :home_rows, :HEAD_SIZE] = k_ref[:, head]
         out_ref[g, :home_rows, HEAD_SIZE:] = v_ref[:, head]
-        info = jnp.where(line == COUNT_ROW, count, lanes[16 * g : 16 * g + INFO_ROWS, :])
-        out_ref[g, home_rows:, :] = info.astype(out_ref.dtype)
+        info = jnp.concatenate(
+            [lse[g * GROUP : (g + 1) * GROUP], count, delta[8 * g : 8 * g + 8]], axis=0
+        )
+        out_ref[g, home_rows:, :home_rows] = info.astype(out_ref.dtype)
 
 
 def pack_pairs(limit, ranks, lse, keys, values, output_gradient, outputs):
@@ -260,41 +256,31 @@
         ),
         in_specs=[VMEM] * 6,
         out_specs=VMEM,
-        scratch_shapes=[
-            pltpu.VMEM((home_rows, HEAD_SIZE), jnp.float32),
-            pltpu.VMEM((HEAD_SIZE, AUX_LANES), jnp.float32),
-        ],
+        scratch_shapes=[pltpu.VMEM((home_rows, HEAD_SIZE), jnp.float32)],
         compiler_params=pltpu.CompilerParams(vmem_limit_bytes=32 * 1024 * 1024),
         name="pack_pairs",
-    )(ranks.reshape(1, home_rows), lse, keys, values, output_gradient, outputs)
-
-
-def pack_rows_kernel(partners, me_ref, q_hbm, do_hbm, out, sems):
-    copies = []
-    for n, partner in enumerate(partners):
-        start = pl.multiple_of((me_ref[0] ^ partner) * WIDTH, HEAD_SIZE)
-        for m, source in enumerate((q_hbm, do_hbm)):
-            copies.append(
-                pltpu.make_async_copy(
-                    source.at[:, pl.ds(start, WIDTH)],
-                    out.at[n, :, pl.ds(m * WIDTH, WIDTH)],
-                    sems.at[2 * n + m],
-                )
-            )
-    for copy in copies:
-        copy.start()
-    for copy in copies:
-        copy.wait()
-
-
-def pack_rows(partners, me, queries, output_gradient):
+    )(ranks.reshape(1, home_rows), lse.T, keys, values, output_gradient, outputs)
+
+
+def pack_rows_kernel(me_ref, q_ref, do_ref, *outs):
+    me = me_ref[0]
+    for out, partners in zip(outs, [(chip, chip ^ CORE) for chip in CHIPS] + [(CORE,)]):
+        for n, partner in enumerate(partners):
+            start = pl.multiple_of((me ^ partner) * WIDTH, HEAD_SIZE)
+            out[n, :, :WIDTH] = q_ref[:, pl.ds(start, WIDTH)]
+            out[n, :, WIDTH:] = do_ref[:, pl.ds(start, WIDTH)]
+
+
+def pack_rows(me, queries, output_gradient):
     home_rows = queries.shape[0]
+    pair = jax.ShapeDtypeStruct((2, home_rows, 2 * WIDTH), queries.dtype)
+    beside = jax.ShapeDtypeStruct((1, home_rows, 2 * WIDTH), queries.dtype)
     return pl.pallas_call(
-        functools.partial(pack_rows_kernel, partners),
-        out_shape=jax.ShapeDtypeStruct((len(partners), home_rows, 2 * WIDTH), queries.dtype),
-        in_specs=[SMEM, HBM, HBM],
-        out_specs=VMEM,
-        scratch_shapes=[pltpu.SemaphoreType.DMA((2 * len(partners),))],
+        pack_rows_kernel,
+        out_shape=(pair, pair, pair, beside),
+        in_specs=[SMEM] + [VMEM] * 2,
+        out_specs=[VMEM] * 4,
+        compiler_params=pltpu.CompilerParams(vmem_limit_bytes=32 * 1024 * 1024),
         name="pack_rows",
     )(me, queries, output_gradient)
 
@@ -309,7 +295,7 @@
     for block in range(KEY_VALUE_HEADS):
         info = arrived[block, home_rows:, :]
         small[block] = info
-        count = jnp.max(info[COUNT_ROW : COUNT_ROW + 1].astype(jnp.float32)).astype(jnp.int32)
+        count = jnp.max(info.astype(jnp.float32)[GROUP : GROUP + 1, :home_rows]).astype(jnp.int32)
         counts_ref[block] = count
         hit = (row == within + total) & (within < count)
         picked.append(jnp.where(hit, 1.0, 0.0).astype(jnp.bfloat16))
@@ -348,10 +334,10 @@
 def load_rows(me, counts_ref, arrays, q_s, do_s, sems):
     home_rows = q_s.shape[0] // KEY_VALUE_HEADS
     q_hbm, do_hbm, beside, pairs, crossed = arrays
-    column = pl.multiple_of(me * WIDTH, HEAD_SIZE)
+    column = pl.ds(pl.multiple_of(me * WIDTH, HEAD_SIZE), WIDTH)
     left, right = pl.ds(0, WIDTH), pl.ds(WIDTH, WIDTH)
     sources = [
-        (0, q_hbm.at[:, pl.ds(column, WIDTH)], do_hbm.at[:, pl.ds(column, WIDTH)]),
+        (0, q_hbm.at[:, column], do_hbm.at[:, column]),
         (CORE, beside.at[0, :, left], beside.at[0, :, right]),
     ]
     for chip, pair, cross in zip(CHIPS, pairs, crossed):
@@ -452,11 +438,11 @@
         dqt_in, far, downs, rest = rest[0], 1, rest[1:2], rest[2:]
         dq_out, own_out, full_ref, rest = rest[0], rest[1], rest[2], rest[3:]
     (
-        q_s, do_s, lse_s, delta_s, dqt, kv_s, acc_k, acc_v, tiles, starts, limits, sems, kv_sem,
-        down_sem, dqt_sem, down_s,
+        q_s, do_s, lse_s, delta_s, dqt, kv_s, acc_k, acc_v, tiles, starts, limits, sems,
+        kv_sem, down_sem, dqt_sem, down_s,
     ) = rest[:16]
     if not first:
-        out_sem, dq_s, own = rest[16:]
+        out_sem, dq_s, own, before = rest[16:]
     capacity = downs[0].shape[0] - INFO_ROWS
     scale = HEAD_SIZE ** (-0.5)
     each = load_rows(me_ref[0], counts_ref, arrays, q_s, do_s, sems)
@@ -476,20 +462,18 @@
 
         lax.fori_loop(0, length, step, 0)
 
-    if first:
-
-        def zero_tile(n, tile):
-            dqt[tile] = jnp.zeros(dqt.shape[1:], jnp.float32)
-
-        each_tile(zero_tile)
-    else:
+    def zero_tile(n, tile):
+        dqt[tile] = jnp.zeros(dqt.shape[1:], jnp.float32)
+
+    each_tile(zero_tile)
+    spread_lanes(aux_s, lse_s, delta_s)
+    if not first:
 
         def load(n, tile):
-            return pltpu.make_async_copy(dqt_in.at[tile], dqt.at[tile], dqt_sem.at[n])
+            return pltpu.make_async_copy(dqt_in.at[tile], before.at[tile], dqt_sem.at[n])
 
         each_tile(lambda n, tile: load(n, tile).start())
         own[...] = jnp.zeros_like(own)
-    spread_lanes(aux_s, lse_s, delta_s)
     for copy in kv_copies:
         copy.wait()
     most = total
@@ -504,8 +488,6 @@
             (INFO_ROWS, 2 * HEAD_SIZE), jnp.where(most > capacity, 1.0, 0.0)
         ).astype(jnp.bfloat16)
     each(lambda copy: copy.wait())
-    if not first:
-        each_tile(lambda n, tile: load(n, tile).wait())
     lane = lax.broadcasted_iota(jnp.int32, (1, WIDTH), 1) % ROW_TILE
 
     def block_step(step, carry):
@@ -619,6 +601,7 @@
     lax.fori_loop(0, (limit + KEY_TILE - 1) // KEY_TILE, key_step, 0)
     own_copy = pltpu.make_async_copy(own, own_out, down_sem.at[1])
     own_copy.start()
+    each_tile(lambda n, tile: load(n, tile).wait())
 
     half = ROW_TILE // 2
     copies = []
@@ -637,7 +620,8 @@
             def _():
                 for h in range(GROUP):
                     columns = slice(h * HEAD_SIZE, (h + 1) * HEAD_SIZE)
-                    part = (dqt[SHARD_TILES * shard + t, :, columns] * scale).T
+                    tile = SHARD_TILES * shard + t
+                    part = ((dqt[tile, :, columns] + before[tile, :, columns]) * scale).T
                     dq_s[block, rows, columns] = part[first : first + size].astype(jnp.bfloat16)
 
             @pl.when(jnp.logical_not(live))
@@ -685,6 +669,7 @@
             pltpu.SemaphoreType.DMA((blocks,)),
             pltpu.VMEM(dq, bf16),
             pltpu.VMEM((capacity, columns), f32),
+            pltpu.VMEM(dqt, f32),
         ]
     return pl.pallas_call(
         functools.partial(attention_kernel, first),
@@ -786,10 +771,9 @@
     )
     me, sent = lax.optimization_barrier((me, sent))
     arrived = lax.all_to_all(sent, plane, split_axis=0, concat_axis=0, tiled=True)
-    packed = [pack_rows((chip, chip ^ CORE), me, queries, output_gradient) for chip in CHIPS]
-    me, packed[-1] = lax.optimization_barrier((me, packed[-1]))
+    *packed, beside = pack_rows(me, queries, output_gradient)
     pairs = [swap(rows, chip) for rows, chip in zip(packed, CHIPS)]
-    beside = swap(pack_rows((CORE,), me, queries, output_gradient), CORE)
+    beside = swap(beside, CORE)
     arrived, beside = lax.optimization_barrier((arrived, beside))
     mine, small, counts = compact(arrived)
     up = [lax.ppermute(mine, "outer", [(i, i + 1) for i in range(planes - 1)])]
@@ -809,11 +793,10 @@
     dq, back2 = lax.optimization_barrier((dq, back2))
     backs = [lower(down3, 3), back2, lower(down1, 1)]
     dq = lax.all_to_all(dq, plane, split_axis=0, concat_axis=0, tiled=True)
-    dq, own = lax.optimization_barrier((dq, own))
+    spread = combine(counts, own, backs, home_rows)
+    dq, spread = lax.optimization_barrier((dq, spread))
     dq_home = unpack_rows(dq)
-    kv_home = lax.all_to_all(
-        combine(counts, own, backs, home_rows), plane, split_axis=0, concat_axis=0, tiled=True
-    )
+    kv_home = lax.all_to_all(spread, plane, split_axis=0, concat_axis=0, tiled=True)
     full = (full1[0] + full2[0]) > 0
     for back in backs:
         full = full | (back[capacity, 0] > 0)

time: 165 us -> 163 us (0.988)
  Pallas kernels: 38 us -> 32.1 us
  waiting for transfers between devices: 73.5 us -> 77.3 us
    all_to_all x1, waiting for transfers between devices: 21.8 us -> 0.01 us  [plane_device(): dq = lax.all_to_all(dq, plane, split_axis=0, concat_axis=0, tiled=True)]
    ppermute x3, waiting for transfers between devices: 12.2 us -> 33.6 us  [lower(): return lax.ppermute(rows, 'outer', [(i + k, i) for i in range(planes - k)])]
    pallas_call x4 -> x1, Pallas kernels: 8.56 us -> 3.38 us  [pack_rows(): pl.pallas_call(pack_rows_kernel, out_shape=(pair, pair, pair, beside), in...]
    all_to_all x1, waiting for transfers between devices: 0.12 us -> 4.74 us  [plane_device(): lax.all_to_all(sent, plane, split_axis=0, concat_axis=0, tiled=True)]
  transfers between devices with their start and end apart: 16 -> 16, of which waited for: 11 -> 11; matrix products, arithmetic and copies ran while one was open for 2% -> 2% of each run, Pallas kernels for 16% -> 14%
where the time goes in v6:
time: 163 us; the launch traced here: 162 us
  waiting for transfers between devices  77.3 us (47%)
  Pallas kernels  32.1 us (20%)
  starting transfers between devices  29.6 us (18%)
  between operations  17.2 us (11%)
  local copies, waits for them, and re-layouts  5.38 us (3%)
    ppermute x3, waiting for transfers between devices, lower(): return lax.ppermute(rows, 'outer', [(i + k, i) for i in range(planes - k)])  33.6 us
    ppermute x7, waiting for transfers between devices, swap(): return lax.ppermute(array, plane, [(i, i ^ k) for i in range(blocks)])  28.6 us
    pallas_call x2, Pallas kernels, attention(): pl.pallas_call(functools.partial(attention_kernel, first), out_shape=outs...  17.5 us
    ppermute x1, waiting for transfers between devices, plane_device(): up = [lax.ppermute(mine, 'outer', [(i, i + 1) for i in range(planes - 1)])]  6.3 us
    all_to_all x1, starting transfers between devices, plane_device(): lax.all_to_all(sent, plane, split_axis=0, concat_axis=0, tiled=True)  5.17 us
    all_to_all x1, waiting for transfers between devices, plane_device(): lax.all_to_all(sent, plane, split_axis=0, concat_axis=0, tiled=True)  4.74 us
    ppermute x7, starting transfers between devices, swap(): return lax.ppermute(array, plane, [(i, i ^ k) for i in range(blocks)])  4.7 us
    pallas_call x1, Pallas kernels, pack_pairs(): pl.pallas_call(functools.partial(pack_pairs_kernel, limit), out_shape=jax...  4.68 us
  transfers between devices with their start and end apart: 16, of which 11 were waited for; matrix products, arithmetic and copies ran while one was open for 2% of the time, Pallas kernels for 14%

profile of v6, /device:TPU:0, one launch (start us, length us, event | category | flops | bytes accessed | tf_op | source)
XLA Modules:
  0.0 161.7 jit_solution(3340253868982584487)
XLA Ops:
  7.2 0.0 copy-start.10
  7.2 4.7 %pack_pairs.1 = bf16[8,208,256]{2,1,0:T(8,128)(2,1)} custom-call(s32[1,192]{1,0:T(1,128)} %bitcast.286, bf16[40,192]{1,0:T(8,128)(2,1)} %bitcast.284, bf16[192,1024]{1,0:T(8,128)(2,1)} %k_ref.1, bf16[192,1024]{1,0:T(8,128)(2,1)} %v_ref.1, bf16[192,5120]{1,0:T(8,128)(2,1)} %rest_2_.3, bf16[192,5120]{1,0:T(8,128)(2,1)} %o_ref.1), custom_call_target="tpu_custom_call" | custom-call | tf_op jit(solution)/shard_map/pack_pairs/pallas_call | solution.py:252
  11.9 5.2 %all-to-all-start.20 = ((bf16[8,208,256]{2,1,0:T(8,128)(2,1)}), bf16[8,208,256]{2,1,0:T(8,128)(2,1)S(1)}, u32[]{:S(2)}, u32[]{:S(2)}) async-start(bf16[8,208,256]{2,1,0:T(8,128)(2,1)} %pack_pairs.1), calls=%async_computation.20 | async-start | bytes 1703936 | tf_op jit(solution)/shard_map/all_to_all | solution.py:773
  17.0 0.0 copy-done.10
  17.0 3.4 %pack_rows.1 = (bf16[2,192,1280]{2,1,0:T(8,128)(2,1)}, bf16[2,192,1280]{2,1,0:T(8,128)(2,1)}, bf16[2,192,1280]{2,1,0:T(8,128)(2,1)}, bf16[1,192,1280]{2,1,0:T(8,128)(2,1)S(1)}) custom-call(s32[1]{0:T(128)} %bitcast.48.me_ref, bf16[192,5120]{1,0:T(8,128)(2,1)} %rest_1_.3, bf16[192,5120]{1,0:T(8,128)(2,1)S(1)} %copy-done.10), custom_call_target="tpu_custom_call" | custom-call | tf_op jit(solution)/shard_map/pack_rows/pallas_call | solution.py:278
  20.4 0.5 collective-permute-start
  20.9 2.6 %collective-permute-start.4 = (bf16[2,192,1280]{2,1,0:T(8,128)(2,1)}, bf16[2,192,1280]{2,1,0:T(8,128)(2,1)S(1)}, u32[]{:S(2)}, u32[]{:S(2)}) collective-permute-start(bf16[2,192,1280]{2,1,0:T(8,128)(2,1)} %get-tuple-element.402), channel_id=1, source_target_pairs={{0,5},{1,4},{2,7},{3,6},{4,1},{5,0},{6,3},{7,2},{8,13},{9,12},{10,... | collective-permute-start | bytes 2949128 | tf_op jit(solution)/shard_map/ppermute | solution.py:767
  23.5 0.6 collective-permute-start.5
  24.1 0.3 collective-permute-start.6
  24.4 0.0 collective-permute-done.rest_3_
  24.4 0.8 copy-done
  25.2 4.7 %all-to-all-done.20.arrived = bf16[8,208,256]{2,1,0:T(8,128)(2,1)S(1)} async-done(((bf16[8,208,256]{2,1,0:T(8,128)(2,1)}), bf16[8,208,256]{2,1,0:T(8,128)(2,1)S(1)}, u32[]{:S(2)}, u32[]{:S(2)}) %all-to-all-start.20) | async-done | bytes 852000 | tf_op jit(solution)/shard_map/all_to_all | solution.py:773
  30.0 1.1 compact.1
  31.1 3.5 %collective-permute-start.1 = (bf16[784,256]{1,0:T(8,128)(2,1)S(1)}, bf16[784,256]{1,0:T(8,128)(2,1)S(1)}, u32[]{:S(2)}, u32[]{:S(2)}) collective-permute-start(bf16[784,256]{1,0:T(8,128)(2,1)S(1)} %get-tuple-element.401.rest_11_), channel_id=1, source_target_pairs={{0,8},{8,16},{16,24},{1,9},{9,17},{17,25},{2,10},{10,18},{18,26},{... | collective-permute-start | bytes 1204232 | tf_op jit(solution)/shard_map/ppermute | solution.py:779
  34.6 3.3 %collective-permute-start.3 = (bf16[784,256]{1,0:T(8,128)(2,1)S(1)}, bf16[784,256]{1,0:T(8,128)(2,1)S(1)}, u32[]{:S(2)}, u32[]{:S(2)}) collective-permute-start(bf16[784,256]{1,0:T(8,128)(2,1)S(1)} %get-tuple-element.401.rest_11_), channel_id=1, source_target_pairs={{0,24},{1,25},{2,26},{3,27},{4,28},{5,29},{6,30},{7,31}} | collective-permute-start | bytes 1204232 | tf_op jit(solution)/shard_map/ppermute | solution.py:780
  37.9 6.3 %collective-permute-done.1.rest_10_ = bf16[784,256]{1,0:T(8,128)(2,1)S(1)} collective-permute-done((bf16[784,256]{1,0:T(8,128)(2,1)S(1)}, bf16[784,256]{1,0:T(8,128)(2,1)S(1)}, u32[]{:S(2)}, u32[]{:S(2)}) %collective-permute-start.1) | collective-permute-done | bytes 401440 | tf_op jit(solution)/shard_map/ppermute | solution.py:779
  44.2 0.7 collective-permute-start.2
  44.9 7.1 %collective-permute-done.4.rest_4_ = bf16[2,192,1280]{2,1,0:T(8,128)(2,1)S(1)} collective-permute-done((bf16[2,192,1280]{2,1,0:T(8,128)(2,1)}, bf16[2,192,1280]{2,1,0:T(8,128)(2,1)S(1)}, u32[]{:S(2)}, u32[]{:S(2)}) %collective-permute-start.4) | collective-permute-done | bytes 983072 | tf_op jit(solution)/shard_map/ppermute | solution.py:767
  52.0 19.7 %collective-permute-done.5.rest_5_ = bf16[2,192,1280]{2,1,0:T(8,128)(2,1)S(1)} collective-permute-done((bf16[2,192,1280]{2,1,0:T(8,128)(2,1)}, bf16[2,192,1280]{2,1,0:T(8,128)(2,1)S(1)}, u32[]{:S(2)}, u32[]{:S(2)}) %collective-permute-start.5) | collective-permute-done | bytes 983072 | tf_op jit(solution)/shard_map/ppermute | solution.py:767
  71.7 0.0 collective-permute-done.6.rest_6_
  71.7 0.0 collective-permute-done.3.rest_11_
  71.7 0.0 collective-permute-done.2.rest_10_
  71.7 0.1 collective-permute-start.7
  71.8 0.6 collective-permute-start.8
  72.4 1.1 slice.35
  73.4 0.1 collective-permute-start.9
  73.5 0.1 collective-permute-done.7.rest_7_
  73.6 0.7 collective-permute-done.8.rest_8_
  74.3 1.0 collective-permute-done.9.rest_9_
  75.4 0.0 copy-done.1
  75.4 0.0 copy-done.11
  75.4 4.5 %attention.2 = (bf16[784,256]{1,0:T(8,128)(2,1)S(1)}, bf16[784,256]{1,0:T(8,128)(2,1)S(1)}, f32[12,128,640]{2,1,0:T(8,128)}, s32[1]{0:T(128)}) custom-call(s32[1]{0:T(128)} %bitcast.48.me_ref, s32[8]{0:T(128)S(1)} %get-tuple-element.398.counts_ref, bf16[8,16,256]{2,1,0:T(8,128)(2,1)S(1)} %get-tuple-element.399.rest_0_, bf16[192,5120]{1,0:T(8,128)(2,1)} %rest_1_.3, ...), custom_call_target="tpu_custom_call" | custom-call | flops 5000000000 | bytes 12000000 | tf_op jit(solution)/shard_map/attention/pallas_call | solution.py:674
  79.9 0.0 copy-start.2
  79.9 1.3 collective-permute-start.11
  81.2 0.0 copy-done.13
  81.2 13.0 %attention.3 = (bf16[784,256]{1,0:T(8,128)(2,1)S(1)}, bf16[8,192,640]{2,1,0:T(8,128)(2,1)}, f32[768,256]{1,0:T(8,128)S(1)}, s32[1]{0:T(128)}) custom-call(s32[1]{0:T(128)} %bitcast.48.me_ref, s32[8]{0:T(128)S(1)} %get-tuple-element.398.counts_ref, bf16[8,16,256]{2,1,0:T(8,128)(2,1)S(1)} %get-tuple-element.399.rest_0_, bf16[192,5120]{1,0:T(8,128)(2,1)S(1)} %copy-done.13, ...), custom_call_target="tpu_custom_call" | custom-call | flops 5000000000 | bytes 12000000 | tf_op jit(solution)/shard_map/attention/pallas_call | solution.py:674
  94.2 0.0 copy-done.2
  94.2 0.0 copy-start.4
  94.2 0.7 copy-done.4
  95.0 12.8 %collective-permute-done.11.rest_1_ = bf16[784,256]{1,0:T(8,128)(2,1)S(1)} collective-permute-done((bf16[784,256]{1,0:T(8,128)(2,1)S(1)}, bf16[784,256]{1,0:T(8,128)(2,1)S(1)}, u32[]{:S(2)}, u32[]{:S(2)}) %collective-permute-start.11) | collective-permute-done | bytes 401440 | tf_op jit(solution)/shard_map/ppermute | solution.py:788
  107.8 4.5 %all-to-all-start.21 = ((bf16[8,192,640]{2,1,0:T(8,128)(2,1)}), bf16[8,192,640]{2,1,0:T(8,128)(2,1)}, u32[]{:S(2)}, u32[]{:S(2)}) async-start(bf16[8,192,640]{2,1,0:T(8,128)(2,1)} %get-tuple-element.418), calls=%async_computation.21 | async-start | bytes 3932160 | tf_op jit(solution)/shard_map/all_to_all | solution.py:795
  112.3 0.0 copy-done.3
  112.3 1.3 collective-permute-start.10
  113.6 0.0 copy-done.5
  113.6 1.3 collective-permute-start.12
  114.9 13.3 %collective-permute-done.10.rest_0_ = bf16[784,256]{1,0:T(8,128)(2,1)S(1)} collective-permute-done((bf16[784,256]{1,0:T(8,128)(2,1)S(1)}, bf16[784,256]{1,0:T(8,128)(2,1)S(1)}, u32[]{:S(2)}, u32[]{:S(2)}) %collective-permute-start.10) | collective-permute-done | bytes 401440 | tf_op jit(solution)/shard_map/ppermute | solution.py:788
  128.1 7.5 %collective-permute-done.12.rest_2_ = bf16[784,256]{1,0:T(8,128)(2,1)S(1)} collective-permute-done((bf16[784,256]{1,0:T(8,128)(2,1)S(1)}, bf16[784,256]{1,0:T(8,128)(2,1)S(1)}, u32[]{:S(2)}, u32[]{:S(2)}) %collective-permute-start.12) | collective-permute-done | bytes 401440 | tf_op jit(solution)/shard_map/ppermute | solution.py:788
  135.6 2.3 %combine.1 = bf16[8,192,256]{2,1,0:T(8,128)(2,1)} custom-call(s32[8]{0:T(128)S(1)} %get-tuple-element.398.counts_ref, f32[768,256]{1,0:T(8,128)S(1)} %get-tuple-element.419.own, bf16[784,256]{1,0:T(8,128)(2,1)S(1)} %collective-permute-done.10.rest_0_, bf16[784,256]{1,0:T(8,128)(2,1)S(1)} %collective-permute-done.11.rest_1_, ...), custom_call_target="tpu_custom_call" | custom-call | tf_op jit(solution)/shard_map/combine/pallas_call | solution.py:745
  138.0 0.0 all-to-all-done.21.parts
  138.0 3.9 %all-to-all-start.22 = ((bf16[8,192,256]{2,1,0:T(8,128)(2,1)}), bf16[8,192,256]{2,1,0:T(8,128)(2,1)S(1)}, u32[]{:S(2)}, u32[]{:S(2)}) async-start(bf16[8,192,256]{2,1,0:T(8,128)(2,1)} %combine.1), calls=%async_computation.22 | async-start | bytes 1572864 | tf_op jit(solution)/shard_map/all_to_all | solution.py:799
  143.0 0.5 slice.37
  143.5 0.5 slice.49
  145.2 0.5 slice.50
  146.3 0.0 copy-start.12
  146.3 0.0 copy-start.16
  146.3 0.0 copy-start.21
  146.3 3.1 %unpack_rows.1 = bf16[192,5120]{1,0:T(8,128)(2,1)} custom-call(bf16[8,192,640]{2,1,0:T(8,128)(2,1)} %all-to-all-done.21.parts), custom_call_target="tpu_custom_call" | custom-call | tf_op jit(solution)/shard_map/unpack_rows/pallas_call | solution.py:712
  149.4 4.1 %all-to-all-done.22 = bf16[8,192,256]{2,1,0:T(8,128)(2,1)S(1)} async-done(((bf16[8,192,256]{2,1,0:T(8,128)(2,1)}), bf16[8,192,256]{2,1,0:T(8,128)(2,1)S(1)}, u32[]{:S(2)}, u32[]{:S(2)}) %all-to-all-start.22) | async-done | bytes 786464 | tf_op jit(solution)/shard_map/all_to_all | solution.py:799
  153.6 0.2 slice_bitcast_fusion
  153.8 0.0 copy-done.12
  153.8 0.0 copy-done.16
  153.8 0.0 copy-done.21
  153.8 1.0 conditional.1
  153.8 1.0 copy_bitcast_fusion
  (8 shorter events, 0.1 us)
Async XLA Ops:
  7.2 9.9 %copy-start.10 = (bf16[192,5120]{1,0:T(8,128)(2,1)S(1)}, bf16[192,5120]{1,0:T(8,128)(2,1)}, u32[]{:S(2)}) copy-start(bf16[192,5120]{1,0:T(8,128)(2,1)} %rest_2_.3) | copy-start | bytes 5898244
  11.9 18.1 %all-to-all-start.20 = ((bf16[8,208,256]{2,1,0:T(8,128)(2,1)}), bf16[8,208,256]{2,1,0:T(8,128)(2,1)S(1)}, u32[]{:S(2)}, u32[]{:S(2)}) async-start(bf16[8,208,256]{2,1,0:T(8,128)(2,1)} %pack_pairs.1), calls=%async_computation.20 | async-start | bytes 1703936 | tf_op jit(solution)/shard_map/all_to_all | solution.py:773
  20.4 4.0 %collective-permute-start = (bf16[1,192,1280]{2,1,0:T(8,128)(2,1)S(1)}, bf16[1,192,1280]{2,1,0:T(8,128)(2,1)S(1)}, u32[]{:S(2)}, u32[]{:S(2)}) collective-permute-start(bf16[1,192,1280]{2,1,0:T(8,128)(2,1)S(1)} %get-tuple-element.396), channel_id=1, source_target_pairs={{0,2},{1,3},{2,0},{3,1},{4,6},{5,7},{6,4},{7,5},{8,10},{9,11},{10,... | collective-permute-start | bytes 1474568 | tf_op jit(solution)/shard_map/ppermute | solution.py:767
  20.9 31.0 %collective-permute-start.4 = (bf16[2,192,1280]{2,1,0:T(8,128)(2,1)}, bf16[2,192,1280]{2,1,0:T(8,128)(2,1)S(1)}, u32[]{:S(2)}, u32[]{:S(2)}) collective-permute-start(bf16[2,192,1280]{2,1,0:T(8,128)(2,1)} %get-tuple-element.402), channel_id=1, source_target_pairs={{0,5},{1,4},{2,7},{3,6},{4,1},{5,0},{6,3},{7,2},{8,13},{9,12},{10,... | collective-permute-start | bytes 2949128 | tf_op jit(solution)/shard_map/ppermute | solution.py:767
  23.5 48.2 %collective-permute-start.5 = (bf16[2,192,1280]{2,1,0:T(8,128)(2,1)}, bf16[2,192,1280]{2,1,0:T(8,128)(2,1)S(1)}, u32[]{:S(2)}, u32[]{:S(2)}) collective-permute-start(bf16[2,192,1280]{2,1,0:T(8,128)(2,1)} %get-tuple-element.403), channel_id=1, source_target_pairs={{0,4},{1,5},{2,6},{3,7},{4,0},{5,1},{6,2},{7,3},{8,12},{9,13},{10,... | collective-permute-start | bytes 2949128 | tf_op jit(solution)/shard_map/ppermute | solution.py:767
  24.1 47.6 %collective-permute-start.6 = (bf16[2,192,1280]{2,1,0:T(8,128)(2,1)}, bf16[2,192,1280]{2,1,0:T(8,128)(2,1)}, u32[]{:S(2)}, u32[]{:S(2)}) collective-permute-start(bf16[2,192,1280]{2,1,0:T(8,128)(2,1)} %get-tuple-element.404), channel_id=1, source_target_pairs={{0,1},{1,0},{2,3},{3,2},{4,5},{5,4},{6,7},{7,6},{8,9},{9,8},{10,11... | collective-permute-start | bytes 2949128 | tf_op jit(solution)/shard_map/ppermute | solution.py:767
  24.4 0.8 copy-start
  29.9 45.4 %copy-start.1 = (bf16[1,192,1280]{2,1,0:T(8,128)(2,1)S(1)}, bf16[1,192,1280]{2,1,0:T(8,128)(2,1)}, u32[]{:S(2)}) copy-start(bf16[1,192,1280]{2,1,0:T(8,128)(2,1)} %copy-done) | copy-start | bytes 1474564
  30.0 45.4 %copy-start.11 = (bf16[192,5120]{1,0:T(8,128)(2,1)S(1)}, bf16[192,5120]{1,0:T(8,128)(2,1)}, u32[]{:S(2)}) copy-start(bf16[192,5120]{1,0:T(8,128)(2,1)} %rest_2_.3) | copy-start | bytes 5898244
  31.1 13.1 %collective-permute-start.1 = (bf16[784,256]{1,0:T(8,128)(2,1)S(1)}, bf16[784,256]{1,0:T(8,128)(2,1)S(1)}, u32[]{:S(2)}, u32[]{:S(2)}) collective-permute-start(bf16[784,256]{1,0:T(8,128)(2,1)S(1)} %get-tuple-element.401.rest_11_), channel_id=1, source_target_pairs={{0,8},{8,16},{16,24},{1,9},{9,17},{17,25},{2,10},{10,18},{18,26},{... | collective-permute-start | bytes 1204232 | tf_op jit(solution)/shard_map/ppermute | solution.py:779
  34.6 37.1 %collective-permute-start.3 = (bf16[784,256]{1,0:T(8,128)(2,1)S(1)}, bf16[784,256]{1,0:T(8,128)(2,1)S(1)}, u32[]{:S(2)}, u32[]{:S(2)}) collective-permute-start(bf16[784,256]{1,0:T(8,128)(2,1)S(1)} %get-tuple-element.401.rest_11_), channel_id=1, source_target_pairs={{0,24},{1,25},{2,26},{3,27},{4,28},{5,29},{6,30},{7,31}} | collective-permute-start | bytes 1204232 | tf_op jit(solution)/shard_map/ppermute | solution.py:780
  44.2 27.4 %collective-permute-start.2 = (bf16[784,256]{1,0:T(8,128)(2,1)S(1)}, bf16[784,256]{1,0:T(8,128)(2,1)S(1)}, u32[]{:S(2)}, u32[]{:S(2)}) collective-permute-start(bf16[784,256]{1,0:T(8,128)(2,1)S(1)} %collective-permute-done.1.rest_10_), channel_id=1, source_target_pairs={{8,16},{16,24},{9,17},{17,25},{10,18},{18,26},{11,19},{19,27},{12,... | collective-permute-start | bytes 1204232 | tf_op jit(solution)/shard_map/ppermute | solution.py:781
  71.7 1.9 %collective-permute-start.7 = (bf16[1,192,1280]{2,1,0:T(8,128)(2,1)S(1)}, bf16[1,192,1280]{2,1,0:T(8,128)(2,1)S(1)}, u32[]{:S(2)}, u32[]{:S(2)}) collective-permute-start(bf16[1,192,1280]{2,1,0:T(8,128)(2,1)S(1)} %slice.33), channel_id=1, source_target_pairs={{0,2},{1,3},{2,0},{3,1},{4,6},{5,7},{6,4},{7,5},{8,10},{9,11},{10,... | collective-permute-start | bytes 1474568 | tf_op jit(solution)/shard_map/ppermute | solution.py:767
  71.8 2.5 %collective-permute-start.8 = (bf16[1,192,1280]{2,1,0:T(8,128)(2,1)S(1)}, bf16[1,192,1280]{2,1,0:T(8,128)(2,1)S(1)}, u32[]{:S(2)}, u32[]{:S(2)}) collective-permute-start(bf16[1,192,1280]{2,1,0:T(8,128)(2,1)S(1)} %slice.34), channel_id=1, source_target_pairs={{0,2},{1,3},{2,0},{3,1},{4,6},{5,7},{6,4},{7,5},{8,10},{9,11},{10,... | collective-permute-start | bytes 1474568 | tf_op jit(solution)/shard_map/ppermute | solution.py:767
  73.4 1.9 %collective-permute-start.9 = (bf16[1,192,1280]{2,1,0:T(8,128)(2,1)S(1)}, bf16[1,192,1280]{2,1,0:T(8,128)(2,1)S(1)}, u32[]{:S(2)}, u32[]{:S(2)}) collective-permute-start(bf16[1,192,1280]{2,1,0:T(8,128)(2,1)S(1)} %slice.35), channel_id=1, source_target_pairs={{0,2},{1,3},{2,0},{3,1},{4,6},{5,7},{6,4},{7,5},{8,10},{9,11},{10,... | collective-permute-start | bytes 1474568 | tf_op jit(solution)/shard_map/ppermute | solution.py:767
  75.4 5.8 %copy-start.13 = (bf16[192,5120]{1,0:T(8,128)(2,1)S(1)}, bf16[192,5120]{1,0:T(8,128)(2,1)}, u32[]{:S(2)}) copy-start(bf16[192,5120]{1,0:T(8,128)(2,1)} %rest_1_.3) | copy-start | bytes 5898244
  79.9 14.3 %copy-start.2 = (bf16[784,256]{1,0:T(8,128)(2,1)}, bf16[784,256]{1,0:T(8,128)(2,1)S(1)}, u32[]{:S(2)}) copy-start(bf16[784,256]{1,0:T(8,128)(2,1)S(1)} %get-tuple-element.413) | copy-start | bytes 1204228
  79.9 27.9 %collective-permute-start.11 = (bf16[784,256]{1,0:T(8,128)(2,1)S(1)}, bf16[784,256]{1,0:T(8,128)(2,1)S(1)}, u32[]{:S(2)}, u32[]{:S(2)}) collective-permute-start(bf16[784,256]{1,0:T(8,128)(2,1)S(1)} %get-tuple-element.415), channel_id=1, source_target_pairs={{16,0},{24,8},{17,1},{25,9},{18,2},{26,10},{19,3},{27,11},{20,4},{... | collective-permute-start | bytes 1204232 | tf_op jit(solution)/shard_map/ppermute | solution.py:788
  94.2 0.7 copy-start.4
  107.8 4.5 %copy-start.3 = (bf16[784,256]{1,0:T(8,128)(2,1)S(1)}, bf16[784,256]{1,0:T(8,128)(2,1)}, u32[]{:S(2)}) copy-start(bf16[784,256]{1,0:T(8,128)(2,1)} %copy-done.2) | copy-start | bytes 1204228
  107.8 5.8 %copy-start.5 = (bf16[784,256]{1,0:T(8,128)(2,1)S(1)}, bf16[784,256]{1,0:T(8,128)(2,1)}, u32[]{:S(2)}) copy-start(bf16[784,256]{1,0:T(8,128)(2,1)} %copy-done.4) | copy-start | bytes 1204228
  107.8 30.2 %all-to-all-start.21 = ((bf16[8,192,640]{2,1,0:T(8,128)(2,1)}), bf16[8,192,640]{2,1,0:T(8,128)(2,1)}, u32[]{:S(2)}, u32[]{:S(2)}) async-start(bf16[8,192,640]{2,1,0:T(8,128)(2,1)} %get-tuple-element.418), calls=%async_computation.21 | async-start | bytes 3932160 | tf_op jit(solution)/shard_map/all_to_all | solution.py:795
  112.3 15.9 %collective-permute-start.10 = (bf16[784,256]{1,0:T(8,128)(2,1)S(1)}, bf16[784,256]{1,0:T(8,128)(2,1)S(1)}, u32[]{:S(2)}, u32[]{:S(2)}) collective-permute-start(bf16[784,256]{1,0:T(8,128)(2,1)S(1)} %copy-done.3), channel_id=1, source_target_pairs={{24,0},{25,1},{26,2},{27,3},{28,4},{29,5},{30,6},{31,7}} | collective-permute-start | bytes 1204232 | tf_op jit(solution)/shard_map/ppermute | solution.py:788
  113.6 22.1 %collective-permute-start.12 = (bf16[784,256]{1,0:T(8,128)(2,1)S(1)}, bf16[784,256]{1,0:T(8,128)(2,1)S(1)}, u32[]{:S(2)}, u32[]{:S(2)}) collective-permute-start(bf16[784,256]{1,0:T(8,128)(2,1)S(1)} %copy-done.5), channel_id=1, source_target_pairs={{8,0},{16,8},{24,16},{9,1},{17,9},{25,17},{10,2},{18,10},{26,18},{... | collective-permute-start | bytes 1204232 | tf_op jit(solution)/shard_map/ppermute | solution.py:788
  138.0 15.6 %all-to-all-start.22 = ((bf16[8,192,256]{2,1,0:T(8,128)(2,1)}), bf16[8,192,256]{2,1,0:T(8,128)(2,1)S(1)}, u32[]{:S(2)}, u32[]{:S(2)}) async-start(bf16[8,192,256]{2,1,0:T(8,128)(2,1)} %combine.1), calls=%async_computation.22 | async-start | bytes 1572864 | tf_op jit(solution)/shard_map/all_to_all | solution.py:799
  146.3 7.5 %copy-start.12 = (bf16[192,5120]{1,0:T(8,128)(2,1)S(1)}, bf16[192,5120]{1,0:T(8,128)(2,1)}, u32[]{:S(2)}) copy-start(bf16[192,5120]{1,0:T(8,128)(2,1)} %rest_2_.3) | copy-start | bytes 5898244
  146.3 7.5 %copy-start.16 = (bf16[192,1024]{1,0:T(8,128)(2,1)S(1)}, bf16[192,1024]{1,0:T(8,128)(2,1)}, u32[]{:S(2)}) copy-start(bf16[192,1024]{1,0:T(8,128)(2,1)} %k_ref.1) | copy-start | bytes 1179652
  146.3 7.5 %copy-start.21 = (s32[192]{0:T(256)S(1)}, s32[192]{0:T(256)}, u32[]{:S(2)}) copy-start(s32[192]{0:T(256)} %param.21) | copy-start | bytes 2308

commit v7 on v6

--- a/solution.py
+++ b/solution.py
@@ -15,6 +15,13 @@
 
 
 block_keys = 512
+
+
+def gather(array, axis):
+    count = lax.axis_size(axis)
+    copies = jnp.broadcast_to(array[None], (count, *array.shape))
+    got = lax.all_to_all(copies, axis, split_axis=0, concat_axis=0, tiled=True)
+    return got.reshape(count * array.shape[0], *array.shape[1:])
 
 
 def per_device(queries, keys, values, outputs, output_gradient, lse, ranks, seq="seq"):
@@ -41,12 +48,10 @@
         lax.all_to_all(split_heads(lse), "head", split_axis=1, concat_axis=0, tiled=True),
         lax.all_to_all(split_heads(outputs), "head", split_axis=1, concat_axis=0, tiled=True),
     )
-    shard_rank_list = lax.all_gather(ranks, "head", axis=0, tiled=True)
+    shard_rank_list = gather(ranks, "head")
     first_rank = shard_rank_list[0]
     living_count = jnp.sum((shard_rank_list < surviving_tokens).astype(jnp.int32))
-    table = lax.all_gather(
-        jnp.stack([first_rank, living_count])[None, :], seq, axis=0, tiled=True
-    )
+    table = gather(jnp.stack([first_rank, living_count])[None, :], seq)
 
     def to_pairs(array):
         flat = array.reshape(slots, sequence_count, array.shape[-1])
@@ -98,8 +103,8 @@
         .astype(jnp.float32)
     )
     gathered = (
-        lax.all_gather(key_row_block, seq, axis=0, tiled=True),
-        lax.all_gather(value_row_block, seq, axis=0, tiled=True),
+        gather(key_row_block, seq),
+        gather(value_row_block, seq),
     )
     all_keys = gathered[0].reshape(sequence_count, BALANCED_TOKENS, local_key_value, HEAD_SIZE)
     all_values = gathered[1].reshape(sequence_count, BALANCED_TOKENS, local_key_value, HEAD_SIZE)

time: 163 us -> 150 us (0.920)
  the two profiles are of different devices: /device:TPU:0 before, /device:TPU:17 now
where the time goes in v7:
time: 150 us; the launch traced here: 152 us
  waiting for transfers between devices  69.4 us (46%)
  starting transfers between devices  36.8 us (25%)
  Pallas kernels  36.3 us (24%)
  local copies, waits for them, and re-layouts  5.6 us (4%)
  between operations  4.19 us (3%)
    ppermute x3, waiting for transfers between devices, lower(): return lax.ppermute(rows, 'outer', [(i + k, i) for i in range(planes - k)])  26.4 us
    ppermute x7, waiting for transfers between devices, swap(): return lax.ppermute(array, plane, [(i, i ^ k) for i in range(blocks)])  26 us
    pallas_call x2, Pallas kernels, attention(): pl.pallas_call(functools.partial(attention_kernel, first), out_shape=outs...  21.7 us
    ppermute x3, starting transfers between devices, lower(): return lax.ppermute(rows, 'outer', [(i + k, i) for i in range(planes - k)])  11.4 us
    ppermute x1, waiting for transfers between devices, plane_device(): up = [lax.ppermute(mine, 'outer', [(i, i + 1) for i in range(planes - 1)])]  8.56 us
    all_to_all x1, waiting for transfers between devices, plane_device(): lax.all_to_all(sent, plane, split_axis=0, concat_axis=0, tiled=True)  5.34 us
    all_to_all x1, starting transfers between devices, plane_device(): dq = lax.all_to_all(dq, plane, split_axis=0, concat_axis=0, tiled=True)  4.75 us
    pallas_call x1, Pallas kernels, pack_pairs(): pl.pallas_call(functools.partial(pack_pairs_kernel, limit), out_shape=jax...  4.7 us
  transfers between devices with their start and end apart: 16, of which 8 were waited for; matrix products, arithmetic and copies ran while one was open for 2% of the time, Pallas kernels for 15%

profile of v7, /device:TPU:17, one launch (start us, length us, event | category | flops | bytes accessed | tf_op | source)
XLA Modules:
  0.0 152.3 jit_solution(3943638899228315574)
XLA Ops:
  0.6 0.0 copy-start.10
  0.6 4.7 %pack_pairs.1 = bf16[8,208,256]{2,1,0:T(8,128)(2,1)} custom-call(s32[1,192]{1,0:T(1,128)} %bitcast.289, bf16[40,192]{1,0:T(8,128)(2,1)} %bitcast.285, bf16[192,1024]{1,0:T(8,128)(2,1)} %k_ref.1, bf16[192,1024]{1,0:T(8,128)(2,1)} %v_ref.1, bf16[192,5120]{1,0:T(8,128)(2,1)} %rest_2_.3, bf16[192,5120]{1,0:T(8,128)(2,1)} %o_ref.1), custom_call_target="tpu_custom_call" | custom-call | tf_op jit(solution)/shard_map/pack_pairs/pallas_call | solution.py:257
  5.4 4.4 %all-to-all-start.24 = ((bf16[8,208,256]{2,1,0:T(8,128)(2,1)}), bf16[8,208,256]{2,1,0:T(8,128)(2,1)S(1)}, u32[]{:S(2)}, u32[]{:S(2)}) async-start(bf16[8,208,256]{2,1,0:T(8,128)(2,1)} %pack_pairs.1), calls=%async_computation.24 | async-start | bytes 1703936 | tf_op jit(solution)/shard_map/all_to_all | solution.py:778
  9.7 0.0 copy-done.10
  9.8 3.4 %pack_rows.1 = (bf16[2,192,1280]{2,1,0:T(8,128)(2,1)}, bf16[2,192,1280]{2,1,0:T(8,128)(2,1)}, bf16[2,192,1280]{2,1,0:T(8,128)(2,1)}, bf16[1,192,1280]{2,1,0:T(8,128)(2,1)S(1)}) custom-call(s32[1]{0:T(128)} %bitcast.47.me_ref, bf16[192,5120]{1,0:T(8,128)(2,1)} %rest_1_.3, bf16[192,5120]{1,0:T(8,128)(2,1)S(1)} %copy-done.10), custom_call_target="tpu_custom_call" | custom-call | tf_op jit(solution)/shard_map/pack_rows/pallas_call | solution.py:283
  13.1 0.0 collective-permute-start
  13.1 2.6 %collective-permute-start.4 = (bf16[2,192,1280]{2,1,0:T(8,128)(2,1)}, bf16[2,192,1280]{2,1,0:T(8,128)(2,1)S(1)}, u32[]{:S(2)}, u32[]{:S(2)}) collective-permute-start(bf16[2,192,1280]{2,1,0:T(8,128)(2,1)} %get-tuple-element.402), channel_id=1, source_target_pairs={{0,5},{1,4},{2,7},{3,6},{4,1},{5,0},{6,3},{7,2},{8,13},{9,12},{10,... | collective-permute-start | bytes 2949128 | tf_op jit(solution)/shard_map/ppermute | solution.py:772
  15.8 0.3 collective-permute-start.5
  16.0 0.0 collective-permute-start.6
  16.0 0.0 collective-permute-done.rest_3_
  16.0 0.8 copy-done
  16.8 5.3 %all-to-all-done.24.arrived = bf16[8,208,256]{2,1,0:T(8,128)(2,1)S(1)} async-done(((bf16[8,208,256]{2,1,0:T(8,128)(2,1)}), bf16[8,208,256]{2,1,0:T(8,128)(2,1)S(1)}, u32[]{:S(2)}, u32[]{:S(2)}) %all-to-all-start.24) | async-done | bytes 852000 | tf_op jit(solution)/shard_map/all_to_all | solution.py:778
  22.2 1.1 compact.1
  23.3 3.2 %collective-permute-start.1 = (bf16[784,256]{1,0:T(8,128)(2,1)S(1)}, bf16[784,256]{1,0:T(8,128)(2,1)S(1)}, u32[]{:S(2)}, u32[]{:S(2)}) collective-permute-start(bf16[784,256]{1,0:T(8,128)(2,1)S(1)} %get-tuple-element.401.rest_11_), channel_id=1, source_target_pairs={{0,8},{8,16},{16,24},{1,9},{9,17},{17,25},{2,10},{10,18},{18,26},{... | collective-permute-start | bytes 1204232 | tf_op jit(solution)/shard_map/ppermute | solution.py:784
  26.5 0.7 collective-permute-start.3
  27.2 8.6 %collective-permute-done.1.rest_10_ = bf16[784,256]{1,0:T(8,128)(2,1)S(1)} collective-permute-done((bf16[784,256]{1,0:T(8,128)(2,1)S(1)}, bf16[784,256]{1,0:T(8,128)(2,1)S(1)}, u32[]{:S(2)}, u32[]{:S(2)}) %collective-permute-start.1) | collective-permute-done | bytes 401440 | tf_op jit(solution)/shard_map/ppermute | solution.py:784
  35.8 3.3 %collective-permute-start.2 = (bf16[784,256]{1,0:T(8,128)(2,1)S(1)}, bf16[784,256]{1,0:T(8,128)(2,1)S(1)}, u32[]{:S(2)}, u32[]{:S(2)}) collective-permute-start(bf16[784,256]{1,0:T(8,128)(2,1)S(1)} %collective-permute-done.1.rest_10_), channel_id=1, source_target_pairs={{8,16},{16,24},{9,17},{17,25},{10,18},{18,26},{11,19},{19,27},{12,... | collective-permute-start | bytes 1204232 | tf_op jit(solution)/shard_map/ppermute | solution.py:786
  39.1 4.2 %collective-permute-done.4.rest_4_ = bf16[2,192,1280]{2,1,0:T(8,128)(2,1)S(1)} collective-permute-done((bf16[2,192,1280]{2,1,0:T(8,128)(2,1)}, bf16[2,192,1280]{2,1,0:T(8,128)(2,1)S(1)}, u32[]{:S(2)}, u32[]{:S(2)}) %collective-permute-start.4) | collective-permute-done | bytes 983072 | tf_op jit(solution)/shard_map/ppermute | solution.py:772
  43.3 20.3 %collective-permute-done.5.rest_5_ = bf16[2,192,1280]{2,1,0:T(8,128)(2,1)S(1)} collective-permute-done((bf16[2,192,1280]{2,1,0:T(8,128)(2,1)}, bf16[2,192,1280]{2,1,0:T(8,128)(2,1)S(1)}, u32[]{:S(2)}, u32[]{:S(2)}) %collective-permute-start.5) | collective-permute-done | bytes 983072 | tf_op jit(solution)/shard_map/ppermute | solution.py:772
  63.6 0.0 collective-permute-done.6.rest_6_
  63.6 0.0 collective-permute-done.3.rest_11_
  63.6 0.0 collective-permute-done.2.rest_10_
  63.7 0.8 collective-permute-start.7
  64.5 0.1 collective-permute-start.8
  64.6 1.1 slice.35
  65.7 0.6 collective-permute-start.9
  66.2 0.0 collective-permute-done.7.rest_7_
  66.2 0.4 collective-permute-done.8.rest_8_
  66.7 1.0 collective-permute-done.9.rest_9_
  67.7 0.0 copy-done.1
  67.7 0.0 copy-done.11
  67.7 8.6 %attention.2 = (bf16[784,256]{1,0:T(8,128)(2,1)S(1)}, bf16[784,256]{1,0:T(8,128)(2,1)S(1)}, f32[12,128,640]{2,1,0:T(8,128)}, s32[1]{0:T(128)}) custom-call(s32[1]{0:T(128)} %bitcast.47.me_ref, s32[8]{0:T(128)S(1)} %get-tuple-element.398.counts_ref, bf16[8,16,256]{2,1,0:T(8,128)(2,1)S(1)} %get-tuple-element.399.rest_0_, bf16[192,5120]{1,0:T(8,128)(2,1)} %rest_1_.3, ...), custom_call_target="tpu_custom_call" | custom-call | flops 5000000000 | bytes 12000000 | tf_op jit(solution)/shard_map/attention/pallas_call | solution.py:679
  76.3 0.0 copy-start.2
  76.3 1.3 collective-permute-start.11
  77.6 0.0 copy-done.14
  77.7 13.2 %attention.3 = (bf16[784,256]{1,0:T(8,128)(2,1)S(1)}, bf16[8,192,640]{2,1,0:T(8,128)(2,1)}, f32[768,256]{1,0:T(8,128)S(1)}, s32[1]{0:T(128)}) custom-call(s32[1]{0:T(128)} %bitcast.47.me_ref, s32[8]{0:T(128)S(1)} %get-tuple-element.398.counts_ref, bf16[8,16,256]{2,1,0:T(8,128)(2,1)S(1)} %get-tuple-element.399.rest_0_, bf16[192,5120]{1,0:T(8,128)(2,1)S(1)} %copy-done.14, ...), custom_call_target="tpu_custom_call" | custom-call | flops 5000000000 | bytes 12000000 | tf_op jit(solution)/shard_map/attention/pallas_call | solution.py:679
  90.8 0.0 copy-done.2
  90.8 0.0 copy-start.4
  90.8 0.7 copy-done.4
  91.6 0.0 collective-permute-done.11.rest_1_
  91.6 4.7 %all-to-all-start.25 = ((bf16[8,192,640]{2,1,0:T(8,128)(2,1)}), bf16[8,192,640]{2,1,0:T(8,128)(2,1)}, u32[]{:S(2)}, u32[]{:S(2)}) async-start(bf16[8,192,640]{2,1,0:T(8,128)(2,1)} %get-tuple-element.418), calls=%async_computation.25 | async-start | bytes 3932160 | tf_op jit(solution)/shard_map/all_to_all | solution.py:800
  96.3 0.0 copy-done.3
  96.3 0.7 collective-permute-start.10
  97.0 0.0 copy-done.5
  97.0 9.5 %collective-permute-start.12 = (bf16[784,256]{1,0:T(8,128)(2,1)S(1)}, bf16[784,256]{1,0:T(8,128)(2,1)S(1)}, u32[]{:S(2)}, u32[]{:S(2)}) collective-permute-start(bf16[784,256]{1,0:T(8,128)(2,1)S(1)} %copy-done.5), channel_id=1, source_target_pairs={{8,0},{16,8},{24,16},{9,1},{17,9},{25,17},{10,2},{18,10},{26,18},{... | collective-permute-start | bytes 1204232 | tf_op jit(solution)/shard_map/ppermute | solution.py:793
  106.5 0.0 collective-permute-done.10.rest_0_
  106.5 26.4 %collective-permute-done.12.rest_2_ = bf16[784,256]{1,0:T(8,128)(2,1)S(1)} collective-permute-done((bf16[784,256]{1,0:T(8,128)(2,1)S(1)}, bf16[784,256]{1,0:T(8,128)(2,1)S(1)}, u32[]{:S(2)}, u32[]{:S(2)}) %collective-permute-start.12) | collective-permute-done | bytes 401440 | tf_op jit(solution)/shard_map/ppermute | solution.py:793
  132.9 2.3 %combine.1 = bf16[8,192,256]{2,1,0:T(8,128)(2,1)} custom-call(s32[8]{0:T(128)S(1)} %get-tuple-element.398.counts_ref, f32[768,256]{1,0:T(8,128)S(1)} %get-tuple-element.419.own, bf16[784,256]{1,0:T(8,128)(2,1)S(1)} %collective-permute-done.10.rest_0_, bf16[784,256]{1,0:T(8,128)(2,1)S(1)} %collective-permute-done.11.rest_1_, ...), custom_call_target="tpu_custom_call" | custom-call | tf_op jit(solution)/shard_map/combine/pallas_call | solution.py:750
  135.2 0.0 all-to-all-done.25.parts
  135.2 4.6 %all-to-all-start.26 = ((bf16[8,192,256]{2,1,0:T(8,128)(2,1)}), bf16[8,192,256]{2,1,0:T(8,128)(2,1)S(1)}, u32[]{:S(2)}, u32[]{:S(2)}) async-start(bf16[8,192,256]{2,1,0:T(8,128)(2,1)} %combine.1), calls=%async_computation.26 | async-start | bytes 1572864 | tf_op jit(solution)/shard_map/all_to_all | solution.py:804
  141.1 0.6 slice.37
  141.7 0.5 slice.47
  143.5 0.6 slice.48
  144.8 0.0 copy-start.12
  144.8 0.0 copy-start.21
  144.8 0.0 copy-start.26
  144.9 3.1 %unpack_rows.1 = bf16[192,5120]{1,0:T(8,128)(2,1)} custom-call(bf16[8,192,640]{2,1,0:T(8,128)(2,1)} %all-to-all-done.25.parts), custom_call_target="tpu_custom_call" | custom-call | tf_op jit(solution)/shard_map/unpack_rows/pallas_call | solution.py:717
  148.0 3.1 %all-to-all-done.26 = bf16[8,192,256]{2,1,0:T(8,128)(2,1)S(1)} async-done(((bf16[8,192,256]{2,1,0:T(8,128)(2,1)}), bf16[8,192,256]{2,1,0:T(8,128)(2,1)S(1)}, u32[]{:S(2)}, u32[]{:S(2)}) %all-to-all-start.26) | async-done | bytes 786464 | tf_op jit(solution)/shard_map/all_to_all | solution.py:804
  151.1 0.2 slice_bitcast_fusion.2
  151.3 0.0 copy-done.12
  151.3 0.0 copy-done.21
  151.3 0.0 copy-done.26
  151.3 1.0 conditional.1
  151.3 1.0 copy_bitcast_fusion
  (8 shorter events, 0.1 us)
Async XLA Ops:
  0.6 9.1 %copy-start.10 = (bf16[192,5120]{1,0:T(8,128)(2,1)S(1)}, bf16[192,5120]{1,0:T(8,128)(2,1)}, u32[]{:S(2)}) copy-start(bf16[192,5120]{1,0:T(8,128)(2,1)} %rest_2_.3) | copy-start | bytes 5898244
  5.4 16.8 %all-to-all-start.24 = ((bf16[8,208,256]{2,1,0:T(8,128)(2,1)}), bf16[8,208,256]{2,1,0:T(8,128)(2,1)S(1)}, u32[]{:S(2)}, u32[]{:S(2)}) async-start(bf16[8,208,256]{2,1,0:T(8,128)(2,1)} %pack_pairs.1), calls=%async_computation.24 | async-start | bytes 1703936 | tf_op jit(solution)/shard_map/all_to_all | solution.py:778
  13.1 2.9 %collective-permute-start = (bf16[1,192,1280]{2,1,0:T(8,128)(2,1)S(1)}, bf16[1,192,1280]{2,1,0:T(8,128)(2,1)S(1)}, u32[]{:S(2)}, u32[]{:S(2)}) collective-permute-start(bf16[1,192,1280]{2,1,0:T(8,128)(2,1)S(1)} %get-tuple-element.396), channel_id=1, source_target_pairs={{0,2},{1,3},{2,0},{3,1},{4,6},{5,7},{6,4},{7,5},{8,10},{9,11},{10,... | collective-permute-start | bytes 1474568 | tf_op jit(solution)/shard_map/ppermute | solution.py:772
  13.1 30.2 %collective-permute-start.4 = (bf16[2,192,1280]{2,1,0:T(8,128)(2,1)}, bf16[2,192,1280]{2,1,0:T(8,128)(2,1)S(1)}, u32[]{:S(2)}, u32[]{:S(2)}) collective-permute-start(bf16[2,192,1280]{2,1,0:T(8,128)(2,1)} %get-tuple-element.402), channel_id=1, source_target_pairs={{0,5},{1,4},{2,7},{3,6},{4,1},{5,0},{6,3},{7,2},{8,13},{9,12},{10,... | collective-permute-start | bytes 2949128 | tf_op jit(solution)/shard_map/ppermute | solution.py:772
  15.8 47.8 %collective-permute-start.5 = (bf16[2,192,1280]{2,1,0:T(8,128)(2,1)}, bf16[2,192,1280]{2,1,0:T(8,128)(2,1)S(1)}, u32[]{:S(2)}, u32[]{:S(2)}) collective-permute-start(bf16[2,192,1280]{2,1,0:T(8,128)(2,1)} %get-tuple-element.403), channel_id=1, source_target_pairs={{0,4},{1,5},{2,6},{3,7},{4,0},{5,1},{6,2},{7,3},{8,12},{9,13},{10,... | collective-permute-start | bytes 2949128 | tf_op jit(solution)/shard_map/ppermute | solution.py:772
  16.0 47.6 %collective-permute-start.6 = (bf16[2,192,1280]{2,1,0:T(8,128)(2,1)}, bf16[2,192,1280]{2,1,0:T(8,128)(2,1)}, u32[]{:S(2)}, u32[]{:S(2)}) collective-permute-start(bf16[2,192,1280]{2,1,0:T(8,128)(2,1)} %get-tuple-element.404), channel_id=1, source_target_pairs={{0,1},{1,0},{2,3},{3,2},{4,5},{5,4},{6,7},{7,6},{8,9},{9,8},{10,11... | collective-permute-start | bytes 2949128 | tf_op jit(solution)/shard_map/ppermute | solution.py:772
  16.0 0.8 copy-start
  22.2 45.5 %copy-start.1 = (bf16[1,192,1280]{2,1,0:T(8,128)(2,1)S(1)}, bf16[1,192,1280]{2,1,0:T(8,128)(2,1)}, u32[]{:S(2)}) copy-start(bf16[1,192,1280]{2,1,0:T(8,128)(2,1)} %copy-done) | copy-start | bytes 1474564
  22.2 45.5 %copy-start.11 = (bf16[192,5120]{1,0:T(8,128)(2,1)S(1)}, bf16[192,5120]{1,0:T(8,128)(2,1)}, u32[]{:S(2)}) copy-start(bf16[192,5120]{1,0:T(8,128)(2,1)} %rest_2_.3) | copy-start | bytes 5898244
  23.3 12.5 %collective-permute-start.1 = (bf16[784,256]{1,0:T(8,128)(2,1)S(1)}, bf16[784,256]{1,0:T(8,128)(2,1)S(1)}, u32[]{:S(2)}, u32[]{:S(2)}) collective-permute-start(bf16[784,256]{1,0:T(8,128)(2,1)S(1)} %get-tuple-element.401.rest_11_), channel_id=1, source_target_pairs={{0,8},{8,16},{16,24},{1,9},{9,17},{17,25},{2,10},{10,18},{18,26},{... | collective-permute-start | bytes 1204232 | tf_op jit(solution)/shard_map/ppermute | solution.py:784
  26.5 37.1 %collective-permute-start.3 = (bf16[784,256]{1,0:T(8,128)(2,1)S(1)}, bf16[784,256]{1,0:T(8,128)(2,1)S(1)}, u32[]{:S(2)}, u32[]{:S(2)}) collective-permute-start(bf16[784,256]{1,0:T(8,128)(2,1)S(1)} %get-tuple-element.401.rest_11_), channel_id=1, source_target_pairs={{0,24},{1,25},{2,26},{3,27},{4,28},{5,29},{6,30},{7,31}} | collective-permute-start | bytes 1204232 | tf_op jit(solution)/shard_map/ppermute | solution.py:785
  35.8 27.8 %collective-permute-start.2 = (bf16[784,256]{1,0:T(8,128)(2,1)S(1)}, bf16[784,256]{1,0:T(8,128)(2,1)S(1)}, u32[]{:S(2)}, u32[]{:S(2)}) collective-permute-start(bf16[784,256]{1,0:T(8,128)(2,1)S(1)} %collective-permute-done.1.rest_10_), channel_id=1, source_target_pairs={{8,16},{16,24},{9,17},{17,25},{10,18},{18,26},{11,19},{19,27},{12,... | collective-permute-start | bytes 1204232 | tf_op jit(solution)/shard_map/ppermute | solution.py:786
  63.7 2.6 %collective-permute-start.7 = (bf16[1,192,1280]{2,1,0:T(8,128)(2,1)S(1)}, bf16[1,192,1280]{2,1,0:T(8,128)(2,1)S(1)}, u32[]{:S(2)}, u32[]{:S(2)}) collective-permute-start(bf16[1,192,1280]{2,1,0:T(8,128)(2,1)S(1)} %slice.33), channel_id=1, source_target_pairs={{0,2},{1,3},{2,0},{3,1},{4,6},{5,7},{6,4},{7,5},{8,10},{9,11},{10,... | collective-permute-start | bytes 1474568 | tf_op jit(solution)/shard_map/ppermute | solution.py:772
  64.5 2.2 %collective-permute-start.8 = (bf16[1,192,1280]{2,1,0:T(8,128)(2,1)S(1)}, bf16[1,192,1280]{2,1,0:T(8,128)(2,1)S(1)}, u32[]{:S(2)}, u32[]{:S(2)}) collective-permute-start(bf16[1,192,1280]{2,1,0:T(8,128)(2,1)S(1)} %slice.34), channel_id=1, source_target_pairs={{0,2},{1,3},{2,0},{3,1},{4,6},{5,7},{6,4},{7,5},{8,10},{9,11},{10,... | collective-permute-start | bytes 1474568 | tf_op jit(solution)/shard_map/ppermute | solution.py:772
  65.7 2.0 %collective-permute-start.9 = (bf16[1,192,1280]{2,1,0:T(8,128)(2,1)S(1)}, bf16[1,192,1280]{2,1,0:T(8,128)(2,1)S(1)}, u32[]{:S(2)}, u32[]{:S(2)}) collective-permute-start(bf16[1,192,1280]{2,1,0:T(8,128)(2,1)S(1)} %slice.35), channel_id=1, source_target_pairs={{0,2},{1,3},{2,0},{3,1},{4,6},{5,7},{6,4},{7,5},{8,10},{9,11},{10,... | collective-permute-start | bytes 1474568 | tf_op jit(solution)/shard_map/ppermute | solution.py:772
  67.7 9.9 %copy-start.14 = (bf16[192,5120]{1,0:T(8,128)(2,1)S(1)}, bf16[192,5120]{1,0:T(8,128)(2,1)}, u32[]{:S(2)}) copy-start(bf16[192,5120]{1,0:T(8,128)(2,1)} %rest_1_.3) | copy-start | bytes 5898244
  76.3 14.5 %copy-start.2 = (bf16[784,256]{1,0:T(8,128)(2,1)}, bf16[784,256]{1,0:T(8,128)(2,1)S(1)}, u32[]{:S(2)}) copy-start(bf16[784,256]{1,0:T(8,128)(2,1)S(1)} %get-tuple-element.413) | copy-start | bytes 1204228
  76.3 15.3 %collective-permute-start.11 = (bf16[784,256]{1,0:T(8,128)(2,1)S(1)}, bf16[784,256]{1,0:T(8,128)(2,1)S(1)}, u32[]{:S(2)}, u32[]{:S(2)}) collective-permute-start(bf16[784,256]{1,0:T(8,128)(2,1)S(1)} %get-tuple-element.415), channel_id=1, source_target_pairs={{16,0},{24,8},{17,1},{25,9},{18,2},{26,10},{19,3},{27,11},{20,4},{... | collective-permute-start | bytes 1204232 | tf_op jit(solution)/shard_map/ppermute | solution.py:793
  90.8 0.8 copy-start.4
  91.6 4.8 %copy-start.3 = (bf16[784,256]{1,0:T(8,128)(2,1)S(1)}, bf16[784,256]{1,0:T(8,128)(2,1)}, u32[]{:S(2)}) copy-start(bf16[784,256]{1,0:T(8,128)(2,1)} %copy-done.2) | copy-start | bytes 1204228
  91.6 5.4 %copy-start.5 = (bf16[784,256]{1,0:T(8,128)(2,1)S(1)}, bf16[784,256]{1,0:T(8,128)(2,1)}, u32[]{:S(2)}) copy-start(bf16[784,256]{1,0:T(8,128)(2,1)} %copy-done.4) | copy-start | bytes 1204228
  91.6 43.6 %all-to-all-start.25 = ((bf16[8,192,640]{2,1,0:T(8,128)(2,1)}), bf16[8,192,640]{2,1,0:T(8,128)(2,1)}, u32[]{:S(2)}, u32[]{:S(2)}) async-start(bf16[8,192,640]{2,1,0:T(8,128)(2,1)} %get-tuple-element.418), calls=%async_computation.25 | async-start | bytes 3932160 | tf_op jit(solution)/shard_map/all_to_all | solution.py:800
  96.3 10.2 %collective-permute-start.10 = (bf16[784,256]{1,0:T(8,128)(2,1)S(1)}, bf16[784,256]{1,0:T(8,128)(2,1)S(1)}, u32[]{:S(2)}, u32[]{:S(2)}) collective-permute-start(bf16[784,256]{1,0:T(8,128)(2,1)S(1)} %copy-done.3), channel_id=1, source_target_pairs={{24,0},{25,1},{26,2},{27,3},{28,4},{29,5},{30,6},{31,7}} | collective-permute-start | bytes 1204232 | tf_op jit(solution)/shard_map/ppermute | solution.py:793
  97.0 35.9 %collective-permute-start.12 = (bf16[784,256]{1,0:T(8,128)(2,1)S(1)}, bf16[784,256]{1,0:T(8,128)(2,1)S(1)}, u32[]{:S(2)}, u32[]{:S(2)}) collective-permute-start(bf16[784,256]{1,0:T(8,128)(2,1)S(1)} %copy-done.5), channel_id=1, source_target_pairs={{8,0},{16,8},{24,16},{9,1},{17,9},{25,17},{10,2},{18,10},{26,18},{... | collective-permute-start | bytes 1204232 | tf_op jit(solution)/shard_map/ppermute | solution.py:793
  135.2 15.8 %all-to-all-start.26 = ((bf16[8,192,256]{2,1,0:T(8,128)(2,1)}), bf16[8,192,256]{2,1,0:T(8,128)(2,1)S(1)}, u32[]{:S(2)}, u32[]{:S(2)}) async-start(bf16[8,192,256]{2,1,0:T(8,128)(2,1)} %combine.1), calls=%async_computation.26 | async-start | bytes 1572864 | tf_op jit(solution)/shard_map/all_to_all | solution.py:804
  144.8 6.4 %copy-start.12 = (bf16[192,5120]{1,0:T(8,128)(2,1)S(1)}, bf16[192,5120]{1,0:T(8,128)(2,1)}, u32[]{:S(2)}) copy-start(bf16[192,5120]{1,0:T(8,128)(2,1)} %rest_2_.3) | copy-start | bytes 5898244
  144.8 6.4 %copy-start.21 = (bf16[192,1024]{1,0:T(8,128)(2,1)S(1)}, bf16[192,1024]{1,0:T(8,128)(2,1)}, u32[]{:S(2)}) copy-start(bf16[192,1024]{1,0:T(8,128)(2,1)} %k_ref.1) | copy-start | bytes 1179652
  144.8 6.4 %copy-start.26 = (s32[192]{0:T(256)S(1)}, s32[192]{0:T(256)}, u32[]{:S(2)}) copy-start(s32[192]{0:T(256)} %param.21) | copy-start | bytes 2308

commit v8 on v7

--- a/solution.py
+++ b/solution.py
@@ -700,7 +700,7 @@
             pltpu.VMEM((2, rows, columns), bf16),
             *more,
         ],
-        compiler_params=pltpu.CompilerParams(vmem_limit_bytes=48 * 1024 * 1024),
+        compiler_params=pltpu.CompilerParams(vmem_limit_bytes=60 * 1024 * 1024),
         cost_estimate=pl.CostEstimate(
             flops=5_000_000_000, bytes_accessed=12_000_000, transcendentals=4_000_000
         ),

time: 150 us -> 154 us (1.027); the launches traced: 152 us -> 151 us
  Pallas kernels: 36.3 us -> 47.2 us
  starting transfers between devices: 36.8 us -> 29.2 us
  waiting for transfers between devices: 69.4 us -> 62.3 us
  local copies, waits for them, and re-layouts: 5.6 us -> 8.22 us
    pallas_call x2, Pallas kernels: 21.7 us -> 32.8 us  [attention(): pl.pallas_call(functools.partial(attention_kernel, first), out_shape=outs...]
    ppermute x3, waiting for transfers between devices: 26.4 us -> 18.8 us  [lower(): return lax.ppermute(rows, 'outer', [(i + k, i) for i in range(planes - k)])]
    ppermute x3, starting transfers between devices: 11.4 us -> 3.91 us  [lower(): return lax.ppermute(rows, 'outer', [(i + k, i) for i in range(planes - k)])]
    slice x3, local copies, waits for them, and re-layouts: 1.13 us -> 3.19 us  [plane_device(): crossed = [swap(pair[1:], CORE) for pair in pairs]]
  transfers between devices with their start and end apart: 16 -> 16, of which waited for: 8 -> 9; matrix products, arithmetic and copies ran while one was open for 2% -> 3% of each run, Pallas kernels for 15% -> 20%
where the time goes in v8:
time: 154 us; the launch traced here: 151 us
  waiting for transfers between devices  62.3 us (40%)
  Pallas kernels  47.2 us (31%)
  starting transfers between devices  29.2 us (19%)
  local copies, waits for them, and re-layouts  8.22 us (5%)
  between operations  4.25 us (3%)
    pallas_call x2, Pallas kernels, attention(): pl.pallas_call(functools.partial(attention_kernel, first), out_shape=outs...  32.8 us
    ppermute x7, waiting for transfers between devices, swap(): return lax.ppermute(array, plane, [(i, i ^ k) for i in range(blocks)])  25.4 us
    ppermute x3, waiting for transfers between devices, lower(): return lax.ppermute(rows, 'outer', [(i + k, i) for i in range(planes - k)])  18.8 us
    ppermute x1, waiting for transfers between devices, plane_device(): up = [lax.ppermute(mine, 'outer', [(i, i + 1) for i in range(planes - 1)])]  8.57 us
    all_to_all x1, waiting for transfers between devices, plane_device(): lax.all_to_all(sent, plane, split_axis=0, concat_axis=0, tiled=True)  6.15 us
    all_to_all x1, starting transfers between devices, plane_device(): dq = lax.all_to_all(dq, plane, split_axis=0, concat_axis=0, tiled=True)  4.73 us
    pallas_call x1, Pallas kernels, pack_pairs(): pl.pallas_call(functools.partial(pack_pairs_kernel, limit), out_shape=jax...  4.57 us
    ppermute x7, starting transfers between devices, swap(): return lax.ppermute(array, plane, [(i, i ^ k) for i in range(blocks)])  4.51 us
  transfers between devices with their start and end apart: 16, of which 9 were waited for; matrix products, arithmetic and copies ran while one was open for 3% of the time, Pallas kernels for 20%

profile of v8, /device:TPU:17, one launch (start us, length us, event | category | flops | bytes accessed | tf_op | source)
XLA Modules:
  0.0 151.2 jit_solution(12782115020324302659)
XLA Ops:
  0.6 4.6 %pack_pairs.1 = bf16[8,208,256]{2,1,0:T(8,128)(2,1)} custom-call(s32[1,192]{1,0:T(1,128)} %bitcast.289, bf16[40,192]{1,0:T(8,128)(2,1)} %bitcast.285, bf16[192,1024]{1,0:T(8,128)(2,1)} %k_ref.1, bf16[192,1024]{1,0:T(8,128)(2,1)} %v_ref.1, bf16[192,5120]{1,0:T(8,128)(2,1)} %rest_2_.3, bf16[192,5120]{1,0:T(8,128)(2,1)} %o_ref.1), custom_call_target="tpu_custom_call" | custom-call | tf_op jit(solution)/shard_map/pack_pairs/pallas_call | solution.py:257
  5.2 4.4 %all-to-all-start.24 = ((bf16[8,208,256]{2,1,0:T(8,128)(2,1)}), bf16[8,208,256]{2,1,0:T(8,128)(2,1)S(1)}, u32[]{:S(2)}, u32[]{:S(2)}) async-start(bf16[8,208,256]{2,1,0:T(8,128)(2,1)} %pack_pairs.1), calls=%async_computation.24 | async-start | bytes 1703936 | tf_op jit(solution)/shard_map/all_to_all | solution.py:778
  9.6 3.3 %pack_rows.1 = (bf16[2,192,1280]{2,1,0:T(8,128)(2,1)}, bf16[2,192,1280]{2,1,0:T(8,128)(2,1)S(1)}, bf16[2,192,1280]{2,1,0:T(8,128)(2,1)S(1)}, bf16[1,192,1280]{2,1,0:T(8,128)(2,1)S(1)}) custom-call(s32[1]{0:T(128)} %bitcast.47.me_ref, bf16[192,5120]{1,0:T(8,128)(2,1)} %rest_1_.3, bf16[192,5120]{1,0:T(8,128)(2,1)} %rest_2_.3), custom_call_target="tpu_custom_call" | custom-call | tf_op jit(solution)/shard_map/pack_rows/pallas_call | solution.py:283
  12.9 0.0 collective-permute-start
  12.9 2.6 %collective-permute-start.4 = (bf16[2,192,1280]{2,1,0:T(8,128)(2,1)}, bf16[2,192,1280]{2,1,0:T(8,128)(2,1)}, u32[]{:S(2)}, u32[]{:S(2)}) collective-permute-start(bf16[2,192,1280]{2,1,0:T(8,128)(2,1)} %get-tuple-element.402), channel_id=1, source_target_pairs={{0,5},{1,4},{2,7},{3,6},{4,1},{5,0},{6,3},{7,2},{8,13},{9,12},{10,... | collective-permute-start | bytes 2949128 | tf_op jit(solution)/shard_map/ppermute | solution.py:772
  15.6 0.3 collective-permute-start.5
  15.9 0.0 collective-permute-start.6
  15.9 0.0 collective-permute-done.rest_3_
  15.9 6.1 %all-to-all-done.24.arrived = bf16[8,208,256]{2,1,0:T(8,128)(2,1)S(1)} async-done(((bf16[8,208,256]{2,1,0:T(8,128)(2,1)}), bf16[8,208,256]{2,1,0:T(8,128)(2,1)S(1)}, u32[]{:S(2)}, u32[]{:S(2)}) %all-to-all-start.24) | async-done | bytes 852000 | tf_op jit(solution)/shard_map/all_to_all | solution.py:778
  22.0 1.1 compact.1
  23.1 0.0 copy-start.1
  23.2 0.6 copy-done.1
  23.7 3.2 %collective-permute-start.1 = (bf16[784,256]{1,0:T(8,128)(2,1)S(1)}, bf16[784,256]{1,0:T(8,128)(2,1)S(1)}, u32[]{:S(2)}, u32[]{:S(2)}) collective-permute-start(bf16[784,256]{1,0:T(8,128)(2,1)S(1)} %get-tuple-element.401.rest_11_), channel_id=1, source_target_pairs={{0,8},{8,16},{16,24},{1,9},{9,17},{17,25},{2,10},{10,18},{18,26},{... | collective-permute-start | bytes 1204232 | tf_op jit(solution)/shard_map/ppermute | solution.py:784
  26.9 0.7 collective-permute-start.3
  27.6 8.6 %collective-permute-done.1.rest_10_ = bf16[784,256]{1,0:T(8,128)(2,1)S(1)} collective-permute-done((bf16[784,256]{1,0:T(8,128)(2,1)S(1)}, bf16[784,256]{1,0:T(8,128)(2,1)S(1)}, u32[]{:S(2)}, u32[]{:S(2)}) %collective-permute-start.1) | collective-permute-done | bytes 401440 | tf_op jit(solution)/shard_map/ppermute | solution.py:784
  36.2 3.3 %collective-permute-start.2 = (bf16[784,256]{1,0:T(8,128)(2,1)S(1)}, bf16[784,256]{1,0:T(8,128)(2,1)}, u32[]{:S(2)}, u32[]{:S(2)}) collective-permute-start(bf16[784,256]{1,0:T(8,128)(2,1)S(1)} %collective-permute-done.1.rest_10_), channel_id=1, source_target_pairs={{8,16},{16,24},{9,17},{17,25},{10,18},{18,26},{11,19},{19,27},{12,... | collective-permute-start | bytes 1204232 | tf_op jit(solution)/shard_map/ppermute | solution.py:786
  39.5 3.8 %collective-permute-done.4.rest_4_ = bf16[2,192,1280]{2,1,0:T(8,128)(2,1)} collective-permute-done((bf16[2,192,1280]{2,1,0:T(8,128)(2,1)}, bf16[2,192,1280]{2,1,0:T(8,128)(2,1)}, u32[]{:S(2)}, u32[]{:S(2)}) %collective-permute-start.4) | collective-permute-done | bytes 983072 | tf_op jit(solution)/shard_map/ppermute | solution.py:772
  43.3 20.2 %collective-permute-done.5.rest_5_ = bf16[2,192,1280]{2,1,0:T(8,128)(2,1)} collective-permute-done((bf16[2,192,1280]{2,1,0:T(8,128)(2,1)S(1)}, bf16[2,192,1280]{2,1,0:T(8,128)(2,1)}, u32[]{:S(2)}, u32[]{:S(2)}) %collective-permute-start.5) | collective-permute-done | bytes 983072 | tf_op jit(solution)/shard_map/ppermute | solution.py:772
  63.5 0.0 collective-permute-done.6.rest_6_
  63.5 0.0 collective-permute-done.3.rest_11_
  63.5 0.0 copy-done.28
  63.5 0.0 copy-start.29
  63.5 0.7 copy-done.29
  64.2 0.0 collective-permute-done.2.rest_10_
  64.2 1.1 slice.33
  65.3 0.9 collective-permute-start.7
  66.2 1.1 slice.34
  67.3 0.1 collective-permute-start.8
  67.4 1.1 slice.35
  68.4 0.6 collective-permute-start.9
  69.0 0.0 collective-permute-done.7.rest_7_
  69.0 0.2 collective-permute-done.8.rest_8_
  69.2 1.3 collective-permute-done.9.rest_9_
  70.5 0.0 copy-done.25
  70.5 0.0 copy-done.26
  70.5 0.8 copy-done.27
  71.3 0.0 copy-done.24
  71.3 0.0 copy-done.4
  71.3 0.0 copy-done.9
  71.3 12.2 %attention.2 = (bf16[784,256]{1,0:T(8,128)(2,1)}, bf16[784,256]{1,0:T(8,128)(2,1)}, f32[12,128,640]{2,1,0:T(8,128)}, s32[1]{0:T(128)}) custom-call(s32[1]{0:T(128)} %bitcast.47.me_ref, s32[8]{0:T(128)} %copy-done.1, bf16[8,16,256]{2,1,0:T(8,128)(2,1)} %copy-done.4, bf16[192,5120]{1,0:T(8,128)(2,1)} %rest_1_.3, bf16[192,5120]{1,0:T(8,128)(2,1)S(1)} %copy-done.9, ...), custom_call_target="tpu_custom_call" | custom-call | flops 5000000000 | bytes 12000000 | tf_op jit(solution)/shard_map/attention/pallas_call | solution.py:679
  83.5 0.0 copy-done.3
  83.5 1.3 collective-permute-start.11
  84.8 20.6 %attention.3 = (bf16[784,256]{1,0:T(8,128)(2,1)}, bf16[8,192,640]{2,1,0:T(8,128)(2,1)}, f32[768,256]{1,0:T(8,128)}, s32[1]{0:T(128)}) custom-call(s32[1]{0:T(128)} %bitcast.47.me_ref, s32[8]{0:T(128)} %copy-done.1, bf16[8,16,256]{2,1,0:T(8,128)(2,1)} %copy-done.4, bf16[192,5120]{1,0:T(8,128)(2,1)} %rest_1_.3, bf16[192,5120]{1,0:T(8,128)(2,1)S(1)} %copy-done.9, ...), custom_call_target="tpu_custom_call" | custom-call | flops 5000000000 | bytes 12000000 | tf_op jit(solution)/shard_map/attention/pallas_call | solution.py:679
  105.4 0.0 collective-permute-done.11.rest_1_
  105.5 4.7 %all-to-all-start.25 = ((bf16[8,192,640]{2,1,0:T(8,128)(2,1)}), bf16[8,192,640]{2,1,0:T(8,128)(2,1)}, u32[]{:S(2)}, u32[]{:S(2)}) async-start(bf16[8,192,640]{2,1,0:T(8,128)(2,1)} %get-tuple-element.418), calls=%async_computation.25 | async-start | bytes 3932160 | tf_op jit(solution)/shard_map/all_to_all | solution.py:800
  110.2 0.7 collective-permute-start.10
  110.9 1.9 %collective-permute-start.12 = (bf16[784,256]{1,0:T(8,128)(2,1)S(1)}, bf16[784,256]{1,0:T(8,128)(2,1)S(1)}, u32[]{:S(2)}, u32[]{:S(2)}) collective-permute-start(bf16[784,256]{1,0:T(8,128)(2,1)S(1)} %copy-done.31), channel_id=1, source_target_pairs={{8,0},{16,8},{24,16},{9,1},{17,9},{25,17},{10,2},{18,10},{26,18},{... | collective-permute-start | bytes 1204232 | tf_op jit(solution)/shard_map/ppermute | solution.py:793
  112.8 0.0 collective-permute-done.10.rest_0_
  112.8 18.8 %collective-permute-done.12.rest_2_ = bf16[784,256]{1,0:T(8,128)(2,1)S(1)} collective-permute-done((bf16[784,256]{1,0:T(8,128)(2,1)S(1)}, bf16[784,256]{1,0:T(8,128)(2,1)S(1)}, u32[]{:S(2)}, u32[]{:S(2)}) %collective-permute-start.12) | collective-permute-done | bytes 401440 | tf_op jit(solution)/shard_map/ppermute | solution.py:793
  131.7 2.3 %combine.1 = bf16[8,192,256]{2,1,0:T(8,128)(2,1)} custom-call(s32[8]{0:T(128)S(1)} %copy-done.2, f32[768,256]{1,0:T(8,128)S(1)} %copy-done, bf16[784,256]{1,0:T(8,128)(2,1)S(1)} %collective-permute-done.10.rest_0_, bf16[784,256]{1,0:T(8,128)(2,1)S(1)} %collective-permute-done.11.rest_1_, bf16[784,256]{1,0:T(8,128)(2,1)S(1)} %collective-permute-done.12.rest_2_), custom_call_target="tpu_custom_call" | custom-call | tf_op jit(solution)/shard_map/combine/pallas_call | solution.py:750
  134.0 0.2 all-to-all-done.25.parts
  134.2 4.5 %all-to-all-start.26 = ((bf16[8,192,256]{2,1,0:T(8,128)(2,1)}), bf16[8,192,256]{2,1,0:T(8,128)(2,1)S(1)}, u32[]{:S(2)}, u32[]{:S(2)}) async-start(bf16[8,192,256]{2,1,0:T(8,128)(2,1)} %combine.1), calls=%async_computation.26 | async-start | bytes 1572864 | tf_op jit(solution)/shard_map/all_to_all | solution.py:804
  140.0 0.6 slice.37
  140.6 0.5 slice.47
  142.4 0.6 slice.48
  143.7 0.0 copy-start.10
  143.7 0.0 copy-start.18
  143.7 0.0 copy-start.19
  143.7 0.0 copy-start.23
  143.8 3.1 %unpack_rows.1 = bf16[192,5120]{1,0:T(8,128)(2,1)} custom-call(bf16[8,192,640]{2,1,0:T(8,128)(2,1)} %all-to-all-done.25.parts), custom_call_target="tpu_custom_call" | custom-call | tf_op jit(solution)/shard_map/unpack_rows/pallas_call | solution.py:717
  146.9 3.1 %all-to-all-done.26 = bf16[8,192,256]{2,1,0:T(8,128)(2,1)S(1)} async-done(((bf16[8,192,256]{2,1,0:T(8,128)(2,1)}), bf16[8,192,256]{2,1,0:T(8,128)(2,1)S(1)}, u32[]{:S(2)}, u32[]{:S(2)}) %all-to-all-start.26) | async-done | bytes 786464 | tf_op jit(solution)/shard_map/all_to_all | solution.py:804
  149.9 0.2 slice_bitcast_fusion.2
  150.2 1.0 conditional.1
  150.2 1.0 copy_bitcast_fusion
  (20 shorter events, 0.0 us)
Async XLA Ops:
  5.2 16.8 %all-to-all-start.24 = ((bf16[8,208,256]{2,1,0:T(8,128)(2,1)}), bf16[8,208,256]{2,1,0:T(8,128)(2,1)S(1)}, u32[]{:S(2)}, u32[]{:S(2)}) async-start(bf16[8,208,256]{2,1,0:T(8,128)(2,1)} %pack_pairs.1), calls=%async_computation.24 | async-start | bytes 1703936 | tf_op jit(solution)/shard_map/all_to_all | solution.py:778
  12.9 2.9 %collective-permute-start = (bf16[1,192,1280]{2,1,0:T(8,128)(2,1)S(1)}, bf16[1,192,1280]{2,1,0:T(8,128)(2,1)S(1)}, u32[]{:S(2)}, u32[]{:S(2)}) collective-permute-start(bf16[1,192,1280]{2,1,0:T(8,128)(2,1)S(1)} %get-tuple-element.396), channel_id=1, source_target_pairs={{0,2},{1,3},{2,0},{3,1},{4,6},{5,7},{6,4},{7,5},{8,10},{9,11},{10,... | collective-permute-start | bytes 1474568 | tf_op jit(solution)/shard_map/ppermute | solution.py:772
  12.9 30.3 %collective-permute-start.4 = (bf16[2,192,1280]{2,1,0:T(8,128)(2,1)}, bf16[2,192,1280]{2,1,0:T(8,128)(2,1)}, u32[]{:S(2)}, u32[]{:S(2)}) collective-permute-start(bf16[2,192,1280]{2,1,0:T(8,128)(2,1)} %get-tuple-element.402), channel_id=1, source_target_pairs={{0,5},{1,4},{2,7},{3,6},{4,1},{5,0},{6,3},{7,2},{8,13},{9,12},{10,... | collective-permute-start | bytes 2949128 | tf_op jit(solution)/shard_map/ppermute | solution.py:772
  15.6 47.9 %collective-permute-start.5 = (bf16[2,192,1280]{2,1,0:T(8,128)(2,1)S(1)}, bf16[2,192,1280]{2,1,0:T(8,128)(2,1)}, u32[]{:S(2)}, u32[]{:S(2)}) collective-permute-start(bf16[2,192,1280]{2,1,0:T(8,128)(2,1)S(1)} %get-tuple-element.403), channel_id=1, source_target_pairs={{0,4},{1,5},{2,6},{3,7},{4,0},{5,1},{6,2},{7,3},{8,12},{9,13},{10,... | collective-permute-start | bytes 2949128 | tf_op jit(solution)/shard_map/ppermute | solution.py:772
  15.9 47.6 %collective-permute-start.6 = (bf16[2,192,1280]{2,1,0:T(8,128)(2,1)S(1)}, bf16[2,192,1280]{2,1,0:T(8,128)(2,1)}, u32[]{:S(2)}, u32[]{:S(2)}) collective-permute-start(bf16[2,192,1280]{2,1,0:T(8,128)(2,1)S(1)} %get-tuple-element.404), channel_id=1, source_target_pairs={{0,1},{1,0},{2,3},{3,2},{4,5},{5,4},{6,7},{7,6},{8,9},{9,8},{10,11... | collective-permute-start | bytes 2949128 | tf_op jit(solution)/shard_map/ppermute | solution.py:772
  15.9 55.4 %copy-start.24 = (bf16[1,192,1280]{2,1,0:T(8,128)(2,1)}, bf16[1,192,1280]{2,1,0:T(8,128)(2,1)S(1)}, u32[]{:S(2)}) copy-start(bf16[1,192,1280]{2,1,0:T(8,128)(2,1)S(1)} %collective-permute-done.rest_3_) | copy-start | bytes 1474564
  23.1 0.6 copy-start.1
  23.7 47.6 %copy-start.4 = (bf16[8,16,256]{2,1,0:T(8,128)(2,1)}, bf16[8,16,256]{2,1,0:T(8,128)(2,1)S(1)}, u32[]{:S(2)}) copy-start(bf16[8,16,256]{2,1,0:T(8,128)(2,1)S(1)} %get-tuple-element.399.rest_0_) | copy-start | bytes 196612
  23.7 59.8 %copy-start.3 = (bf16[784,256]{1,0:T(8,128)(2,1)}, bf16[784,256]{1,0:T(8,128)(2,1)S(1)}, u32[]{:S(2)}) copy-start(bf16[784,256]{1,0:T(8,128)(2,1)S(1)} %get-tuple-element.401.rest_11_) | copy-start | bytes 1204228
  23.7 12.5 %collective-permute-start.1 = (bf16[784,256]{1,0:T(8,128)(2,1)S(1)}, bf16[784,256]{1,0:T(8,128)(2,1)S(1)}, u32[]{:S(2)}, u32[]{:S(2)}) collective-permute-start(bf16[784,256]{1,0:T(8,128)(2,1)S(1)} %get-tuple-element.401.rest_11_), channel_id=1, source_target_pairs={{0,8},{8,16},{16,24},{1,9},{9,17},{17,25},{2,10},{10,18},{18,26},{... | collective-permute-start | bytes 1204232 | tf_op jit(solution)/shard_map/ppermute | solution.py:784
  26.9 36.5 %collective-permute-start.3 = (bf16[784,256]{1,0:T(8,128)(2,1)S(1)}, bf16[784,256]{1,0:T(8,128)(2,1)S(1)}, u32[]{:S(2)}, u32[]{:S(2)}) collective-permute-start(bf16[784,256]{1,0:T(8,128)(2,1)S(1)} %get-tuple-element.401.rest_11_), channel_id=1, source_target_pairs={{0,24},{1,25},{2,26},{3,27},{4,28},{5,29},{6,30},{7,31}} | collective-permute-start | bytes 1204232 | tf_op jit(solution)/shard_map/ppermute | solution.py:785
  36.2 27.3 %copy-start.28 = (bf16[784,256]{1,0:T(8,128)(2,1)}, bf16[784,256]{1,0:T(8,128)(2,1)S(1)}, u32[]{:S(2)}) copy-start(bf16[784,256]{1,0:T(8,128)(2,1)S(1)} %collective-permute-done.1.rest_10_) | copy-start | bytes 1204228
  36.2 28.0 %collective-permute-start.2 = (bf16[784,256]{1,0:T(8,128)(2,1)S(1)}, bf16[784,256]{1,0:T(8,128)(2,1)}, u32[]{:S(2)}, u32[]{:S(2)}) collective-permute-start(bf16[784,256]{1,0:T(8,128)(2,1)S(1)} %collective-permute-done.1.rest_10_), channel_id=1, source_target_pairs={{8,16},{16,24},{9,17},{17,25},{10,18},{18,26},{11,19},{19,27},{12,... | collective-permute-start | bytes 1204232 | tf_op jit(solution)/shard_map/ppermute | solution.py:786
  63.5 7.8 %copy-start.9 = (bf16[192,5120]{1,0:T(8,128)(2,1)S(1)}, bf16[192,5120]{1,0:T(8,128)(2,1)}, u32[]{:S(2)}) copy-start(bf16[192,5120]{1,0:T(8,128)(2,1)} %rest_2_.3) | copy-start | bytes 5898244
  63.5 0.8 copy-start.29
  65.3 3.7 %collective-permute-start.7 = (bf16[1,192,1280]{2,1,0:T(8,128)(2,1)S(1)}, bf16[1,192,1280]{2,1,0:T(8,128)(2,1)S(1)}, u32[]{:S(2)}, u32[]{:S(2)}) collective-permute-start(bf16[1,192,1280]{2,1,0:T(8,128)(2,1)S(1)} %slice.33), channel_id=1, source_target_pairs={{0,2},{1,3},{2,0},{3,1},{4,6},{5,7},{6,4},{7,5},{8,10},{9,11},{10,... | collective-permute-start | bytes 1474568 | tf_op jit(solution)/shard_map/ppermute | solution.py:772
  67.3 1.9 %collective-permute-start.8 = (bf16[1,192,1280]{2,1,0:T(8,128)(2,1)S(1)}, bf16[1,192,1280]{2,1,0:T(8,128)(2,1)S(1)}, u32[]{:S(2)}, u32[]{:S(2)}) collective-permute-start(bf16[1,192,1280]{2,1,0:T(8,128)(2,1)S(1)} %slice.34), channel_id=1, source_target_pairs={{0,2},{1,3},{2,0},{3,1},{4,6},{5,7},{6,4},{7,5},{8,10},{9,11},{10,... | collective-permute-start | bytes 1474568 | tf_op jit(solution)/shard_map/ppermute | solution.py:772
  68.4 2.1 %collective-permute-start.9 = (bf16[1,192,1280]{2,1,0:T(8,128)(2,1)S(1)}, bf16[1,192,1280]{2,1,0:T(8,128)(2,1)S(1)}, u32[]{:S(2)}, u32[]{:S(2)}) collective-permute-start(bf16[1,192,1280]{2,1,0:T(8,128)(2,1)S(1)} %slice.35), channel_id=1, source_target_pairs={{0,2},{1,3},{2,0},{3,1},{4,6},{5,7},{6,4},{7,5},{8,10},{9,11},{10,... | collective-permute-start | bytes 1474568 | tf_op jit(solution)/shard_map/ppermute | solution.py:772
  69.0 1.5 copy-start.25
  69.2 1.3 copy-start.26
  70.5 0.8 copy-start.27
  83.5 21.9 %collective-permute-start.11 = (bf16[784,256]{1,0:T(8,128)(2,1)}, bf16[784,256]{1,0:T(8,128)(2,1)S(1)}, u32[]{:S(2)}, u32[]{:S(2)}) collective-permute-start(bf16[784,256]{1,0:T(8,128)(2,1)} %get-tuple-element.415), channel_id=1, source_target_pairs={{16,0},{24,8},{17,1},{25,9},{18,2},{26,10},{19,3},{27,11},{20,4},{... | collective-permute-start | bytes 1204232 | tf_op jit(solution)/shard_map/ppermute | solution.py:793
  105.4 4.8 %copy-start.30 = (bf16[784,256]{1,0:T(8,128)(2,1)S(1)}, bf16[784,256]{1,0:T(8,128)(2,1)}, u32[]{:S(2)}) copy-start(bf16[784,256]{1,0:T(8,128)(2,1)} %get-tuple-element.413) | copy-start | bytes 1204228
  105.4 5.5 %copy-start.31 = (bf16[784,256]{1,0:T(8,128)(2,1)S(1)}, bf16[784,256]{1,0:T(8,128)(2,1)}, u32[]{:S(2)}) copy-start(bf16[784,256]{1,0:T(8,128)(2,1)} %get-tuple-element.417) | copy-start | bytes 1204228
  105.5 26.2 %copy-start = (f32[768,256]{1,0:T(8,128)S(1)}, f32[768,256]{1,0:T(8,128)}, u32[]{:S(2)}) copy-start(f32[768,256]{1,0:T(8,128)} %get-tuple-element.419.own) | copy-start | bytes 2359300
  105.5 26.2 %copy-start.2 = (s32[8]{0:T(128)S(1)}, s32[8]{0:T(128)}, u32[]{:S(2)}) copy-start(s32[8]{0:T(128)} %copy-done.1) | copy-start | bytes 100
  105.5 28.7 %all-to-all-start.25 = ((bf16[8,192,640]{2,1,0:T(8,128)(2,1)}), bf16[8,192,640]{2,1,0:T(8,128)(2,1)}, u32[]{:S(2)}, u32[]{:S(2)}) async-start(bf16[8,192,640]{2,1,0:T(8,128)(2,1)} %get-tuple-element.418), calls=%async_computation.25 | async-start | bytes 3932160 | tf_op jit(solution)/shard_map/all_to_all | solution.py:800
  110.2 2.6 %collective-permute-start.10 = (bf16[784,256]{1,0:T(8,128)(2,1)S(1)}, bf16[784,256]{1,0:T(8,128)(2,1)S(1)}, u32[]{:S(2)}, u32[]{:S(2)}) collective-permute-start(bf16[784,256]{1,0:T(8,128)(2,1)S(1)} %copy-done.30), channel_id=1, source_target_pairs={{24,0},{25,1},{26,2},{27,3},{28,4},{29,5},{30,6},{31,7}} | collective-permute-start | bytes 1204232 | tf_op jit(solution)/shard_map/ppermute | solution.py:793
  110.9 20.7 %collective-permute-start.12 = (bf16[784,256]{1,0:T(8,128)(2,1)S(1)}, bf16[784,256]{1,0:T(8,128)(2,1)S(1)}, u32[]{:S(2)}, u32[]{:S(2)}) collective-permute-start(bf16[784,256]{1,0:T(8,128)(2,1)S(1)} %copy-done.31), channel_id=1, source_target_pairs={{8,0},{16,8},{24,16},{9,1},{17,9},{25,17},{10,2},{18,10},{26,18},{... | collective-permute-start | bytes 1204232 | tf_op jit(solution)/shard_map/ppermute | solution.py:793
  134.2 15.7 %all-to-all-start.26 = ((bf16[8,192,256]{2,1,0:T(8,128)(2,1)}), bf16[8,192,256]{2,1,0:T(8,128)(2,1)S(1)}, u32[]{:S(2)}, u32[]{:S(2)}) async-start(bf16[8,192,256]{2,1,0:T(8,128)(2,1)} %combine.1), calls=%async_computation.26 | async-start | bytes 1572864 | tf_op jit(solution)/shard_map/all_to_all | solution.py:804
  143.7 6.4 %copy-start.10 = (bf16[192,5120]{1,0:T(8,128)(2,1)S(1)}, bf16[192,5120]{1,0:T(8,128)(2,1)}, u32[]{:S(2)}) copy-start(bf16[192,5120]{1,0:T(8,128)(2,1)} %rest_2_.3) | copy-start | bytes 5898244
  143.7 6.4 %copy-start.18 = (bf16[192,1024]{1,0:T(8,128)(2,1)S(1)}, bf16[192,1024]{1,0:T(8,128)(2,1)}, u32[]{:S(2)}) copy-start(bf16[192,1024]{1,0:T(8,128)(2,1)} %k_ref.1) | copy-start | bytes 1179652
  143.7 6.4 %copy-start.19 = (bf16[192,1024]{1,0:T(8,128)(2,1)S(1)}, bf16[192,1024]{1,0:T(8,128)(2,1)}, u32[]{:S(2)}) copy-start(bf16[192,1024]{1,0:T(8,128)(2,1)} %v_ref.1) | copy-start | bytes 1179652
  143.7 6.4 %copy-start.23 = (s32[192]{0:T(256)S(1)}, s32[192]{0:T(256)}, u32[]{:S(2)}) copy-start(s32[192]{0:T(256)} %param.21) | copy-start | bytes 2308
